TPU v7x, 128 devices: a whole 4x4x4 slice. The times are simulated.
128 devices in a mesh: row: 32 (over x, z, core), col: 4 (over y).
Axes of the slice: x: 4, y: 4, z: 4, core: 2. Of those that a mesh axis runs over, the one named last changes fastest.
Arguments:
- grad_joined: bfloat16 [48, 1024, 1024], P(None, 'row', 'col'), may hold values from -6 to 6
- joined_fine: bfloat16 [48, 1024, 1024], P(None, 'row', 'col'), as said below
- input_fine: bfloat16 [48, 1024, 1024], P(None, 'row', 'col'), may hold values from -6 to 6
- inner_fine: bfloat16 [48, 1024, 1024], P(None, 'row', 'col'), as said below
- unit_fine: bfloat16 [48, 1024, 1024], P(None, 'row', 'col'), as said below
- input_mid: bfloat16 [96, 512, 512], P(None, 'row', 'col'), may hold values from -6 to 6
- inner_mid: bfloat16 [96, 512, 512], P(None, 'row', 'col'), as said below
- unit_mid: bfloat16 [96, 512, 512], P(None, 'row', 'col'), as said below
- input_coarse: bfloat16 [192, 256, 256], P(None, 'row', 'col'), may hold values from -6 to 6
- inner_coarse: bfloat16 [192, 256, 256], P(None, 'row', 'col'), as said below
- unit_coarse: bfloat16 [192, 256, 256], P(None, 'row', 'col'), as said below
- first_fine: bfloat16 [3, 3, 48, 48], replicated, may hold values from -0.3125 to 0.3125
- second_fine: bfloat16 [3, 3, 48, 48], replicated, may hold values from -0.3125 to 0.3125
- first_mid: bfloat16 [3, 3, 96, 96], replicated, may hold values from -0.21875 to 0.21875
- second_mid: bfloat16 [3, 3, 96, 96], replicated, may hold values from -0.21875 to 0.21875
- first_coarse: bfloat16 [3, 3, 192, 192], replicated, may hold values from -0.15625 to 0.15625
- second_coarse: bfloat16 [3, 3, 192, 192], replicated, may hold values from -0.15625 to 0.15625
- lift_mid: bfloat16 [96, 48], replicated, may hold values from -0.625 to 0.625
- lift_coarse: bfloat16 [192, 48], replicated, may hold values from -0.4375 to 0.4375
Outputs:
- grad_input_fine: bfloat16 [48, 1024, 1024], P(None, 'row', 'col')
- grad_input_mid: bfloat16 [96, 512, 512], P(None, 'row', 'col')
- grad_input_coarse: bfloat16 [192, 256, 256], P(None, 'row', 'col')
- grad_first_fine: float32 [3, 3, 48, 48], replicated
- grad_second_fine: float32 [3, 3, 48, 48], replicated
- grad_first_mid: float32 [3, 3, 96, 96], replicated
- grad_second_mid: float32 [3, 3, 96, 96], replicated
- grad_first_coarse: float32 [3, 3, 192, 192], replicated
- grad_second_coarse: float32 [3, 3, 192, 192], replicated
- grad_lift_mid: float32 [96, 48], replicated
- grad_lift_coarse: float32 [192, 48], replicated
Inputs may be any that keep to these rules, and one draw needn't show every extreme that they name: `joined_fine`: saved ReLU outputs. `inner_fine`: saved ReLU outputs. `unit_fine`: saved ReLU outputs. `inner_mid`: saved ReLU outputs. `unit_mid`: saved ReLU outputs. `inner_coarse`: saved ReLU outputs. `unit_coarse`: saved ReLU outputs.
All inputs are finite; a program needn't handle non-finite values.
Results may differ from a plain program's by a relative error of at most 0.015.
Values may be sent and summed in bfloat16 or wider, within the bound.
No kernel may reach another device: no remote copies, remote signals or barrier semaphores. Data moves between devices by JAX's collectives and lax.ppermute only.
A program may use at most 128 MiB of HBM per device.

v0:
```python
import jax
import jax.numpy as jnp
import numpy as np
from jax import lax
from jax.experimental import pallas as pl
from jax.experimental.pallas import tpu as pltpu
from jax.sharding import PartitionSpec as P

ROWS, COLS = 32, 4
CELLS = 1536
FINE, MID = 48, 96
COARSE_ROWS, COARSE_COLS, COARSE = 8, 64, 192
PITCH = 80
PARAMS = pltpu.CompilerParams(vmem_limit_bytes=56 * 2**20)

AXES = ("row", "col")
ORDER = (("y", "x", "z"), ("x", "z", "y"))
CORE_PAIRS = [(d, d ^ 4) for d in range(128)]


def stage_pairs(stage, k):
    pairs = []
    for d in range(128):
        row, col = divmod(d, 4)
        at = {"x": row // 8, "z": (row // 2) % 4, "y": col}
        core = row % 2
        at[ORDER[core][stage]] ^= k
        pairs.append((d, (at["x"] * 8 + at["z"] * 2 + core) * 4 + at["y"]))
    return pairs


def my_place():
    row, col = lax.axis_index("row"), lax.axis_index("col")
    at = {"x": row // 8, "z": (row // 2) % 4, "y": col}
    core = row % 2
    return core, [jnp.where(core == 0, at[ORDER[0][s]], at[ORDER[1][s]]) for s in range(3)]


def send(block, pairs):
    return lax.ppermute(block, AXES, pairs)


def add4(own, others):
    a, b, c = [other.astype(jnp.float32) for other in others]
    return ((own.astype(jnp.float32) + a) + (b + c)).astype(jnp.bfloat16)


def scatter_stage(block, stage, mine):
    parts = block.reshape(4, block.shape[0] // 4, block.shape[1])
    own = lax.dynamic_index_in_dim(parts, mine, 0, keepdims=False)
    others = [
        send(lax.dynamic_index_in_dim(parts, mine ^ k, 0, keepdims=False), stage_pairs(stage, k))
        for k in (1, 2, 3)
    ]
    return add4(own, others)


def reduce_stage(block, stage):
    return add4(block, [send(block, stage_pairs(stage, k)) for k in (1, 2, 3)])


def gather_stage(block, stage, mine):
    parts = [block] + [send(block, stage_pairs(stage, k)) for k in (1, 2, 3)]
    whole = jnp.zeros((4,) + block.shape, block.dtype)
    for k in range(4):
        whole = lax.dynamic_update_index_in_dim(whole, parts[k], mine ^ k, 0)
    return whole.reshape(4 * block.shape[0], block.shape[1])


def all_sum(block):
    core, mine = my_place()
    half = block.shape[0] // 2
    halves = block.reshape(2, half, block.shape[1])
    other = send(lax.dynamic_index_in_dim(halves, 1 - core, 0, keepdims=False), CORE_PAIRS)
    own = lax.dynamic_index_in_dim(halves, core, 0, keepdims=False)
    part = (own.astype(jnp.float32) + other.astype(jnp.float32)).astype(jnp.bfloat16)
    part = scatter_stage(part, 0, mine[0])
    part = scatter_stage(part, 1, mine[1])
    part = reduce_stage(part, 2)
    part = gather_stage(part, 1, mine[1])
    part = gather_stage(part, 0, mine[0])
    other = send(part, CORE_PAIRS)
    return jnp.where(core == 0, jnp.concatenate([part, other]), jnp.concatenate([other, part]))


def shift_pairs(down, right):
    return [
        (row * COLS + col, (row + down) * COLS + col + right)
        for row in range(ROWS)
        for col in range(COLS)
        if 0 <= row + down < ROWS and 0 <= col + right < COLS
    ]


def iota(shape, dim):
    return lax.broadcasted_iota(jnp.int32, shape, dim)


def picks(shape, pairs):
    rows, cols = iota(shape, 0), iota(shape, 1)
    hit = jnp.zeros(shape, jnp.bool_)
    for row, col in pairs:
        hit = hit | ((rows == row) & (cols == col))
    return hit.astype(jnp.float32).astype(jnp.bfloat16)


def dot(a, b, a_dim=1, b_dim=0):
    return lax.dot_general(
        a, b, (((a_dim,), (b_dim,)), ((), ())), preferred_element_type=jnp.float32
    )


def keep(gate, value):
    return jnp.where(gate > 0, value, jnp.zeros_like(value))


def prep_kernel(
    grad, joined, unit_fine, inner_fine, unit_mid, inner_mid, unit_coarse, inner_coarse, lift_mid, lift_coarse,
    fine, mid, coarse, up, down, left, right, lift, upstream, gate_mid, in_fine, in_mid,
):
    above = keep(joined[...], grad[...])
    upstream[...] = jnp.transpose(above, (1, 0, 2)).reshape(CELLS, 256)
    fine[...] = jnp.transpose(keep(unit_fine[...], above), (1, 0, 2)).reshape(CELLS, 256)
    gate_mid[...] = jnp.transpose(unit_mid[...], (1, 0, 2)).reshape(CELLS, 128)
    in_fine[...] = jnp.transpose(inner_fine[...], (1, 0, 2)).reshape(CELLS, 256)
    in_mid[...] = jnp.transpose(inner_mid[...], (1, 0, 2)).reshape(CELLS, 128)

    cells, target = iota((256, 192), 0), iota((256, 192), 1)
    pooling = jnp.where(target < 128, cells // 2, cells // 4 + 128) == target
    pooling = pooling.astype(jnp.float32).astype(jnp.bfloat16)
    sum_mid = jnp.zeros((MID, FINE), jnp.float32)
    sum_coarse = jnp.zeros((FINE, COARSE), jnp.float32)
    for row in range(COARSE_ROWS):
        pooled = dot(upstream[row * 192 : (row + 1) * 192, :], pooling)
        quarter = [pooled[k * FINE : (k + 1) * FINE] for k in range(4)]
        for half in range(2):
            cell = (quarter[2 * half] + quarter[2 * half + 1])[:, :128].astype(jnp.bfloat16)
            rows = slice((2 * row + half) * MID, (2 * row + half + 1) * MID)
            gate = gate_mid[rows, :]
            mid[rows, :] = keep(gate, dot(lift_mid[...], cell).astype(jnp.bfloat16))
            sum_mid += dot(gate, cell, 1, 1)
        cell = ((quarter[0] + quarter[1]) + (quarter[2] + quarter[3]))[:, 128:].astype(jnp.bfloat16)
        gate = unit_coarse[row]
        coarse[row] = keep(gate, dot(cell, lift_coarse[...], 0, 1).astype(jnp.bfloat16))
        sum_coarse += dot(cell, gate)

    lift[...] = jnp.zeros(lift.shape, lift.dtype)
    lift[0:96, 0:48] = sum_mid.astype(jnp.bfloat16)
    lift[0:48, 64:128] = sum_coarse[:, 128:].astype(jnp.bfloat16)
    lift[96:144, :] = sum_coarse[:, :128].astype(jnp.bfloat16)

    edges = (
        dot(picks((32, 256), ((0, 0), (1, 1), (16, 254), (17, 255))), fine[...], 1, 1)
        + dot(picks((32, 256), ((2, 0), (18, 255))), in_fine[...], 1, 1)
        + dot(picks((32, 128), ((3, 0), (4, 1), (19, 126), (20, 127))), mid[...], 1, 1)
        + dot(picks((32, 128), ((5, 0), (21, 127))), in_mid[...], 1, 1)
    ).astype(jnp.bfloat16)
    masked = coarse[...].reshape(COARSE_ROWS * COARSE_COLS, COARSE)
    inner = inner_coarse[...].reshape(COARSE_ROWS * COARSE_COLS, COARSE)
    for side, out, cols in ((0, left, (0, 1, 0)), (1, right, (62, 63, 63))):
        for tile in range(12):
            out[tile * 16 : (tile + 1) * 16, :] = edges[side * 16 : (side + 1) * 16, tile * 128 : (tile + 1) * 128]
        row, cell = iota((32, 512), 0), iota((32, 512), 1)
        here = cell - (row % 8) * 64
        first = ((row < 8) & (here == cols[0])) | ((row >= 8) & (row < 16) & (here == cols[1]))
        second = (row >= 16) & (row < 24) & (here == cols[2])
        rim = dot(first.astype(jnp.float32).astype(jnp.bfloat16), masked) + dot(
            second.astype(jnp.float32).astype(jnp.bfloat16), inner
        )
        rim = rim.astype(jnp.bfloat16)
        out[192:224, :] = rim[:, :128]
        out[224:256, :] = jnp.zeros((32, 128), jnp.bfloat16)
        out[224:256, 0:64] = rim[:, 128:]

    for out, last in ((up, False), (down, True)):
        two = slice(CELLS - 2 * FINE, CELLS) if last else slice(0, 2 * FINE)
        one = slice(CELLS - FINE, CELLS) if last else slice(0, FINE)
        out[0:96, :] = fine[two, 0:128]
        out[96:192, :] = fine[two, 128:256]
        out[192:240, :] = in_fine[one, 0:128]
        out[240:288, :] = in_fine[one, 128:256]
        out[288:480, :] = mid[slice(CELLS - 2 * MID, CELLS) if last else slice(0, 2 * MID), :]
        out[480:576, :] = in_mid[slice(CELLS - MID, CELLS) if last else slice(0, MID), :]
        at = 6 if last else 0
        pair = coarse[at : at + 2].reshape(128, COARSE)
        out[576:704, :] = pair[:, :128]
        single = inner_coarse[7 if last else 0]
        out[704:768, :] = single[:, :128]
        out[768:896, :] = jnp.zeros((128, 128), jnp.bfloat16)
        out[768:896, 0:64] = pair[:, 128:]
        out[768:832, 64:128] = single[:, 128:]


def prep(*args):
    half = jnp.bfloat16
    shapes = (
        (CELLS, 256), (CELLS, 128), (COARSE_ROWS, COARSE_COLS, COARSE),
        (896, 128), (896, 128), (256, 128), (256, 128), (144, 128),
    )
    return pl.pallas_call(
        prep_kernel,
        out_shape=[jax.ShapeDtypeStruct(shape, half) for shape in shapes],
        scratch_shapes=[pltpu.VMEM((CELLS, width), half) for width in (256, 128, 256, 128)],
        compiler_params=PARAMS,
        name="prep",
    )(*args)


def unit_kernel(
    source, inner, masked, top, bottom, lt, rt, top_lt, top_rt, bottom_lt, bottom_rt, first, second,
    out, grads, mx, ix, px, sx, ox, acc_first, acc_second, *, chans, rows, width, edge, fill_rows, write_grads,
):
    ring = width + 128
    half = jnp.bfloat16

    mx[2 * chans : 2 * chans + CELLS, 0:width] = masked[...]
    ix[chans : chans + CELLS, 0:width] = jnp.transpose(inner[...], (1, 0, 2)).reshape(CELLS, width)
    sx[...] = jnp.transpose(source[...], (1, 0, 2)).reshape(CELLS, width)
    fill_rows(mx, ix, top, 0, 0)
    fill_rows(mx, ix, bottom, 2 * chans + CELLS, chans + CELLS)
    place = picks(
        (32, 256),
        ((edge, 0), (edge + 1, 1), (16 + edge, 126), (17 + edge, 127), (edge + 2, 128), (18 + edge, 255)),
    )

    def columns(right, left, tile):
        rows16 = slice(tile * 16, (tile + 1) * 16)
        both = jnp.concatenate([right[rows16, :], left[rows16, :]], axis=0)
        return dot(both, place, 0, 0).astype(half)

    for tile in range(12):
        cols = columns(rt, lt, tile)
        mx[2 * chans + tile * 128 : 2 * chans + (tile + 1) * 128, width:ring] = cols[:, :128]
        ix[chans + tile * 128 : chans + (tile + 1) * 128, width:ring] = cols[:, 128:]
    for tile in range((CELLS - 2 * chans) // 128, 12):
        cols = columns(top_rt, top_lt, tile)
        skip = max(0, CELLS - 2 * chans - tile * 128)
        at = tile * 128 + skip - (CELLS - 2 * chans)
        mx[at : at + 128 - skip, width:ring] = cols[skip:, :128]
        if tile == 11:
            ix[0:chans, width:ring] = cols[128 - chans :, 128:]
    for tile in range(-(-2 * chans // 128)):
        cols = columns(bottom_rt, bottom_lt, tile)
        size = min(128, 2 * chans - tile * 128)
        at = 2 * chans + CELLS + tile * 128
        mx[at : at + size, width:ring] = cols[:size, :128]
        if tile == 0:
            ix[chans + CELLS :, width:ring] = cols[:chans, 128:]

    def taps(weight, window):
        parts = dot(weight, window)
        return (
            pltpu.roll(parts[:chans], ring - 1, 1) + parts[chans : 2 * chans] + pltpu.roll(parts[2 * chans :], 1, 1)
        )

    def before(row, carry):
        at = pl.multiple_of(row * chans, 16)
        inner_grad = taps(second[...], mx[pl.ds(at, 3 * chans), :])
        px[pl.ds(at, chans), :] = keep(ix[pl.ds(at, chans), :].astype(jnp.float32), inner_grad).astype(half)
        return carry

    lax.fori_loop(0, rows + 2, before, 0, unroll=2)

    def spread(tile):
        wide = jnp.concatenate([tile.astype(jnp.float32), jnp.zeros((chans, 128), jnp.float32)], axis=1)
        return jnp.concatenate([pltpu.roll(wide, 1, 1), wide, pltpu.roll(wide, ring - 1, 1)], axis=0).astype(half)

    acc_first[...] = jnp.zeros(acc_first.shape, jnp.float32)
    acc_second[...] = jnp.zeros(acc_second.shape, jnp.float32)

    def after(row, carry):
        at = pl.multiple_of(row * chans, 16)
        window = px[pl.ds(at, 3 * chans), :]
        grad = taps(first[...], window)[:, :width]
        ox[pl.ds(row, 1), :, :] = (masked[pl.ds(at, chans), :].astype(jnp.float32) + grad).astype(half)[None]
        acc_first[...] += dot(spread(sx[pl.ds(at, chans), :]), window, 1, 1)
        own = ix[pl.ds(pl.multiple_of(at + chans, 16), chans), 0:width]
        acc_second[...] += dot(spread(own), mx[pl.ds(pl.multiple_of(at + chans, 16), 3 * chans), :], 1, 1)
        return carry

    lax.fori_loop(0, rows, after, 0, unroll=2)
    out[...] = jnp.transpose(ox[...], (1, 0, 2))
    write_grads(grads, acc_first, acc_second)


def fine_rows(mx, ix, halo, at, inner_at):
    mx[at : at + 96, 0:128] = halo[0:96, :]
    mx[at : at + 96, 128:256] = halo[96:192, :]
    ix[inner_at : inner_at + 48, 0:128] = halo[192:240, :]
    ix[inner_at : inner_at + 48, 128:256] = halo[240:288, :]


def mid_rows(mx, ix, halo, at, inner_at):
    mx[at : at + 192, 0:128] = halo[288:480, :]
    ix[inner_at : inner_at + 96, 0:128] = halo[480:576, :]


def fine_grads(grads, acc_first, acc_second):
    for tap in range(3):
        cols = slice((2 - tap) * FINE, (3 - tap) * FINE)
        pair = jnp.concatenate([acc_second[:, cols], acc_first[:, cols], jnp.zeros((144, 32), jnp.float32)], axis=1)
        grads[tap * 144 : (tap + 1) * 144, :] = pair.astype(jnp.bfloat16)


def mid_grads(grads, acc_first, acc_second):
    for index, acc in enumerate((acc_second, acc_first)):
        for tap in range(3):
            part = jnp.concatenate(
                [acc[:, (2 - tap) * MID : (3 - tap) * MID], jnp.zeros((288, 32), jnp.float32)], axis=1
            )
            at = (3 * index + tap) * 288
            grads[at : at + 288, :] = part.astype(jnp.bfloat16)


def channel_unit(source, inner, masked, halo, first, second, chans, rows, width, edge, fill_rows, grad_rows, write_grads, name):
    half = jnp.bfloat16
    ring = width + 128

    def kernel(*refs):
        unit_kernel(
            *refs, chans=chans, rows=rows, width=width, edge=edge, fill_rows=fill_rows, write_grads=write_grads
        )

    def stacked(weight):
        return jnp.transpose(weight[::-1], (1, 2, 0, 3)).reshape(3 * chans, 3 * chans)

    return pl.pallas_call(
        kernel,
        out_shape=[
            jax.ShapeDtypeStruct((chans, rows, width), half),
            jax.ShapeDtypeStruct((grad_rows, 128), half),
        ],
        scratch_shapes=[
            pltpu.VMEM(((rows + 4) * chans, ring), half),
            pltpu.VMEM(((rows + 2) * chans, ring), half),
            pltpu.VMEM(((rows + 2) * chans, ring), half),
            pltpu.VMEM((CELLS, width), half),
            pltpu.VMEM((rows, chans, width), half),
            pltpu.VMEM((3 * chans, 3 * chans), jnp.float32),
            pltpu.VMEM((3 * chans, 3 * chans), jnp.float32),
        ],
        compiler_params=PARAMS,
        name=name,
    )(source, inner, masked, *halo, stacked(first), stacked(second))


def coarse_places():
    place = np.zeros((2, 13 * 16, 6 * 32), np.float32)
    for index, first_row, count, sides in ((0, -2, 12, ((0, 0, "r"), (1, 1, "r"), (14, 0, "l"), (15, 1, "l"))), (1, -1, 10, ((0, 2, "r"), (15, 2, "l")))):
        for block in range(count + 1):
            for at, which, side in sides:
                row = first_row + block - (1 if side == "r" else 0)
                if row < first_row or row >= first_row + count:
                    continue
                message = 0 if 0 <= row < 8 else 1 if row < 0 else 2
                source = 2 * message + (0 if side == "r" else 1)
                place[index, block * 16 + at, source * 32 + which * 8 + row % 8] = 1
    return place.reshape(2 * 13 * 16, 6 * 32)


def coarse_kernel(
    source, inner, masked, top, bottom, lt, rt, top_lt, top_rt, bottom_lt, bottom_rt, first, second, place,
    out, grads, mx, ix, px, own, turned, tail,
):
    half = jnp.bfloat16
    lead = 16
    rims = jnp.concatenate(
        [
            jnp.concatenate([ref[192:224, :], ref[224:256, 0:64]], axis=1)
            for ref in (rt, lt, top_rt, top_lt, bottom_rt, bottom_lt)
        ],
        axis=0,
    )
    rims = dot(place[...], rims).astype(half)

    def rows_of(halo):
        pair = jnp.concatenate([halo[576:704, :], halo[768:896, 0:64]], axis=1)
        single = jnp.concatenate([halo[704:768, :], halo[768:832, 64:128]], axis=1)
        return pair, single

    above, above_inner = rows_of(top)
    below, below_inner = rows_of(bottom)
    grid = [above[:64], above[64:]] + [masked[k] for k in range(8)] + [below[:64], below[64:]]
    inner_grid = [above_inner] + [inner[k] for k in range(8)] + [below_inner]
    for ref, blocks, at in ((mx.at[1], grid, 0), (ix, inner_grid, 208)):
        ref[0:lead, :] = rims[at : at + 16]
        for k, block in enumerate(blocks):
            start = lead + k * PITCH
            ref[start : start + 64, :] = block
            ref[start + 64 : start + PITCH, :] = rims[at + (k + 1) * 16 : at + (k + 2) * 16]

    def shifted(ref, size):
        whole = ref[1].astype(jnp.float32)
        ref[0] = pltpu.roll(whole, size - 1, 0).astype(half)
        ref[2] = pltpu.roll(whole, 1, 0).astype(half)

    def taps(ref, weight, start, size):
        total = jnp.zeros((size, COARSE), jnp.float32)
        for row_tap in range(3):
            for col_tap in range(3):
                at = start + (2 - row_tap) * PITCH
                total += dot(ref[col_tap, at : at + size, :], weight[row_tap, col_tap], 1, 1)
        return total

    shifted(mx, 976)
    for start in range(0, 816, 272):
        inner_grad = taps(mx, second, start, 272)
        px[1, start : start + 272, :] = keep(
            ix[start : start + 272, :].astype(jnp.float32), inner_grad
        ).astype(half)
    shifted(px, 816)
    for row in range(8):
        grad = taps(px, first, lead + row * PITCH, 64)
        out[row] = (masked[row].astype(jnp.float32) + grad).astype(half)

    def corr(tile, ref, start, write):
        own[...] = jnp.zeros(own.shape, half)
        for row in range(8):
            own[row * PITCH : row * PITCH + 64, :] = tile[row]
        turned[...] = jnp.transpose(own[...].astype(jnp.float32)).astype(half)
        for row_tap in range(3):
            for col_tap in range(3):
                at = start + (2 - row_tap) * PITCH
                write(row_tap * 3 + col_tap, dot(turned[...], ref[col_tap, at : at + 8 * PITCH, :]))

    def write_second(tap, value):
        grads[tap * COARSE : (tap + 1) * COARSE, :] = value[:, :128].astype(half)
        tail[tap * COARSE : (tap + 1) * COARSE, :] = value[:, 128:].astype(half)

    def write_first(tap, value):
        at = 1728 + tap * COARSE
        grads[at : at + COARSE, :] = value[:, :128].astype(half)
        rows = slice(3456 + tap * COARSE, 3456 + (tap + 1) * COARSE)
        grads[rows, :] = jnp.concatenate(
            [tail[tap * COARSE : (tap + 1) * COARSE, :], value[:, 128:].astype(half)], axis=1
        )

    corr(inner, mx, lead + PITCH, write_second)
    corr(source, px, lead, write_first)
    grads[5184:, :] = jnp.zeros((192, 128), half)


def coarse_unit(source, inner, masked, halo, first, second):
    half = jnp.bfloat16
    return pl.pallas_call(
        coarse_kernel,
        out_shape=[
            jax.ShapeDtypeStruct((COARSE_ROWS, COARSE_COLS, COARSE), half),
            jax.ShapeDtypeStruct((5376, 128), half),
        ],
        scratch_shapes=[
            pltpu.VMEM((3, 976, COARSE), half),
            pltpu.VMEM((816, COARSE), half),
            pltpu.VMEM((3, 816, COARSE), half),
            pltpu.VMEM((8 * PITCH, COARSE), half),
            pltpu.VMEM((COARSE, 8 * PITCH), half),
            pltpu.VMEM((1728, 64), half),
        ],
        compiler_params=PARAMS,
        name="coarse_unit",
    )(source, inner, masked, *halo, first, second, jnp.asarray(coarse_places(), half))


def unpack_kernel(large, small, first_fine, second_fine, first_mid, second_mid, first_coarse, second_coarse, lift_mid, lift_coarse):
    full = jnp.float32
    for tap in range(9):
        row_tap, col_tap = tap // 3, tap % 3
        rows = slice(tap * COARSE, (tap + 1) * COARSE)
        tails = large[3456 + tap * COARSE : 3456 + (tap + 1) * COARSE, :].astype(full)
        second_coarse[row_tap, col_tap, :, 0:128] = large[rows, :].astype(full)
        second_coarse[row_tap, col_tap, :, 128:192] = tails[:, :64]
        first_coarse[row_tap, col_tap, :, 0:128] = large[1728 + tap * COARSE : 1728 + (tap + 1) * COARSE, :].astype(full)
        first_coarse[row_tap, col_tap, :, 128:192] = tails[:, 64:]
        pair = small[tap * FINE : (tap + 1) * FINE, :].astype(full)
        second_fine[row_tap, col_tap] = pair[:, 0:48]
        first_fine[row_tap, col_tap] = pair[:, 48:96]
        second_mid[row_tap, col_tap] = small[432 + tap * MID : 432 + (tap + 1) * MID, 0:96].astype(full)
        first_mid[row_tap, col_tap] = small[1296 + tap * MID : 1296 + (tap + 1) * MID, 0:96].astype(full)
    lift_mid[...] = small[2160:2256, 0:48].astype(full)
    wide = jnp.concatenate([small[2256:2304, :], small[2160:2208, 64:128]], axis=1).astype(full)
    lift_coarse[...] = jnp.transpose(wide)


def unpack(large, small):
    shapes = ((3, 3, 48, 48),) * 2 + ((3, 3, 96, 96),) * 2 + ((3, 3, 192, 192),) * 2 + ((96, 48), (192, 48))
    return pl.pallas_call(
        unpack_kernel,
        out_shape=[jax.ShapeDtypeStruct(shape, jnp.float32) for shape in shapes],
        compiler_params=PARAMS,
        name="unpack",
    )(large, small)


def on_device(
    grad_joined, joined_fine, input_fine, inner_fine, unit_fine, input_mid, inner_mid, unit_mid,
    input_coarse, inner_coarse, unit_coarse, first_fine, second_fine, first_mid, second_mid,
    first_coarse, second_coarse, lift_mid, lift_coarse,
):
    input_coarse, inner_coarse, unit_coarse = (
        jnp.transpose(x, (1, 2, 0)) for x in (input_coarse, inner_coarse, unit_coarse)
    )
    fine, mid, coarse, up, down, left, right, lift = prep(
        grad_joined, joined_fine, unit_fine, inner_fine, unit_mid, inner_mid, unit_coarse, inner_coarse, lift_mid, lift_coarse
    )
    halo = (
        send(down, shift_pairs(1, 0)),
        send(up, shift_pairs(-1, 0)),
        send(right, shift_pairs(0, 1)),
        send(left, shift_pairs(0, -1)),
        send(right, shift_pairs(1, 1)),
        send(left, shift_pairs(1, -1)),
        send(right, shift_pairs(-1, 1)),
        send(left, shift_pairs(-1, -1)),
    )
    coarse_input, large = coarse_unit(input_coarse, inner_coarse, coarse, halo, first_coarse, second_coarse)
    mid_input, mid_part = channel_unit(
        input_mid, inner_mid, mid, halo, first_mid, second_mid, MID, 16, 128, 3, mid_rows, 1728, mid_grads, "mid_unit"
    )
    fine_input, fine_part = channel_unit(
        input_fine, inner_fine, fine, halo, first_fine, second_fine, FINE, 32, 256, 0, fine_rows, 432, fine_grads, "fine_unit"
    )
    large = all_sum(large)
    small = all_sum(jnp.concatenate([fine_part, mid_part, lift]))
    grads = unpack(large, small)
    return (fine_input, mid_input, jnp.transpose(coarse_input, (2, 0, 1)), *grads)


def solution(mesh):
    tiled = P(None, "row", "col")
    return jax.shard_map(
        on_device,
        mesh=mesh,
        in_specs=(tiled,) * 11 + (P(),) * 8,
        out_specs=(tiled,) * 3 + (P(),) * 8,
        check_vma=False,
    )
```

profile of v0, /device:TPU:1, one launch (start us, length us, event | category | flops | bytes accessed | tf_op | source)
XLA Modules:
  0.0 167.3 jit_solution(14554121697722064410)
XLA Ops:
  0.6 1.4 copy.39.lift_mid
  2.1 1.5 copy.40.lift_coarse
  3.5 6.1 %prep.1 = (bf16[1536,256]{1,0:T(8,128)(2,1)}, bf16[1536,128]{1,0:T(8,128)(2,1)}, bf16[8,64,192]{2,1,0:T(8,128)(2,1)}, bf16[896,128]{1,0:T(8,128)(2,1)}, bf16[896...) custom-call(bf16[48,32,256]{2,1,0:T(8,128)(2,1)} %grad.1, ...), custom_call_target="tpu_custom_call" | custom-call | tf_op jit(solution)/shard_map/prep/pallas_call | solution.py:200
  9.7 4.7 %collective-permute-start.6 = (bf16[256,128]{1,0:T(8,128)(2,1)}, bf16[256,128]{1,0:T(8,128)(2,1)S(1)}, u32[]{:S(2)}, u32[]{:S(2)}) collective-permute-start(bf16[256,128]{1,0:T(8,128)(2,1)} %get-tuple-element.36), channel_id=1, source_target_pairs={{4,1},{5,2},{6,3},{8,5},{9,6},{10,7},{12,9},{13,10},{14,11},{16,13... | collective-permute-start | bytes 196616 | tf_op jit(solution)/shard_map/ppermute | solution.py:40
  14.4 3.8 %collective-permute-start.4 = (bf16[256,128]{1,0:T(8,128)(2,1)}, bf16[256,128]{1,0:T(8,128)(2,1)S(1)}, u32[]{:S(2)}, u32[]{:S(2)}) collective-permute-start(bf16[256,128]{1,0:T(8,128)(2,1)} %get-tuple-element.36), channel_id=1, source_target_pairs={{0,5},{1,6},{2,7},{4,9},{5,10},{6,11},{8,13},{9,14},{10,15},{12,17... | collective-permute-start | bytes 196616 | tf_op jit(solution)/shard_map/ppermute | solution.py:40
  18.2 2.9 %collective-permute-start.2 = (bf16[256,128]{1,0:T(8,128)(2,1)}, bf16[256,128]{1,0:T(8,128)(2,1)S(1)}, u32[]{:S(2)}, u32[]{:S(2)}) collective-permute-start(bf16[256,128]{1,0:T(8,128)(2,1)} %get-tuple-element.36), channel_id=1, source_target_pairs={{0,1},{1,2},{2,3},{4,5},{5,6},{6,7},{8,9},{9,10},{10,11},{12,13},{... | collective-permute-start | bytes 196616 | tf_op jit(solution)/shard_map/ppermute | solution.py:40
  21.1 3.5 %collective-permute-start = (bf16[896,128]{1,0:T(8,128)(2,1)}, bf16[896,128]{1,0:T(8,128)(2,1)S(1)}, u32[]{:S(2)}, u32[]{:S(2)}) collective-permute-start(bf16[896,128]{1,0:T(8,128)(2,1)} %get-tuple-element.34), channel_id=1, source_target_pairs={{0,4},{1,5},{2,6},{3,7},{4,8},{5,9},{6,10},{7,11},{8,12},{9,13},{1... | collective-permute-start | bytes 688136 | tf_op jit(solution)/shard_map/ppermute | solution.py:40
  24.6 1.9 %collective-permute-start.1 = (bf16[896,128]{1,0:T(8,128)(2,1)}, bf16[896,128]{1,0:T(8,128)(2,1)S(1)}, u32[]{:S(2)}, u32[]{:S(2)}) collective-permute-start(bf16[896,128]{1,0:T(8,128)(2,1)} %get-tuple-element.35), channel_id=1, source_target_pairs={{4,0},{5,1},{6,2},{7,3},{8,4},{9,5},{10,6},{11,7},{12,8},{13,9},{1... | collective-permute-start | bytes 688136 | tf_op jit(solution)/shard_map/ppermute | solution.py:40
  29.4 1.3 collective-permute-start.7
  30.7 1.3 collective-permute-start.5
  32.0 1.3 collective-permute-start.3
  34.4 2.1 %collective-permute-done.7.refs_10_.bottom_rt = bf16[256,128]{1,0:T(8,128)(2,1)S(1)} collective-permute-done((bf16[256,128]{1,0:T(8,128)(2,1)S(1)}, bf16[256,128]{1,0:T(8,128)(2,1)S(1)}, u32[]{:S(2)}, u32[]{:S(2)}) %collective-permute-start.7) | collective-permute-done | bytes 65568 | tf_op jit(solution)/shard_map/ppermute | solution.py:40
  36.5 2.6 %collective-permute-done.3.refs_6_.rt = bf16[256,128]{1,0:T(8,128)(2,1)S(1)} collective-permute-done((bf16[256,128]{1,0:T(8,128)(2,1)S(1)}, bf16[256,128]{1,0:T(8,128)(2,1)S(1)}, u32[]{:S(2)}, u32[]{:S(2)}) %collective-permute-start.3) | collective-permute-done | bytes 65568 | tf_op jit(solution)/shard_map/ppermute | solution.py:40
  39.9 15.6 %fine_unit.1 = (bf16[48,32,256]{2,1,0:T(8,128)(2,1)}, bf16[432,128]{1,0:T(8,128)(2,1)}) custom-call(bf16[48,32,256]{2,1,0:T(8,128)(2,1)} %refs_0_.2, bf16[48,32,256]{2,1,0:T(8,128)(2,1)} %refs_1_.2, bf16[1536,256]{1,0:T(8,128)(2,1)} %get-tuple-element.33.refs_2_, bf16[896,128]{1,0:T(8,128)(2,1)} %copy-done, bf16[896,128]{1,0:T(8,128)(2,1)} %copy-done.1, ...), custom_call_target="tpu_custom_call" | custom-call | tf_op jit(solution)/shard_map/fine_unit/pallas_call | solution.py:327
  55.6 12.4 %mid_unit.1 = (bf16[96,16,128]{2,1,0:T(8,128)(2,1)}, bf16[1728,128]{1,0:T(8,128)(2,1)}) custom-call(bf16[96,16,128]{2,1,0:T(8,128)(2,1)} %refs_0_.3, bf16[96,16,128]{2,1,0:T(8,128)(2,1)} %refs_1_.3, bf16[1536,128]{1,0:T(8,128)(2,1)} %get-tuple-element.39.refs_2_, bf16[896,128]{1,0:T(8,128)(2,1)} %copy-done, bf16[896,128]{1,0:T(8,128)(2,1)} %copy-done.1, ...), custom_call_target="tpu_custom_call" | custom-call | tf_op jit(solution)/shard_map/mid_unit/pallas_call | solution.py:327
  69.3 1.5 collective-permute-done.25
  70.9 6.0 %collective-permute-start.26 = (bf16[288,128]{1,0:T(8,128)(2,1)S(1)}, bf16[288,128]{1,0:T(8,128)(2,1)S(1)}, u32[]{:S(2)}, u32[]{:S(2)}) collective-permute-start(bf16[288,128]{1,0:T(8,128)(2,1)S(1)} %get-tuple-element.84), channel_id=1, source_target_pairs={{0,1},{1,0},{2,3},{3,2},{4,36},{5,37},{6,38},{7,39},{8,9},{9,8},{1... | collective-permute-start | bytes 221192 | tf_op jit(solution)/shard_map/ppermute | solution.py:40
  76.9 1.8 %collective-permute-start.28 = (bf16[288,128]{1,0:T(8,128)(2,1)S(1)}, bf16[288,128]{1,0:T(8,128)(2,1)S(1)}, u32[]{:S(2)}, u32[]{:S(2)}) collective-permute-start(bf16[288,128]{1,0:T(8,128)(2,1)S(1)} %get-tuple-element.85), channel_id=1, source_target_pairs={{0,3},{1,2},{2,1},{3,0},{4,100},{5,101},{6,102},{7,103},{8,11},{9,... | collective-permute-start | bytes 221192 | tf_op jit(solution)/shard_map/ppermute | solution.py:40
  79.7 8.2 %coarse_unit.1 = (bf16[8,64,192]{2,1,0:T(8,128)(2,1)}, bf16[5376,128]{1,0:T(8,128)(2,1)}) custom-call(bf16[8,64,192]{2,1,0:T(8,128)(2,1)} %bitcast.129, bf16[8,64,192]{2,1,0:T(8,128)(2,1)} %bitcast.115, bf16[8,64,192]{2,1,0:T(8,128)(2,1)} %get-tuple-element.41.masked, bf16[896,128]{1,0:T(8,128)(2,1)} %copy-done, bf16[896,128]{1,0:T(8,128)(2,1)} %copy-done.1, ...), custom_call_target="tpu_custom_call" | custom-call | tf_op jit(solution)/shard_map/coarse_unit/pallas_call | solution.py:445
  89.1 2.2 %collective-permute-start.30 = (bf16[72,128]{1,0:T(8,128)(2,1)S(1)}, bf16[72,128]{1,0:T(8,128)(2,1)S(1)}, u32[]{:S(2)}, u32[]{:S(2)}) collective-permute-start(bf16[72,128]{1,0:T(8,128)(2,1)S(1)} %get-tuple-element.92), channel_id=1, source_target_pairs={{0,64},{1,65},{2,66},{3,67},{4,20},{5,21},{6,22},{7,23},{8,72},{9,... | collective-permute-start | bytes 55304 | tf_op jit(solution)/shard_map/ppermute | solution.py:40
  92.4 2.3 %collective-permute-start.8 = (bf16[2688,128]{1,0:T(8,128)(2,1)S(1)}, bf16[2688,128]{1,0:T(8,128)(2,1)S(1)}, u32[]{:S(2)}, u32[]{:S(2)}) collective-permute-start(bf16[2688,128]{1,0:T(8,128)(2,1)S(1)} %dynamic-slice_bitcast_fusion), channel_id=1, source_target_pairs={{0,4},{1,5},{2,6},{3,7},{4,0},{5,1},{6,2},{7,3},{8,12},{9,13},{10,... | collective-permute-start | bytes 2064392 | tf_op jit(solution)/shard_map/ppermute | solution.py:40
  94.7 1.7 %collective-permute-start.34 = (bf16[72,128]{1,0:T(8,128)(2,1)S(1)}, bf16[72,128]{1,0:T(8,128)(2,1)S(1)}, u32[]{:S(2)}, u32[]{:S(2)}) collective-permute-start(bf16[72,128]{1,0:T(8,128)(2,1)S(1)} %fusion.9), channel_id=1, source_target_pairs={{0,24},{1,25},{2,26},{3,27},{4,7},{5,6},{6,5},{7,4},{8,16},{9,17},... | collective-permute-start | bytes 55304 | tf_op jit(solution)/shard_map/ppermute | solution.py:40
  96.4 1.8 %collective-permute-start.33 = (bf16[72,128]{1,0:T(8,128)(2,1)S(1)}, bf16[72,128]{1,0:T(8,128)(2,1)S(1)}, u32[]{:S(2)}, u32[]{:S(2)}) collective-permute-start(bf16[72,128]{1,0:T(8,128)(2,1)S(1)} %fusion.9), channel_id=1, source_target_pairs={{0,16},{1,17},{2,18},{3,19},{4,6},{5,7},{6,4},{7,5},{8,24},{9,25},... | collective-permute-start | bytes 55304 | tf_op jit(solution)/shard_map/ppermute | solution.py:40
  98.6 1.9 %collective-permute-done.33 = bf16[72,128]{1,0:T(8,128)(2,1)S(1)} collective-permute-done((bf16[72,128]{1,0:T(8,128)(2,1)S(1)}, bf16[72,128]{1,0:T(8,128)(2,1)S(1)}, u32[]{:S(2)}, u32[]{:S(2)}) %collective-permute-start.33) | collective-permute-done | bytes 18464 | tf_op jit(solution)/shard_map/ppermute | solution.py:40
  101.0 2.5 %collective-permute-start.36 = (bf16[72,128]{1,0:T(8,128)(2,1)S(1)}, bf16[72,128]{1,0:T(8,128)(2,1)S(1)}, u32[]{:S(2)}, u32[]{:S(2)}) collective-permute-start(bf16[72,128]{1,0:T(8,128)(2,1)S(1)} %get-tuple-element.78), channel_id=1, source_target_pairs={{0,64},{1,65},{2,66},{3,67},{4,20},{5,21},{6,22},{7,23},{8,72},{9,... | collective-permute-start | bytes 55304 | tf_op jit(solution)/shard_map/ppermute | solution.py:40
  103.6 1.3 collective-permute-start.37
  106.0 1.8 %collective-permute-start.11 = (bf16[672,128]{1,0:T(8,128)(2,1)S(1)}, bf16[672,128]{1,0:T(8,128)(2,1)S(1)}, u32[]{:S(2)}, u32[]{:S(2)}) collective-permute-start(bf16[672,128]{1,0:T(8,128)(2,1)S(1)} %get-tuple-element.82), channel_id=1, source_target_pairs={{0,3},{1,2},{2,1},{3,0},{4,100},{5,101},{6,102},{7,103},{8,11},{9,... | collective-permute-start | bytes 516104 | tf_op jit(solution)/shard_map/ppermute | solution.py:40
  108.9 1.3 collective-permute-done.9
  110.2 2.1 %collective-permute-done.11 = bf16[672,128]{1,0:T(8,128)(2,1)S(1)} collective-permute-done((bf16[672,128]{1,0:T(8,128)(2,1)S(1)}, bf16[672,128]{1,0:T(8,128)(2,1)S(1)}, u32[]{:S(2)}, u32[]{:S(2)}) %collective-permute-start.11) | collective-permute-done | bytes 172064 | tf_op jit(solution)/shard_map/ppermute | solution.py:40
  112.3 1.5 collective-permute-done.10
  114.0 1.9 %collective-permute-start.14 = (bf16[168,128]{1,0:T(8,128)(2,1)S(1)}, bf16[168,128]{1,0:T(8,128)(2,1)S(1)}, u32[]{:S(2)}, u32[]{:S(2)}) collective-permute-start(bf16[168,128]{1,0:T(8,128)(2,1)S(1)} %get-tuple-element.88), channel_id=1, source_target_pairs={{0,96},{1,97},{2,98},{3,99},{4,28},{5,29},{6,30},{7,31},{8,104},{9... | collective-permute-start | bytes 129032 | tf_op jit(solution)/shard_map/ppermute | solution.py:40
  115.9 1.4 collective-permute-start.13
  117.3 1.7 collective-permute-start.40
  120.6 1.8 %collective-permute-start.17 = (bf16[168,128]{1,0:T(8,128)(2,1)S(1)}, bf16[168,128]{1,0:T(8,128)(2,1)S(1)}, u32[]{:S(2)}, u32[]{:S(2)}) collective-permute-start(bf16[168,128]{1,0:T(8,128)(2,1)S(1)} %fusion.7), channel_id=1, source_target_pairs={{0,24},{1,25},{2,26},{3,27},{4,7},{5,6},{6,5},{7,4},{8,16},{9,17},... | collective-permute-start | bytes 129032 | tf_op jit(solution)/shard_map/ppermute | solution.py:40
  124.8 2.0 %collective-permute-done.16 = bf16[168,128]{1,0:T(8,128)(2,1)S(1)} collective-permute-done((bf16[168,128]{1,0:T(8,128)(2,1)S(1)}, bf16[168,128]{1,0:T(8,128)(2,1)S(1)}, u32[]{:S(2)}, u32[]{:S(2)}) %collective-permute-start.16) | collective-permute-done | bytes 43040 | tf_op jit(solution)/shard_map/ppermute | solution.py:40
  128.1 1.8 %collective-permute-start.19 = (bf16[168,128]{1,0:T(8,128)(2,1)S(1)}, bf16[168,128]{1,0:T(8,128)(2,1)S(1)}, u32[]{:S(2)}, u32[]{:S(2)}) collective-permute-start(bf16[168,128]{1,0:T(8,128)(2,1)S(1)} %get-tuple-element.80), channel_id=1, source_target_pairs={{0,64},{1,65},{2,66},{3,67},{4,20},{5,21},{6,22},{7,23},{8,72},{9,... | collective-permute-start | bytes 129032 | tf_op jit(solution)/shard_map/ppermute | solution.py:40
  131.0 1.9 %collective-permute-done.19 = bf16[168,128]{1,0:T(8,128)(2,1)S(1)} collective-permute-done((bf16[168,128]{1,0:T(8,128)(2,1)S(1)}, bf16[168,128]{1,0:T(8,128)(2,1)S(1)}, u32[]{:S(2)}, u32[]{:S(2)}) %collective-permute-start.19) | collective-permute-done | bytes 43040 | tf_op jit(solution)/shard_map/ppermute | solution.py:40
  132.9 1.7 %collective-permute-done.20 = bf16[168,128]{1,0:T(8,128)(2,1)S(1)} collective-permute-done((bf16[168,128]{1,0:T(8,128)(2,1)S(1)}, bf16[168,128]{1,0:T(8,128)(2,1)S(1)}, u32[]{:S(2)}, u32[]{:S(2)}) %collective-permute-start.20) | collective-permute-done | bytes 43040 | tf_op jit(solution)/shard_map/ppermute | solution.py:40
  135.5 1.5 collective-permute-start.23
  136.9 1.3 collective-permute-start.22
  138.3 1.3 collective-permute-done.21
  139.7 3.4 %collective-permute-done.22 = bf16[672,128]{1,0:T(8,128)(2,1)S(1)} collective-permute-done((bf16[672,128]{1,0:T(8,128)(2,1)S(1)}, bf16[672,128]{1,0:T(8,128)(2,1)S(1)}, u32[]{:S(2)}, u32[]{:S(2)}) %collective-permute-start.22) | collective-permute-done | bytes 172064 | tf_op jit(solution)/shard_map/ppermute | solution.py:40
  143.5 12.1 %collective-permute-start.24 = (bf16[2688,128]{1,0:T(8,128)(2,1)S(1)}, bf16[2688,128]{1,0:T(8,128)(2,1)S(1)}, u32[]{:S(2)}, u32[]{:S(2)}) collective-permute-start(bf16[2688,128]{1,0:T(8,128)(2,1)S(1)} %bitcast.104), channel_id=1, source_target_pairs={{0,4},{1,5},{2,6},{3,7},{4,0},{5,1},{6,2},{7,3},{8,12},{9,13},{10,... | collective-permute-start | bytes 2064392 | tf_op jit(solution)/shard_map/ppermute | solution.py:40
  155.8 2.1 %collective-permute-done.41 = bf16[1152,128]{1,0:T(8,128)(2,1)S(1)} collective-permute-done((bf16[1152,128]{1,0:T(8,128)(2,1)S(1)}, bf16[1152,128]{1,0:T(8,128)(2,1)S(1)}, u32[]{:S(2)}, u32[]{:S(2)}) %collective-permute-start.41) | collective-permute-done | bytes 294944 | tf_op jit(solution)/shard_map/ppermute | solution.py:40
  158.8 1.5 maximum_select_fusion.large
  160.3 3.9 %unpack.1 = (f32[3,3,48,48]{3,2,1,0:T(8,128)}, f32[3,3,48,48]{3,2,1,0:T(8,128)}, f32[3,3,96,96]{3,2,1,0:T(8,128)}, f32[3,3,96,96]{3,2,1,0:T(8,128)}, f32[3,3,192...) custom-call(bf16[5376,128]{1,0:T(8,128)(2,1)} %maximum_select_fusion.large, ...), custom_call_target="tpu_custom_call" | custom-call | tf_op jit(solution)/shard_map/unpack/pallas_call | solution.py:486
  164.2 1.5 copy.45
  165.7 1.6 copy.46
  (124 shorter events, 21.4 us)
Async XLA Ops:
  3.5 23.1 %copy-start.12 = (bf16[3,3,48,48]{3,2,1,0:T(8,128)(2,1)S(1)}, bf16[3,3,48,48]{3,2,1,0:T(8,128)(2,1)}, u32[]{:S(2)}) copy-start(bf16[3,3,48,48]{3,2,1,0:T(8,128)(2,1)} %param.31) | copy-start | bytes 124420
  3.5 24.0 %copy-start.13 = (bf16[3,3,48,48]{3,2,1,0:T(8,128)(2,1)S(1)}, bf16[3,3,48,48]{3,2,1,0:T(8,128)(2,1)}, u32[]{:S(2)}) copy-start(bf16[3,3,48,48]{3,2,1,0:T(8,128)(2,1)} %param.32) | copy-start | bytes 124420
  9.7 18.6 %copy-start.9 = (bf16[3,3,96,96]{3,2,1,0:T(8,128)(2,1)S(1)}, bf16[3,3,96,96]{3,2,1,0:T(8,128)(2,1)}, u32[]{:S(2)}) copy-start(bf16[3,3,96,96]{3,2,1,0:T(8,128)(2,1)} %param.33) | copy-start | bytes 497668
  9.7 19.7 %collective-permute-start.6 = (bf16[256,128]{1,0:T(8,128)(2,1)}, bf16[256,128]{1,0:T(8,128)(2,1)S(1)}, u32[]{:S(2)}, u32[]{:S(2)}) collective-permute-start(bf16[256,128]{1,0:T(8,128)(2,1)} %get-tuple-element.36), channel_id=1, source_target_pairs={{4,1},{5,2},{6,3},{8,5},{9,6},{10,7},{12,9},{13,10},{14,11},{16,13... | collective-permute-start | bytes 196616 | tf_op jit(solution)/shard_map/ppermute | solution.py:40
  14.4 16.3 %collective-permute-start.4 = (bf16[256,128]{1,0:T(8,128)(2,1)}, bf16[256,128]{1,0:T(8,128)(2,1)S(1)}, u32[]{:S(2)}, u32[]{:S(2)}) collective-permute-start(bf16[256,128]{1,0:T(8,128)(2,1)} %get-tuple-element.36), channel_id=1, source_target_pairs={{0,5},{1,6},{2,7},{4,9},{5,10},{6,11},{8,13},{9,14},{10,15},{12,17... | collective-permute-start | bytes 196616 | tf_op jit(solution)/shard_map/ppermute | solution.py:40
  18.2 13.8 %collective-permute-start.2 = (bf16[256,128]{1,0:T(8,128)(2,1)}, bf16[256,128]{1,0:T(8,128)(2,1)S(1)}, u32[]{:S(2)}, u32[]{:S(2)}) collective-permute-start(bf16[256,128]{1,0:T(8,128)(2,1)} %get-tuple-element.36), channel_id=1, source_target_pairs={{0,1},{1,2},{2,3},{4,5},{5,6},{6,7},{8,9},{9,10},{10,11},{12,13},{... | collective-permute-start | bytes 196616 | tf_op jit(solution)/shard_map/ppermute | solution.py:40
  21.1 18.0 %collective-permute-start = (bf16[896,128]{1,0:T(8,128)(2,1)}, bf16[896,128]{1,0:T(8,128)(2,1)S(1)}, u32[]{:S(2)}, u32[]{:S(2)}) collective-permute-start(bf16[896,128]{1,0:T(8,128)(2,1)} %get-tuple-element.34), channel_id=1, source_target_pairs={{0,4},{1,5},{2,6},{3,7},{4,8},{5,9},{6,10},{7,11},{8,12},{9,13},{1... | collective-permute-start | bytes 688136 | tf_op jit(solution)/shard_map/ppermute | solution.py:40
  24.6 14.5 %collective-permute-start.1 = (bf16[896,128]{1,0:T(8,128)(2,1)}, bf16[896,128]{1,0:T(8,128)(2,1)S(1)}, u32[]{:S(2)}, u32[]{:S(2)}) collective-permute-start(bf16[896,128]{1,0:T(8,128)(2,1)} %get-tuple-element.35), channel_id=1, source_target_pairs={{4,0},{5,1},{6,2},{7,3},{8,4},{9,5},{10,6},{11,7},{12,8},{13,9},{1... | collective-permute-start | bytes 688136 | tf_op jit(solution)/shard_map/ppermute | solution.py:40
  29.4 7.2 %collective-permute-start.7 = (bf16[256,128]{1,0:T(8,128)(2,1)S(1)}, bf16[256,128]{1,0:T(8,128)(2,1)S(1)}, u32[]{:S(2)}, u32[]{:S(2)}) collective-permute-start(bf16[256,128]{1,0:T(8,128)(2,1)S(1)} %copy-done.15), channel_id=1, source_target_pairs={{5,0},{6,1},{7,2},{9,4},{10,5},{11,6},{13,8},{14,9},{15,10},{17,12... | collective-permute-start | bytes 196616 | tf_op jit(solution)/shard_map/ppermute | solution.py:40
  30.7 5.8 %collective-permute-start.5 = (bf16[256,128]{1,0:T(8,128)(2,1)S(1)}, bf16[256,128]{1,0:T(8,128)(2,1)S(1)}, u32[]{:S(2)}, u32[]{:S(2)}) collective-permute-start(bf16[256,128]{1,0:T(8,128)(2,1)S(1)} %copy-done.15), channel_id=1, source_target_pairs={{1,4},{2,5},{3,6},{5,8},{6,9},{7,10},{9,12},{10,13},{11,14},{13,16... | collective-permute-start | bytes 196616 | tf_op jit(solution)/shard_map/ppermute | solution.py:40
  32.0 7.1 %collective-permute-start.3 = (bf16[256,128]{1,0:T(8,128)(2,1)S(1)}, bf16[256,128]{1,0:T(8,128)(2,1)S(1)}, u32[]{:S(2)}, u32[]{:S(2)}) collective-permute-start(bf16[256,128]{1,0:T(8,128)(2,1)S(1)} %copy-done.15), channel_id=1, source_target_pairs={{1,0},{2,1},{3,2},{5,4},{6,5},{7,6},{9,8},{10,9},{11,10},{13,12},{... | collective-permute-start | bytes 196616 | tf_op jit(solution)/shard_map/ppermute | solution.py:40
  55.6 12.5 %copy-start.11 = (bf16[432,128]{1,0:T(8,128)(2,1)S(1)}, bf16[432,128]{1,0:T(8,128)(2,1)}, u32[]{:S(2)}) copy-start(bf16[432,128]{1,0:T(8,128)(2,1)} %get-tuple-element.44) | copy-start | bytes 331780
  55.6 12.5 %copy-start.14 = (bf16[144,128]{1,0:T(8,128)(2,1)S(1)}, bf16[144,128]{1,0:T(8,128)(2,1)}, u32[]{:S(2)}) copy-start(bf16[144,128]{1,0:T(8,128)(2,1)} %get-tuple-element.46) | copy-start | bytes 110596
  69.1 1.7 collective-permute-start.25
  70.9 17.0 %collective-permute-start.26 = (bf16[288,128]{1,0:T(8,128)(2,1)S(1)}, bf16[288,128]{1,0:T(8,128)(2,1)S(1)}, u32[]{:S(2)}, u32[]{:S(2)}) collective-permute-start(bf16[288,128]{1,0:T(8,128)(2,1)S(1)} %get-tuple-element.84), channel_id=1, source_target_pairs={{0,1},{1,0},{2,3},{3,2},{4,36},{5,37},{6,38},{7,39},{8,9},{9,8},{1... | collective-permute-start | bytes 221192 | tf_op jit(solution)/shard_map/ppermute | solution.py:40
  76.9 10.9 %collective-permute-start.28 = (bf16[288,128]{1,0:T(8,128)(2,1)S(1)}, bf16[288,128]{1,0:T(8,128)(2,1)S(1)}, u32[]{:S(2)}, u32[]{:S(2)}) collective-permute-start(bf16[288,128]{1,0:T(8,128)(2,1)S(1)} %get-tuple-element.85), channel_id=1, source_target_pairs={{0,3},{1,2},{2,1},{3,0},{4,100},{5,101},{6,102},{7,103},{8,11},{9,... | collective-permute-start | bytes 221192 | tf_op jit(solution)/shard_map/ppermute | solution.py:40
  78.7 9.1 %collective-permute-start.27 = (bf16[288,128]{1,0:T(8,128)(2,1)S(1)}, bf16[288,128]{1,0:T(8,128)(2,1)S(1)}, u32[]{:S(2)}, u32[]{:S(2)}) collective-permute-start(bf16[288,128]{1,0:T(8,128)(2,1)S(1)} %get-tuple-element.86), channel_id=1, source_target_pairs={{0,2},{1,3},{2,0},{3,1},{4,68},{5,69},{6,70},{7,71},{8,10},{9,11},... | collective-permute-start | bytes 221192 | tf_op jit(solution)/shard_map/ppermute | solution.py:40
  87.9 17.0 %copy-start.2 = (bf16[5376,128]{1,0:T(8,128)(2,1)S(1)}, bf16[5376,128]{1,0:T(8,128)(2,1)}, u32[]{:S(2)}) copy-start(bf16[5376,128]{1,0:T(8,128)(2,1)} %get-tuple-element.43) | copy-start | bytes 4128772
  88.0 6.7 %collective-permute-start.29 = (bf16[72,128]{1,0:T(8,128)(2,1)S(1)}, bf16[72,128]{1,0:T(8,128)(2,1)S(1)}, u32[]{:S(2)}, u32[]{:S(2)}) collective-permute-start(bf16[72,128]{1,0:T(8,128)(2,1)S(1)} %get-tuple-element.90), channel_id=1, source_target_pairs={{0,32},{1,33},{2,34},{3,35},{4,12},{5,13},{6,14},{7,15},{8,40},{9,... | collective-permute-start | bytes 55304 | tf_op jit(solution)/shard_map/ppermute | solution.py:40
  88.0 6.6 %collective-permute-start.31 = (bf16[72,128]{1,0:T(8,128)(2,1)S(1)}, bf16[72,128]{1,0:T(8,128)(2,1)S(1)}, u32[]{:S(2)}, u32[]{:S(2)}) collective-permute-start(bf16[72,128]{1,0:T(8,128)(2,1)S(1)} %get-tuple-element.91), channel_id=1, source_target_pairs={{0,96},{1,97},{2,98},{3,99},{4,28},{5,29},{6,30},{7,31},{8,104},{9... | collective-permute-start | bytes 55304 | tf_op jit(solution)/shard_map/ppermute | solution.py:40
  89.1 5.6 %collective-permute-start.30 = (bf16[72,128]{1,0:T(8,128)(2,1)S(1)}, bf16[72,128]{1,0:T(8,128)(2,1)S(1)}, u32[]{:S(2)}, u32[]{:S(2)}) collective-permute-start(bf16[72,128]{1,0:T(8,128)(2,1)S(1)} %get-tuple-element.92), channel_id=1, source_target_pairs={{0,64},{1,65},{2,66},{3,67},{4,20},{5,21},{6,22},{7,23},{8,72},{9,... | collective-permute-start | bytes 55304 | tf_op jit(solution)/shard_map/ppermute | solution.py:40
  92.4 12.4 %collective-permute-start.8 = (bf16[2688,128]{1,0:T(8,128)(2,1)S(1)}, bf16[2688,128]{1,0:T(8,128)(2,1)S(1)}, u32[]{:S(2)}, u32[]{:S(2)}) collective-permute-start(bf16[2688,128]{1,0:T(8,128)(2,1)S(1)} %dynamic-slice_bitcast_fusion), channel_id=1, source_target_pairs={{0,4},{1,5},{2,6},{3,7},{4,0},{5,1},{6,2},{7,3},{8,12},{9,13},{10,... | collective-permute-start | bytes 2064392 | tf_op jit(solution)/shard_map/ppermute | solution.py:40
  94.7 3.9 %collective-permute-start.34 = (bf16[72,128]{1,0:T(8,128)(2,1)S(1)}, bf16[72,128]{1,0:T(8,128)(2,1)S(1)}, u32[]{:S(2)}, u32[]{:S(2)}) collective-permute-start(bf16[72,128]{1,0:T(8,128)(2,1)S(1)} %fusion.9), channel_id=1, source_target_pairs={{0,24},{1,25},{2,26},{3,27},{4,7},{5,6},{6,5},{7,4},{8,16},{9,17},... | collective-permute-start | bytes 55304 | tf_op jit(solution)/shard_map/ppermute | solution.py:40
  96.4 4.1 %collective-permute-start.33 = (bf16[72,128]{1,0:T(8,128)(2,1)S(1)}, bf16[72,128]{1,0:T(8,128)(2,1)S(1)}, u32[]{:S(2)}, u32[]{:S(2)}) collective-permute-start(bf16[72,128]{1,0:T(8,128)(2,1)S(1)} %fusion.9), channel_id=1, source_target_pairs={{0,16},{1,17},{2,18},{3,19},{4,6},{5,7},{6,4},{7,5},{8,24},{9,25},... | collective-permute-start | bytes 55304 | tf_op jit(solution)/shard_map/ppermute | solution.py:40
  98.3 2.6 %collective-permute-start.32 = (bf16[72,128]{1,0:T(8,128)(2,1)S(1)}, bf16[72,128]{1,0:T(8,128)(2,1)S(1)}, u32[]{:S(2)}, u32[]{:S(2)}) collective-permute-start(bf16[72,128]{1,0:T(8,128)(2,1)S(1)} %fusion.9), channel_id=1, source_target_pairs={{0,8},{1,9},{2,10},{3,11},{4,5},{5,4},{6,7},{7,6},{8,0},{9,1},{10,... | collective-permute-start | bytes 55304 | tf_op jit(solution)/shard_map/ppermute | solution.py:40
  100.9 3.9 %collective-permute-start.35 = (bf16[72,128]{1,0:T(8,128)(2,1)S(1)}, bf16[72,128]{1,0:T(8,128)(2,1)S(1)}, u32[]{:S(2)}, u32[]{:S(2)}) collective-permute-start(bf16[72,128]{1,0:T(8,128)(2,1)S(1)} %get-tuple-element.78), channel_id=1, source_target_pairs={{0,32},{1,33},{2,34},{3,35},{4,12},{5,13},{6,14},{7,15},{8,40},{9,... | collective-permute-start | bytes 55304 | tf_op jit(solution)/shard_map/ppermute | solution.py:40
  101.0 7.8 %collective-permute-start.36 = (bf16[72,128]{1,0:T(8,128)(2,1)S(1)}, bf16[72,128]{1,0:T(8,128)(2,1)S(1)}, u32[]{:S(2)}, u32[]{:S(2)}) collective-permute-start(bf16[72,128]{1,0:T(8,128)(2,1)S(1)} %get-tuple-element.78), channel_id=1, source_target_pairs={{0,64},{1,65},{2,66},{3,67},{4,20},{5,21},{6,22},{7,23},{8,72},{9,... | collective-permute-start | bytes 55304 | tf_op jit(solution)/shard_map/ppermute | solution.py:40
  103.6 13.7 %collective-permute-start.37 = (bf16[72,128]{1,0:T(8,128)(2,1)S(1)}, bf16[72,128]{1,0:T(8,128)(2,1)S(1)}, u32[]{:S(2)}, u32[]{:S(2)}) collective-permute-start(bf16[72,128]{1,0:T(8,128)(2,1)S(1)} %get-tuple-element.78), channel_id=1, source_target_pairs={{0,96},{1,97},{2,98},{3,99},{4,28},{5,29},{6,30},{7,31},{8,104},{9... | collective-permute-start | bytes 55304 | tf_op jit(solution)/shard_map/ppermute | solution.py:40
  105.1 5.0 %collective-permute-start.9 = (bf16[672,128]{1,0:T(8,128)(2,1)S(1)}, bf16[672,128]{1,0:T(8,128)(2,1)S(1)}, u32[]{:S(2)}, u32[]{:S(2)}) collective-permute-start(bf16[672,128]{1,0:T(8,128)(2,1)S(1)} %get-tuple-element.81), channel_id=1, source_target_pairs={{0,1},{1,0},{2,3},{3,2},{4,36},{5,37},{6,38},{7,39},{8,9},{9,8},{1... | collective-permute-start | bytes 516104 | tf_op jit(solution)/shard_map/ppermute | solution.py:40
  106.0 6.3 %collective-permute-start.11 = (bf16[672,128]{1,0:T(8,128)(2,1)S(1)}, bf16[672,128]{1,0:T(8,128)(2,1)S(1)}, u32[]{:S(2)}, u32[]{:S(2)}) collective-permute-start(bf16[672,128]{1,0:T(8,128)(2,1)S(1)} %get-tuple-element.82), channel_id=1, source_target_pairs={{0,3},{1,2},{2,1},{3,0},{4,100},{5,101},{6,102},{7,103},{8,11},{9,... | collective-permute-start | bytes 516104 | tf_op jit(solution)/shard_map/ppermute | solution.py:40
  107.8 6.0 %collective-permute-start.10 = (bf16[672,128]{1,0:T(8,128)(2,1)S(1)}, bf16[672,128]{1,0:T(8,128)(2,1)S(1)}, u32[]{:S(2)}, u32[]{:S(2)}) collective-permute-start(bf16[672,128]{1,0:T(8,128)(2,1)S(1)} %get-tuple-element.83), channel_id=1, source_target_pairs={{0,2},{1,3},{2,0},{3,1},{4,68},{5,69},{6,70},{7,71},{8,10},{9,11},... | collective-permute-start | bytes 516104 | tf_op jit(solution)/shard_map/ppermute | solution.py:40
  113.9 5.7 %collective-permute-start.12 = (bf16[168,128]{1,0:T(8,128)(2,1)S(1)}, bf16[168,128]{1,0:T(8,128)(2,1)S(1)}, u32[]{:S(2)}, u32[]{:S(2)}) collective-permute-start(bf16[168,128]{1,0:T(8,128)(2,1)S(1)} %get-tuple-element.87), channel_id=1, source_target_pairs={{0,32},{1,33},{2,34},{3,35},{4,12},{5,13},{6,14},{7,15},{8,40},{9,... | collective-permute-start | bytes 129032 | tf_op jit(solution)/shard_map/ppermute | solution.py:40
  114.0 5.6 %collective-permute-start.14 = (bf16[168,128]{1,0:T(8,128)(2,1)S(1)}, bf16[168,128]{1,0:T(8,128)(2,1)S(1)}, u32[]{:S(2)}, u32[]{:S(2)}) collective-permute-start(bf16[168,128]{1,0:T(8,128)(2,1)S(1)} %get-tuple-element.88), channel_id=1, source_target_pairs={{0,96},{1,97},{2,98},{3,99},{4,28},{5,29},{6,30},{7,31},{8,104},{9... | collective-permute-start | bytes 129032 | tf_op jit(solution)/shard_map/ppermute | solution.py:40
  115.9 4.7 %collective-permute-start.13 = (bf16[168,128]{1,0:T(8,128)(2,1)S(1)}, bf16[168,128]{1,0:T(8,128)(2,1)S(1)}, u32[]{:S(2)}, u32[]{:S(2)}) collective-permute-start(bf16[168,128]{1,0:T(8,128)(2,1)S(1)} %get-tuple-element.89), channel_id=1, source_target_pairs={{0,64},{1,65},{2,66},{3,67},{4,20},{5,21},{6,22},{7,23},{8,72},{9,... | collective-permute-start | bytes 129032 | tf_op jit(solution)/shard_map/ppermute | solution.py:40
  117.3 38.4 %collective-permute-start.40 = (bf16[288,128]{1,0:T(8,128)(2,1)S(1)}, bf16[288,128]{1,0:T(8,128)(2,1)S(1)}, u32[]{:S(2)}, u32[]{:S(2)}) collective-permute-start(bf16[288,128]{1,0:T(8,128)(2,1)S(1)} %bitcast.122), channel_id=1, source_target_pairs={{0,3},{1,2},{2,1},{3,0},{4,100},{5,101},{6,102},{7,103},{8,11},{9,... | collective-permute-start | bytes 221192 | tf_op jit(solution)/shard_map/ppermute | solution.py:40
  118.9 16.5 %collective-permute-start.39 = (bf16[288,128]{1,0:T(8,128)(2,1)S(1)}, bf16[288,128]{1,0:T(8,128)(2,1)S(1)}, u32[]{:S(2)}, u32[]{:S(2)}) collective-permute-start(bf16[288,128]{1,0:T(8,128)(2,1)S(1)} %bitcast.123), channel_id=1, source_target_pairs={{0,2},{1,3},{2,0},{3,1},{4,68},{5,69},{6,70},{7,71},{8,10},{9,11},... | collective-permute-start | bytes 221192 | tf_op jit(solution)/shard_map/ppermute | solution.py:40
  120.6 4.2 %collective-permute-start.17 = (bf16[168,128]{1,0:T(8,128)(2,1)S(1)}, bf16[168,128]{1,0:T(8,128)(2,1)S(1)}, u32[]{:S(2)}, u32[]{:S(2)}) collective-permute-start(bf16[168,128]{1,0:T(8,128)(2,1)S(1)} %fusion.7), channel_id=1, source_target_pairs={{0,24},{1,25},{2,26},{3,27},{4,7},{5,6},{6,5},{7,4},{8,16},{9,17},... | collective-permute-start | bytes 129032 | tf_op jit(solution)/shard_map/ppermute | solution.py:40
  122.4 4.4 %collective-permute-start.16 = (bf16[168,128]{1,0:T(8,128)(2,1)S(1)}, bf16[168,128]{1,0:T(8,128)(2,1)S(1)}, u32[]{:S(2)}, u32[]{:S(2)}) collective-permute-start(bf16[168,128]{1,0:T(8,128)(2,1)S(1)} %fusion.7), channel_id=1, source_target_pairs={{0,16},{1,17},{2,18},{3,19},{4,6},{5,7},{6,4},{7,5},{8,24},{9,25},... | collective-permute-start | bytes 129032 | tf_op jit(solution)/shard_map/ppermute | solution.py:40
  123.1 3.7 %collective-permute-start.15 = (bf16[168,128]{1,0:T(8,128)(2,1)S(1)}, bf16[168,128]{1,0:T(8,128)(2,1)S(1)}, u32[]{:S(2)}, u32[]{:S(2)}) collective-permute-start(bf16[168,128]{1,0:T(8,128)(2,1)S(1)} %fusion.7), channel_id=1, source_target_pairs={{0,8},{1,9},{2,10},{3,11},{4,5},{5,4},{6,7},{7,6},{8,0},{9,1},{10,... | collective-permute-start | bytes 129032 | tf_op jit(solution)/shard_map/ppermute | solution.py:40
  124.8 3.3 %collective-permute-start.38 = (bf16[288,128]{1,0:T(8,128)(2,1)S(1)}, bf16[288,128]{1,0:T(8,128)(2,1)S(1)}, u32[]{:S(2)}, u32[]{:S(2)}) collective-permute-start(bf16[288,128]{1,0:T(8,128)(2,1)S(1)} %bitcast.125), channel_id=1, source_target_pairs={{0,1},{1,0},{2,3},{3,2},{4,36},{5,37},{6,38},{7,39},{8,9},{9,8},{1... | collective-permute-start | bytes 221192 | tf_op jit(solution)/shard_map/ppermute | solution.py:40
  126.9 4.1 %collective-permute-start.18 = (bf16[168,128]{1,0:T(8,128)(2,1)S(1)}, bf16[168,128]{1,0:T(8,128)(2,1)S(1)}, u32[]{:S(2)}, u32[]{:S(2)}) collective-permute-start(bf16[168,128]{1,0:T(8,128)(2,1)S(1)} %get-tuple-element.80), channel_id=1, source_target_pairs={{0,32},{1,33},{2,34},{3,35},{4,12},{5,13},{6,14},{7,15},{8,40},{9,... | collective-permute-start | bytes 129032 | tf_op jit(solution)/shard_map/ppermute | solution.py:40
  128.1 4.8 %collective-permute-start.19 = (bf16[168,128]{1,0:T(8,128)(2,1)S(1)}, bf16[168,128]{1,0:T(8,128)(2,1)S(1)}, u32[]{:S(2)}, u32[]{:S(2)}) collective-permute-start(bf16[168,128]{1,0:T(8,128)(2,1)S(1)} %get-tuple-element.80), channel_id=1, source_target_pairs={{0,64},{1,65},{2,66},{3,67},{4,20},{5,21},{6,22},{7,23},{8,72},{9,... | collective-permute-start | bytes 129032 | tf_op jit(solution)/shard_map/ppermute | solution.py:40
  129.9 4.6 %collective-permute-start.20 = (bf16[168,128]{1,0:T(8,128)(2,1)S(1)}, bf16[168,128]{1,0:T(8,128)(2,1)S(1)}, u32[]{:S(2)}, u32[]{:S(2)}) collective-permute-start(bf16[168,128]{1,0:T(8,128)(2,1)S(1)} %get-tuple-element.80), channel_id=1, source_target_pairs={{0,96},{1,97},{2,98},{3,99},{4,28},{5,29},{6,30},{7,31},{8,104},{9... | collective-permute-start | bytes 129032 | tf_op jit(solution)/shard_map/ppermute | solution.py:40
  134.6 5.1 %collective-permute-start.21 = (bf16[672,128]{1,0:T(8,128)(2,1)S(1)}, bf16[672,128]{1,0:T(8,128)(2,1)S(1)}, u32[]{:S(2)}, u32[]{:S(2)}) collective-permute-start(bf16[672,128]{1,0:T(8,128)(2,1)S(1)} %bitcast.118), channel_id=1, source_target_pairs={{0,1},{1,0},{2,3},{3,2},{4,36},{5,37},{6,38},{7,39},{8,9},{9,8},{1... | collective-permute-start | bytes 516104 | tf_op jit(solution)/shard_map/ppermute | solution.py:40
  135.5 8.0 %collective-permute-start.23 = (bf16[672,128]{1,0:T(8,128)(2,1)S(1)}, bf16[672,128]{1,0:T(8,128)(2,1)S(1)}, u32[]{:S(2)}, u32[]{:S(2)}) collective-permute-start(bf16[672,128]{1,0:T(8,128)(2,1)S(1)} %bitcast.119), channel_id=1, source_target_pairs={{0,3},{1,2},{2,1},{3,0},{4,100},{5,101},{6,102},{7,103},{8,11},{9,... | collective-permute-start | bytes 516104 | tf_op jit(solution)/shard_map/ppermute | solution.py:40
  136.9 6.1 %collective-permute-start.22 = (bf16[672,128]{1,0:T(8,128)(2,1)S(1)}, bf16[672,128]{1,0:T(8,128)(2,1)S(1)}, u32[]{:S(2)}, u32[]{:S(2)}) collective-permute-start(bf16[672,128]{1,0:T(8,128)(2,1)S(1)} %bitcast.120), channel_id=1, source_target_pairs={{0,2},{1,3},{2,0},{3,1},{4,68},{5,69},{6,70},{7,71},{8,10},{9,11},... | collective-permute-start | bytes 516104 | tf_op jit(solution)/shard_map/ppermute | solution.py:40
  143.5 15.3 %collective-permute-start.24 = (bf16[2688,128]{1,0:T(8,128)(2,1)S(1)}, bf16[2688,128]{1,0:T(8,128)(2,1)S(1)}, u32[]{:S(2)}, u32[]{:S(2)}) collective-permute-start(bf16[2688,128]{1,0:T(8,128)(2,1)S(1)} %bitcast.104), channel_id=1, source_target_pairs={{0,4},{1,5},{2,6},{3,7},{4,0},{5,1},{6,2},{7,3},{8,12},{9,13},{10,... | collective-permute-start | bytes 2064392 | tf_op jit(solution)/shard_map/ppermute | solution.py:40
  155.7 2.2 %collective-permute-start.41 = (bf16[1152,128]{1,0:T(8,128)(2,1)S(1)}, bf16[1152,128]{1,0:T(8,128)(2,1)S(1)}, u32[]{:S(2)}, u32[]{:S(2)}) collective-permute-start(bf16[1152,128]{1,0:T(8,128)(2,1)S(1)} %bitcast.112), channel_id=1, source_target_pairs={{0,4},{1,5},{2,6},{3,7},{4,0},{5,1},{6,2},{7,3},{8,12},{9,13},{10,... | collective-permute-start | bytes 884744 | tf_op jit(solution)/shard_map/ppermute | solution.py:40
  (10 other events, 42.2 us)
where the time goes:
time: 168 us; the launch traced here: 167 us
  starting transfers between devices  75.3 us (45%)
  Pallas kernels  46.3 us (28%)
  waiting for transfers between devices  28.3 us (17%)
  local copies, waits for them, and re-layouts  12.1 us (7%)
  other arithmetic  4.04 us (2%)
    ppermute x42, starting transfers between devices, send(): return lax.ppermute(block, AXES, pairs)  75.3 us
    ppermute x42, waiting for transfers between devices, send(): return lax.ppermute(block, AXES, pairs)  28.3 us
    pallas_call x2, Pallas kernels, channel_unit(): pl.pallas_call(kernel, out_shape=[jax.ShapeDtypeStruct((chans, rows, widt...  28.1 us
    pallas_call x1, Pallas kernels, coarse_unit(): pl.pallas_call(coarse_kernel, out_shape=[jax.ShapeDtypeStruct((COARSE_ROW...  8.18 us
    unnamed x36, local copies, waits for them, and re-layouts  6.74 us
    pallas_call x1, Pallas kernels, prep(): pl.pallas_call(prep_kernel, out_shape=[jax.ShapeDtypeStruct(shape, half)...  6.15 us
    pallas_call x1, Pallas kernels, unpack(): pl.pallas_call(unpack_kernel, out_shape=[jax.ShapeDtypeStruct(shape, jnp....  3.9 us
  transfers between devices with their start and end apart: 42, of which 19 were waited for; matrix products, arithmetic and copies ran while one was open for 4% of the time, Pallas kernels for 5%

commit v1 on v0

v1 whole, which is shorter than its diff:
```python
import jax
import jax.numpy as jnp
import numpy as np
from jax import lax
from jax.experimental import pallas as pl
from jax.experimental.pallas import tpu as pltpu
from jax.sharding import PartitionSpec as P

ROWS, COLS = 32, 4
CELLS = 1536
FINE, MID = 48, 96
COARSE_ROWS, COARSE_COLS, COARSE = 8, 64, 192
PITCH = 80
PARAMS = pltpu.CompilerParams(vmem_limit_bytes=56 * 2**20)

AXES = ("row", "col")
ORDER = (("y", "x", "z"), ("x", "z", "y"))
CORE_PAIRS = [(d, d ^ 4) for d in range(128)]


def stage_pairs(stage, k):
    pairs = []
    for d in range(128):
        row, col = divmod(d, 4)
        at = {"x": row // 8, "z": (row // 2) % 4, "y": col}
        core = row % 2
        at[ORDER[core][stage]] ^= k
        pairs.append((d, (at["x"] * 8 + at["z"] * 2 + core) * 4 + at["y"]))
    return pairs


def my_place():
    row, col = lax.axis_index("row"), lax.axis_index("col")
    at = {"x": row // 8, "z": (row // 2) % 4, "y": col}
    core = row % 2
    return core, [jnp.where(core == 0, at[ORDER[0][s]], at[ORDER[1][s]]) for s in range(3)]


def send(block, pairs):
    return lax.ppermute(block, AXES, pairs)


def add4(own, others):
    a, b, c = [other.astype(jnp.float32) for other in others]
    return ((own.astype(jnp.float32) + a) + (b + c)).astype(jnp.bfloat16)


def scatter_stage(block, stage, mine):
    parts = block.reshape(4, block.shape[0] // 4, block.shape[1])
    own = lax.dynamic_index_in_dim(parts, mine, 0, keepdims=False)
    others = [
        send(lax.dynamic_index_in_dim(parts, mine ^ k, 0, keepdims=False), stage_pairs(stage, k))
        for k in (1, 2, 3)
    ]
    return add4(own, others)


def reduce_stage(block, stage):
    return add4(block, [send(block, stage_pairs(stage, k)) for k in (1, 2, 3)])


def gather_stage(block, stage, mine):
    parts = [block] + [send(block, stage_pairs(stage, k)) for k in (1, 2, 3)]
    whole = jnp.zeros((4,) + block.shape, block.dtype)
    for k in range(4):
        whole = lax.dynamic_update_index_in_dim(whole, parts[k], mine ^ k, 0)
    return whole.reshape(4 * block.shape[0], block.shape[1])


def beside(stage, block, work, *operands):
    block, *operands = lax.optimization_barrier((block, *operands))
    return lax.optimization_barrier((stage(block), work(*operands)))


def all_sum(block, works):
    core, mine = my_place()
    half = block.shape[0] // 2
    halves = block.reshape(2, half, block.shape[1])
    other = send(lax.dynamic_index_in_dim(halves, 1 - core, 0, keepdims=False), CORE_PAIRS)
    own = lax.dynamic_index_in_dim(halves, core, 0, keepdims=False)
    part = (own.astype(jnp.float32) + other.astype(jnp.float32)).astype(jnp.bfloat16)
    part, out_0 = beside(lambda x: scatter_stage(x, 0, mine[0]), part, *works[0])
    part = scatter_stage(part, 1, mine[1])
    part = reduce_stage(part, 2)
    part, out_1 = beside(lambda x: gather_stage(x, 1, mine[1]), part, *works[1])
    part, out_2 = beside(lambda x: gather_stage(x, 0, mine[0]), part, *works[2])
    other = send(part, CORE_PAIRS)
    whole = jnp.where(core == 0, jnp.concatenate([part, other]), jnp.concatenate([other, part]))
    return whole, out_0, out_1, out_2


def partner(at, count, pairing):
    other = at + 1 if at % 2 == pairing else at - 1
    return other if 0 <= other < count else None


def swap_pairs(row_pairing, col_pairing):
    pairs = []
    for row in range(ROWS):
        for col in range(COLS):
            to_row = row if row_pairing is None else partner(row, ROWS, row_pairing)
            to_col = col if col_pairing is None else partner(col, COLS, col_pairing)
            if to_row is not None and to_col is not None:
                pairs.append((row * COLS + col, to_row * COLS + to_col))
    return pairs


def iota(shape, dim):
    return lax.broadcasted_iota(jnp.int32, shape, dim)


def picks(shape, pairs):
    rows, cols = iota(shape, 0), iota(shape, 1)
    hit = jnp.zeros(shape, jnp.bool_)
    for row, col in pairs:
        hit = hit | ((rows == row) & (cols == col))
    return hit.astype(jnp.float32).astype(jnp.bfloat16)


def dot(a, b, a_dim=1, b_dim=0):
    return lax.dot_general(
        a, b, (((a_dim,), (b_dim,)), ((), ())), preferred_element_type=jnp.float32
    )


def keep(gate, value):
    return jnp.where(gate > 0, value, jnp.zeros_like(value))


def prep_kernel(
    parity, grad, joined, unit_fine, inner_fine, unit_mid, inner_mid, unit_coarse, inner_coarse, lift_mid, lift_coarse,
    fine, mid, coarse, row_0, row_1, col_0, col_1, lift, upstream, gate_mid, in_fine, in_mid,
):
    above = keep(joined[...], grad[...])
    upstream[...] = jnp.transpose(above, (1, 0, 2)).reshape(CELLS, 256)
    fine[...] = jnp.transpose(keep(unit_fine[...], above), (1, 0, 2)).reshape(CELLS, 256)
    gate_mid[...] = jnp.transpose(unit_mid[...], (1, 0, 2)).reshape(CELLS, 128)
    in_fine[...] = jnp.transpose(inner_fine[...], (1, 0, 2)).reshape(CELLS, 256)
    in_mid[...] = jnp.transpose(inner_mid[...], (1, 0, 2)).reshape(CELLS, 128)

    cells, target = iota((256, 192), 0), iota((256, 192), 1)
    pooling = jnp.where(target < 128, cells // 2, cells // 4 + 128) == target
    pooling = pooling.astype(jnp.float32).astype(jnp.bfloat16)
    sum_mid = jnp.zeros((FINE, MID), jnp.float32)
    sum_coarse = jnp.zeros((FINE, COARSE), jnp.float32)
    for row in range(COARSE_ROWS):
        pooled = dot(upstream[row * 192 : (row + 1) * 192, :], pooling)
        quarter = [pooled[k * FINE : (k + 1) * FINE] for k in range(4)]
        for half in range(2):
            cell = (quarter[2 * half] + quarter[2 * half + 1])[:, :128].astype(jnp.bfloat16)
            rows = slice((2 * row + half) * MID, (2 * row + half + 1) * MID)
            gate = gate_mid[rows, :]
            mid[rows, :] = keep(gate, dot(lift_mid[...], cell, 0, 0).astype(jnp.bfloat16))
            sum_mid += dot(cell, gate, 1, 1)
        cell = ((quarter[0] + quarter[1]) + (quarter[2] + quarter[3]))[:, 128:].astype(jnp.bfloat16)
        gate = unit_coarse[row]
        coarse[row] = keep(gate, dot(cell, lift_coarse[...], 0, 0).astype(jnp.bfloat16))
        sum_coarse += dot(cell, gate)

    lift[...] = jnp.zeros(lift.shape, lift.dtype)
    lift[0:48, 0:96] = sum_mid.astype(jnp.bfloat16)
    lift[48:96, 0:64] = sum_coarse[:, 128:].astype(jnp.bfloat16)
    lift[96:144, :] = sum_coarse[:, :128].astype(jnp.bfloat16)

    edges = (
        dot(picks((32, 256), ((0, 0), (1, 1), (16, 254), (17, 255))), fine[...], 1, 1)
        + dot(picks((32, 256), ((2, 0), (18, 255))), in_fine[...], 1, 1)
        + dot(picks((32, 128), ((3, 0), (4, 1), (19, 126), (20, 127))), mid[...], 1, 1)
        + dot(picks((32, 128), ((5, 0), (21, 127))), in_mid[...], 1, 1)
    ).astype(jnp.bfloat16)
    masked = coarse[...].reshape(COARSE_ROWS * COARSE_COLS, COARSE)
    inner = inner_coarse[...].reshape(COARSE_ROWS * COARSE_COLS, COARSE)
    sides = []
    for side, cols in ((0, (0, 1, 0)), (1, (62, 63, 63))):
        row, cell = iota((32, 512), 0), iota((32, 512), 1)
        here = cell - (row % 8) * 64
        first = ((row < 8) & (here == cols[0])) | ((row >= 8) & (row < 16) & (here == cols[1]))
        second = (row >= 16) & (row < 24) & (here == cols[2])
        rim = dot(first.astype(jnp.float32).astype(jnp.bfloat16), masked) + dot(
            second.astype(jnp.float32).astype(jnp.bfloat16), inner
        )
        sides.append((edges[side * 16 : (side + 1) * 16], rim.astype(jnp.bfloat16)))
    for out, to_right in ((col_0, parity[1] == 0), (col_1, parity[1] == 1)):
        edge = jnp.where(to_right, sides[1][0], sides[0][0])
        rim = jnp.where(to_right, sides[1][1], sides[0][1])
        for tile in range(12):
            out[tile * 16 : (tile + 1) * 16, :] = edge[:, tile * 128 : (tile + 1) * 128]
        out[192:224, :] = rim[:, :128]
        out[224:256, :] = jnp.zeros((32, 128), jnp.bfloat16)
        out[224:256, 0:64] = rim[:, 128:]

    for out, last in ((row_0, parity[0] == 0), (row_1, parity[0] == 1)):

        def rim_rows(size):
            return pl.ds(pl.multiple_of(jnp.where(last, CELLS - size, 0), 16), size)

        out[0:96, :] = fine[rim_rows(2 * FINE), 0:128]
        out[96:192, :] = fine[rim_rows(2 * FINE), 128:256]
        out[192:240, :] = in_fine[rim_rows(FINE), 0:128]
        out[240:288, :] = in_fine[rim_rows(FINE), 128:256]
        out[288:480, :] = mid[rim_rows(2 * MID), :]
        out[480:576, :] = in_mid[rim_rows(MID), :]
        pair = coarse[pl.ds(jnp.where(last, 6, 0), 2)].reshape(128, COARSE)
        out[576:704, :] = pair[:, :128]
        single = inner_coarse[pl.ds(jnp.where(last, 7, 0), 1)].reshape(64, COARSE)
        out[704:768, :] = single[:, :128]
        out[768:896, :] = jnp.zeros((128, 128), jnp.bfloat16)
        out[768:896, 0:64] = pair[:, 128:]
        out[768:832, 64:128] = single[:, 128:]


IN_SMEM = pl.BlockSpec(memory_space=pltpu.SMEM)
IN_VMEM = pl.BlockSpec(memory_space=pltpu.VMEM)


class Halo:
    def __init__(self, parity, refs):
        row_0, row_1, col_0, col_1, *corner = [ref[...] for ref in refs]
        row_even, col_even = parity[0] == 0, parity[1] == 0
        self.top, self.bottom = jnp.where(row_even, row_1, row_0), jnp.where(row_even, row_0, row_1)
        self.left, self.right = jnp.where(col_even, col_1, col_0), jnp.where(col_even, col_0, col_1)
        left = [jnp.where(col_even, corner[2 * p + 1], corner[2 * p]) for p in range(2)]
        right = [jnp.where(col_even, corner[2 * p], corner[2 * p + 1]) for p in range(2)]
        self.top_left, self.bottom_left = jnp.where(row_even, left[1], left[0]), jnp.where(row_even, left[0], left[1])
        self.top_right, self.bottom_right = jnp.where(row_even, right[1], right[0]), jnp.where(row_even, right[0], right[1])


def prep(*args):
    half = jnp.bfloat16
    shapes = (
        (CELLS, 256), (CELLS, 128), (COARSE_ROWS, COARSE_COLS, COARSE),
        (896, 128), (896, 128), (256, 128), (256, 128), (144, 128),
    )
    return pl.pallas_call(
        prep_kernel,
        out_shape=[jax.ShapeDtypeStruct(shape, half) for shape in shapes],
        in_specs=[IN_SMEM] + [IN_VMEM] * 10,
        scratch_shapes=[pltpu.VMEM((CELLS, width), half) for width in (256, 128, 256, 128)],
        compiler_params=PARAMS,
        name="prep",
    )(*args)


def unit_kernel(
    parity, *refs, chans, rows, width, edge, fill_rows, write_grads,
):
    halo = Halo(parity, refs[:8])
    source, inner, masked, second, px, grads, mx, ix, sx, acc_first, acc_second = refs[8:]
    ring = width + 128
    half = jnp.bfloat16

    mx[2 * chans : 2 * chans + CELLS, 0:width] = masked[...]
    ix[chans : chans + CELLS, 0:width] = jnp.transpose(inner[...], (1, 0, 2)).reshape(CELLS, width)
    sx[...] = jnp.transpose(source[...], (1, 0, 2)).reshape(CELLS, width)
    fill_rows(mx, ix, halo.top, 0, 0)
    fill_rows(mx, ix, halo.bottom, 2 * chans + CELLS, chans + CELLS)
    place = picks(
        (32, 256),
        ((edge, 0), (edge + 1, 1), (16 + edge, 126), (17 + edge, 127), (edge + 2, 128), (18 + edge, 255)),
    )

    def columns(right, left, tile):
        rows16 = slice(tile * 16, (tile + 1) * 16)
        both = jnp.concatenate([right[rows16, :], left[rows16, :]], axis=0)
        return dot(both, place, 0, 0).astype(half)

    for tile in range(12):
        cols = columns(halo.right, halo.left, tile)
        mx[2 * chans + tile * 128 : 2 * chans + (tile + 1) * 128, width:ring] = cols[:, :128]
        ix[chans + tile * 128 : chans + (tile + 1) * 128, width:ring] = cols[:, 128:]
    for tile in range((CELLS - 2 * chans) // 128, 12):
        cols = columns(halo.top_right, halo.top_left, tile)
        skip = max(0, CELLS - 2 * chans - tile * 128)
        at = tile * 128 + skip - (CELLS - 2 * chans)
        mx[at : at + 128 - skip, width:ring] = cols[skip:, :128]
        if tile == 11:
            ix[0:chans, width:ring] = cols[128 - chans :, 128:]
    for tile in range(-(-2 * chans // 128)):
        cols = columns(halo.bottom_right, halo.bottom_left, tile)
        size = min(128, 2 * chans - tile * 128)
        at = 2 * chans + CELLS + tile * 128
        mx[at : at + size, width:ring] = cols[:size, :128]
        if tile == 0:
            ix[chans + CELLS :, width:ring] = cols[:chans, 128:]

    def before(row, carry):
        at = pl.multiple_of(row * chans, 16)
        inner_grad = ring_taps(second[...], mx[pl.ds(at, 3 * chans), :], chans, ring)
        px[pl.ds(at, chans), :] = keep(ix[pl.ds(at, chans), :].astype(jnp.float32), inner_grad).astype(half)
        return carry

    lax.fori_loop(0, rows + 2, before, 0, unroll=2)

    def spread(tile):
        wide = jnp.concatenate([tile.astype(jnp.float32), jnp.zeros((chans, 128), jnp.float32)], axis=1)
        return jnp.concatenate([pltpu.roll(wide, 1, 1), wide, pltpu.roll(wide, ring - 1, 1)], axis=0).astype(half)

    acc_first[...] = jnp.zeros(acc_first.shape, jnp.float32)
    acc_second[...] = jnp.zeros(acc_second.shape, jnp.float32)

    def after(row, carry):
        at = pl.multiple_of(row * chans, 16)
        window = px[pl.ds(at, 3 * chans), :]
        acc_first[...] += dot(spread(sx[pl.ds(at, chans), :]), window, 1, 1)
        own = ix[pl.ds(pl.multiple_of(at + chans, 16), chans), 0:width]
        acc_second[...] += dot(spread(own), mx[pl.ds(pl.multiple_of(at + chans, 16), 3 * chans), :], 1, 1)
        return carry

    lax.fori_loop(0, rows, after, 0, unroll=2)
    write_grads(grads, acc_first, acc_second)


def ring_taps(weight, window, chans, ring):
    parts = dot(weight, window)
    return pltpu.roll(parts[:chans], ring - 1, 1) + parts[chans : 2 * chans] + pltpu.roll(parts[2 * chans :], 1, 1)


def input_kernel(masked, px, first, out, ox, *, chans, rows, width):
    def step(row, carry):
        at = pl.multiple_of(row * chans, 16)
        grad = ring_taps(first[...], px[pl.ds(at, 3 * chans), :], chans, width + 128)[:, :width]
        ox[pl.ds(row, 1), :, :] = (masked[pl.ds(at, chans), :].astype(jnp.float32) + grad).astype(jnp.bfloat16)[None]
        return carry

    lax.fori_loop(0, rows, step, 0, unroll=2)
    out[...] = jnp.transpose(ox[...], (1, 0, 2))


def fine_rows(mx, ix, halo, at, inner_at):
    mx[at : at + 96, 0:128] = halo[0:96, :]
    mx[at : at + 96, 128:256] = halo[96:192, :]
    ix[inner_at : inner_at + 48, 0:128] = halo[192:240, :]
    ix[inner_at : inner_at + 48, 128:256] = halo[240:288, :]


def mid_rows(mx, ix, halo, at, inner_at):
    mx[at : at + 192, 0:128] = halo[288:480, :]
    ix[inner_at : inner_at + 96, 0:128] = halo[480:576, :]


def fine_grads(grads, acc_first, acc_second):
    for tap in range(3):
        cols = slice((2 - tap) * FINE, (3 - tap) * FINE)
        pair = jnp.concatenate([acc_second[:, cols], acc_first[:, cols], jnp.zeros((144, 32), jnp.float32)], axis=1)
        grads[tap * 144 : (tap + 1) * 144, :] = pair.astype(jnp.bfloat16)


def mid_grads(grads, acc_first, acc_second):
    for index, acc in enumerate((acc_second, acc_first)):
        for tap in range(3):
            part = jnp.concatenate(
                [acc[:, (2 - tap) * MID : (3 - tap) * MID], jnp.zeros((288, 32), jnp.float32)], axis=1
            )
            at = (3 * index + tap) * 288
            grads[at : at + 288, :] = part.astype(jnp.bfloat16)


def channel_grads(parity, halo, source, inner, masked, second, chans, rows, width, edge, fill_rows, grad_rows, write_grads, name):
    half = jnp.bfloat16
    ring = width + 128

    def kernel(*refs):
        unit_kernel(
            *refs, chans=chans, rows=rows, width=width, edge=edge, fill_rows=fill_rows, write_grads=write_grads
        )

    return pl.pallas_call(
        kernel,
        out_shape=[
            jax.ShapeDtypeStruct(((rows + 2) * chans, ring), half),
            jax.ShapeDtypeStruct((grad_rows, 128), half),
        ],
        in_specs=[IN_SMEM] + [IN_VMEM] * 12,
        scratch_shapes=[
            pltpu.VMEM(((rows + 4) * chans, ring), half),
            pltpu.VMEM(((rows + 2) * chans, ring), half),
            pltpu.VMEM((CELLS, width), half),
            pltpu.VMEM((3 * chans, 3 * chans), jnp.float32),
            pltpu.VMEM((3 * chans, 3 * chans), jnp.float32),
        ],
        compiler_params=PARAMS,
        name=name,
    )(parity, *halo, source, inner, masked, stacked(second, chans))


def stacked(weight, chans):
    return jnp.transpose(weight[::-1], (1, 2, 0, 3)).reshape(3 * chans, 3 * chans)


def channel_input(masked, px, first, chans, rows, width, name):
    def kernel(*refs):
        input_kernel(*refs, chans=chans, rows=rows, width=width)

    return pl.pallas_call(
        kernel,
        out_shape=jax.ShapeDtypeStruct((chans, rows, width), jnp.bfloat16),
        scratch_shapes=[pltpu.VMEM((rows, chans, width), jnp.bfloat16)],
        compiler_params=PARAMS,
        name=name,
    )(masked, px, stacked(first, chans))


def coarse_places():
    place = np.zeros((2, 13 * 16, 6 * 32), np.float32)
    for index, first_row, count, sides in ((0, -2, 12, ((0, 0, "r"), (1, 1, "r"), (14, 0, "l"), (15, 1, "l"))), (1, -1, 10, ((0, 2, "r"), (15, 2, "l")))):
        for block in range(count + 1):
            for at, which, side in sides:
                row = first_row + block - (1 if side == "r" else 0)
                if row < first_row or row >= first_row + count:
                    continue
                message = 0 if 0 <= row < 8 else 1 if row < 0 else 2
                source = 2 * message + (0 if side == "r" else 1)
                place[index, block * 16 + at, source * 32 + which * 8 + row % 8] = 1
    return place.reshape(2 * 13 * 16, 6 * 32)


def coarse_taps(ref, weight, start, size):
    total = jnp.zeros((size, COARSE), jnp.float32)
    for row_tap in range(3):
        for col_tap in range(3):
            at = start + (2 - row_tap) * PITCH
            total += dot(ref[col_tap, at : at + size, :], weight[row_tap, col_tap], 1, 1)
    return total


def coarse_kernel(parity, *refs):
    halo = Halo(parity, refs[:8])
    source, inner, masked, second, place, px, grads, mx, ix, own, turned, tail = refs[8:]
    half = jnp.bfloat16
    lead = 16
    rims = jnp.concatenate(
        [
            jnp.concatenate([ref[192:224, :], ref[224:256, 0:64]], axis=1)
            for ref in (halo.right, halo.left, halo.top_right, halo.top_left, halo.bottom_right, halo.bottom_left)
        ],
        axis=0,
    )
    rims = dot(place[...], rims).astype(half)

    def rows_of(rim):
        pair = jnp.concatenate([rim[576:704, :], rim[768:896, 0:64]], axis=1)
        single = jnp.concatenate([rim[704:768, :], rim[768:832, 64:128]], axis=1)
        return pair, single

    above, above_inner = rows_of(halo.top)
    below, below_inner = rows_of(halo.bottom)
    grid = [above[:64], above[64:]] + [masked[k] for k in range(8)] + [below[:64], below[64:]]
    inner_grid = [above_inner] + [inner[k] for k in range(8)] + [below_inner]
    for ref, blocks, at in ((mx.at[1], grid, 0), (ix, inner_grid, 208)):
        ref[0:lead, :] = rims[at : at + 16]
        for k, block in enumerate(blocks):
            start = lead + k * PITCH
            ref[start : start + 64, :] = block
            ref[start + 64 : start + PITCH, :] = rims[at + (k + 1) * 16 : at + (k + 2) * 16]

    def shifted(ref, size):
        whole = ref[1].astype(jnp.float32)
        ref[0] = pltpu.roll(whole, size - 1, 0).astype(half)
        ref[2] = pltpu.roll(whole, 1, 0).astype(half)

    shifted(mx, 976)
    for start in range(0, 816, 272):
        inner_grad = coarse_taps(mx, second, start, 272)
        px[1, start : start + 272, :] = keep(
            ix[start : start + 272, :].astype(jnp.float32), inner_grad
        ).astype(half)
    shifted(px, 816)
    def corr(tile, ref, start, write):
        own[...] = jnp.zeros(own.shape, half)
        for row in range(8):
            own[row * PITCH : row * PITCH + 64, :] = tile[row]
        turned[...] = jnp.transpose(own[...].astype(jnp.float32)).astype(half)
        for row_tap in range(3):
            for col_tap in range(3):
                at = start + (2 - row_tap) * PITCH
                write(row_tap * 3 + col_tap, dot(turned[...], ref[col_tap, at : at + 8 * PITCH, :]))

    def write_second(tap, value):
        grads[tap * COARSE : (tap + 1) * COARSE, :] = value[:, :128].astype(half)
        tail[tap * COARSE : (tap + 1) * COARSE, :] = value[:, 128:].astype(half)

    def write_first(tap, value):
        at = 1728 + tap * COARSE
        grads[at : at + COARSE, :] = value[:, :128].astype(half)
        rows = slice(3456 + tap * COARSE, 3456 + (tap + 1) * COARSE)
        grads[rows, :] = jnp.concatenate(
            [tail[tap * COARSE : (tap + 1) * COARSE, :], value[:, 128:].astype(half)], axis=1
        )

    corr(inner, mx, lead + PITCH, write_second)
    corr(source, px, lead, write_first)


def coarse_grads(parity, halo, source, inner, masked, second):
    half = jnp.bfloat16
    return pl.pallas_call(
        coarse_kernel,
        out_shape=[
            jax.ShapeDtypeStruct((3, 816, COARSE), half),
            jax.ShapeDtypeStruct((5184, 128), half),
        ],
        in_specs=[IN_SMEM] + [IN_VMEM] * 13,
        scratch_shapes=[
            pltpu.VMEM((3, 976, COARSE), half),
            pltpu.VMEM((816, COARSE), half),
            pltpu.VMEM((8 * PITCH, COARSE), half),
            pltpu.VMEM((COARSE, 8 * PITCH), half),
            pltpu.VMEM((1728, 64), half),
        ],
        compiler_params=PARAMS,
        name="coarse_grads",
    )(parity, *halo, source, inner, masked, second, jnp.asarray(coarse_places(), half))


def coarse_input_kernel(masked, px, first, out):
    for row in range(8):
        grad = coarse_taps(px, first, 16 + row * PITCH, 64)
        out[row] = (masked[row].astype(jnp.float32) + grad).astype(jnp.bfloat16)


def coarse_input(masked, px, first):
    return pl.pallas_call(
        coarse_input_kernel,
        out_shape=jax.ShapeDtypeStruct((COARSE_ROWS, COARSE_COLS, COARSE), jnp.bfloat16),
        compiler_params=PARAMS,
        name="coarse_input",
    )(masked, px, first)


AT_MID, AT_FINE, AT_LIFT, SUM_ROWS = 5184, 6912, 7344, 7680


def unpack_kernel(summed, first_fine, second_fine, first_mid, second_mid, first_coarse, second_coarse, lift_mid, lift_coarse):
    def part(start, size, lanes=slice(0, 128)):
        return summed[start : start + size, lanes].astype(jnp.float32)

    for tap in range(9):
        row_tap, col_tap = tap // 3, tap % 3
        tails = part(3456 + tap * COARSE, COARSE)
        second_coarse[row_tap, col_tap, :, 0:128] = part(tap * COARSE, COARSE)
        second_coarse[row_tap, col_tap, :, 128:192] = tails[:, :64]
        first_coarse[row_tap, col_tap, :, 0:128] = part(1728 + tap * COARSE, COARSE)
        first_coarse[row_tap, col_tap, :, 128:192] = tails[:, 64:]
        pair = part(AT_FINE + tap * FINE, FINE)
        second_fine[row_tap, col_tap] = pair[:, 0:48]
        first_fine[row_tap, col_tap] = pair[:, 48:96]
        second_mid[row_tap, col_tap] = part(AT_MID + tap * MID, MID, slice(0, 96))
        first_mid[row_tap, col_tap] = part(AT_MID + 864 + tap * MID, MID, slice(0, 96))
    lift_mid[...] = part(AT_LIFT, 48, slice(0, 96))
    lift_coarse[:, 0:128] = part(AT_LIFT + 96, 48)
    lift_coarse[:, 128:192] = part(AT_LIFT + 48, 48, slice(0, 64))


def unpack(summed):
    shapes = ((3, 3, 48, 48),) * 2 + ((3, 3, 96, 96),) * 2 + ((3, 3, 192, 192),) * 2 + ((48, 96), (48, 192))
    *taps, lift_mid, lift_coarse = pl.pallas_call(
        unpack_kernel,
        out_shape=[jax.ShapeDtypeStruct(shape, jnp.float32) for shape in shapes],
        compiler_params=PARAMS,
        name="unpack",
    )(summed)
    return *taps, jnp.transpose(lift_mid), jnp.transpose(lift_coarse)


def on_device(
    grad_joined, joined_fine, input_fine, inner_fine, unit_fine, input_mid, inner_mid, unit_mid,
    input_coarse, inner_coarse, unit_coarse, first_fine, second_fine, first_mid, second_mid,
    first_coarse, second_coarse, lift_mid, lift_coarse,
):
    input_coarse, inner_coarse, unit_coarse = (
        jnp.transpose(x, (1, 2, 0)) for x in (input_coarse, inner_coarse, unit_coarse)
    )
    parity = jnp.stack([lax.axis_index("row") % 2, lax.axis_index("col") % 2]).astype(jnp.int32)
    fine, mid, coarse, row_0, row_1, col_0, col_1, lift = prep(
        parity, grad_joined, joined_fine, unit_fine, inner_fine, unit_mid, inner_mid, unit_coarse, inner_coarse,
        jnp.transpose(lift_mid), jnp.transpose(lift_coarse),
    )
    halo = (
        send(row_0, swap_pairs(0, None)),
        send(row_1, swap_pairs(1, None)),
        send(col_0, swap_pairs(None, 0)),
        send(col_1, swap_pairs(None, 1)),
        send(col_0, swap_pairs(0, 0)),
        send(col_1, swap_pairs(0, 1)),
        send(col_0, swap_pairs(1, 0)),
        send(col_1, swap_pairs(1, 1)),
    )
    coarse_px, coarse_part = coarse_grads(parity, halo, input_coarse, inner_coarse, coarse, second_coarse)
    mid_px, mid_part = channel_grads(
        parity, halo, input_mid, inner_mid, mid, second_mid, MID, 16, 128, 3, mid_rows, 1728, mid_grads, "mid_grads"
    )
    fine_px, fine_part = channel_grads(
        parity, halo, input_fine, inner_fine, fine, second_fine, FINE, 32, 256, 0, fine_rows, 432, fine_grads, "fine_grads"
    )
    unused = jnp.zeros((SUM_ROWS - AT_LIFT - 144, 128), jnp.bfloat16)
    summed, fine_input, mid_input, input_grad = all_sum(
        jnp.concatenate([coarse_part, mid_part, fine_part, lift, unused]),
        (
            (lambda px: channel_input(fine, px, first_fine, FINE, 32, 256, "fine_input"), fine_px),
            (lambda px: channel_input(mid, px, first_mid, MID, 16, 128, "mid_input"), mid_px),
            (lambda px: coarse_input(coarse, px, first_coarse), coarse_px),
        ),
    )
    return (fine_input, mid_input, jnp.transpose(input_grad, (2, 0, 1)), *unpack(summed))


def solution(mesh):
    tiled = P(None, "row", "col")
    return jax.shard_map(
        on_device,
        mesh=mesh,
        in_specs=(tiled,) * 11 + (P(),) * 8,
        out_specs=(tiled,) * 3 + (P(),) * 8,
        check_vma=False,
    )
```

time: 168 us -> 136 us (0.81)
  starting transfers between devices: 75.3 us -> 46.7 us
  Pallas kernels: 46.3 us -> 59.9 us
  waiting for transfers between devices: 28.3 us -> 15.3 us
  local copies, waits for them, and re-layouts: 12.1 us -> 8.46 us
    ppermute x42 -> x25, starting transfers between devices: 75.3 us -> 46.7 us  [send(): return lax.ppermute(block, AXES, pairs)]
    pallas_call x3 -> x6, Pallas kernels: 36.3 us -> 49.5 us  [the longest x2 26.1 us: channel_grads(): pl.pallas_call(kernel, out_shape=[jax.ShapeDtypeStruct(((rows + 2) * chan...]
    ppermute x42 -> x25, waiting for transfers between devices: 28.3 us -> 15.3 us  [send(): return lax.ppermute(block, AXES, pairs)]
    unnamed x36 -> x30, local copies, waits for them, and re-layouts: 6.74 us -> 4.17 us
  transfers between devices with their start and end apart: 42 -> 25, of which waited for: 19 -> 9; matrix products, arithmetic and copies ran while one was open for 4% -> 3% of each run, Pallas kernels for 5% -> 13%
where the time goes in v1:
time: 136 us; the launch traced here: 135 us
  Pallas kernels  59.9 us (44%)
  starting transfers between devices  46.7 us (34%)
  waiting for transfers between devices  15.3 us (11%)
  local copies, waits for them, and re-layouts  8.46 us (6%)
  other arithmetic  4.09 us (3%)
    ppermute x25, starting transfers between devices, send(): return lax.ppermute(block, AXES, pairs)  46.7 us
    pallas_call x2, Pallas kernels, channel_grads(): pl.pallas_call(kernel, out_shape=[jax.ShapeDtypeStruct(((rows + 2) * chan...  26.1 us
    ppermute x25, waiting for transfers between devices, send(): return lax.ppermute(block, AXES, pairs)  15.3 us
    pallas_call x2, Pallas kernels, channel_input(): pl.pallas_call(kernel, out_shape=jax.ShapeDtypeStruct((chans, rows, width...  13 us
    pallas_call x1, Pallas kernels, prep(): pl.pallas_call(prep_kernel, out_shape=[jax.ShapeDtypeStruct(shape, half)...  6.46 us
    pallas_call x1, Pallas kernels, coarse_grads(): pl.pallas_call(coarse_kernel, out_shape=[jax.ShapeDtypeStruct((3, 816, CO...  5.71 us
    pallas_call x1, Pallas kernels, coarse_input(): pl.pallas_call(coarse_input_kernel, out_shape=jax.ShapeDtypeStruct((COARS...  4.67 us
    unnamed x30, local copies, waits for them, and re-layouts  4.17 us
  transfers between devices with their start and end apart: 25, of which 9 were waited for; matrix products, arithmetic and copies ran while one was open for 3% of the time, Pallas kernels for 13%

profile of v1, /device:TPU:1, one launch (start us, length us, event | category | flops | bytes accessed | tf_op | source)
XLA Modules:
  0.0 135.5 jit_solution(3126333938210586866)
XLA Ops:
  0.7 0.6 pad_add_fusion.parity.refs_0_
  1.3 6.5 %prep.1 = (bf16[1536,256]{1,0:T(8,128)(2,1)}, bf16[1536,128]{1,0:T(8,128)(2,1)}, bf16[8,64,192]{2,1,0:T(8,128)(2,1)}, bf16[896,128]{1,0:T(8,128)(2,1)}, bf16[896...) custom-call(s32[2]{0:T(128)} %pad_add_fusion.parity.refs_0_, ...), custom_call_target="tpu_custom_call" | custom-call | tf_op jit(solution)/shard_map/prep/pallas_call | solution.py:234
  7.7 2.2 %collective-permute-start.2 = (bf16[256,128]{1,0:T(8,128)(2,1)}, bf16[256,128]{1,0:T(8,128)(2,1)S(1)}, u32[]{:S(2)}, u32[]{:S(2)}) collective-permute-start(bf16[256,128]{1,0:T(8,128)(2,1)} %get-tuple-element.47), channel_id=1, source_target_pairs={{0,1},{1,0},{2,3},{3,2},{4,5},{5,4},{6,7},{7,6},{8,9},{9,8},{10,11... | collective-permute-start | bytes 196616 | tf_op jit(solution)/shard_map/ppermute | solution.py:40
  9.9 0.9 collective-permute-start.4
  10.9 4.0 %collective-permute-start.1 = (bf16[896,128]{1,0:T(8,128)(2,1)}, bf16[896,128]{1,0:T(8,128)(2,1)S(1)}, u32[]{:S(2)}, u32[]{:S(2)}) collective-permute-start(bf16[896,128]{1,0:T(8,128)(2,1)} %get-tuple-element.46), channel_id=1, source_target_pairs={{4,8},{5,9},{6,10},{7,11},{8,4},{9,5},{10,6},{11,7},{12,16},{13,17... | collective-permute-start | bytes 688136 | tf_op jit(solution)/shard_map/ppermute | solution.py:40
  14.8 0.7 collective-permute-start.3
  15.7 0.9 reshape.55.refs_12_
  16.6 0.7 collective-permute-start.5
  17.3 8.8 %collective-permute-start.6 = (bf16[256,128]{1,0:T(8,128)(2,1)}, bf16[256,128]{1,0:T(8,128)(2,1)S(1)}, u32[]{:S(2)}, u32[]{:S(2)}) collective-permute-start(bf16[256,128]{1,0:T(8,128)(2,1)} %get-tuple-element.47), channel_id=1, source_target_pairs={{4,9},{5,8},{6,11},{7,10},{8,5},{9,4},{10,7},{11,6},{12,17},{13,16... | collective-permute-start | bytes 196616 | tf_op jit(solution)/shard_map/ppermute | solution.py:40
  26.1 0.7 collective-permute-start.7
  26.9 0.8 reshape.56.refs_12_
  27.6 0.6 collective-permute-done.6.refs_6_.refs_7_
  28.3 0.5 copy-done.6
  29.0 5.7 %coarse_grads.1 = (bf16[3,816,192]{2,1,0:T(8,128)(2,1)}, bf16[5184,128]{1,0:T(8,128)(2,1)}) custom-call(s32[2]{0:T(128)} %pad_add_fusion.parity.refs_0_, bf16[896,128]{1,0:T(8,128)(2,1)} %copy-done, bf16[896,128]{1,0:T(8,128)(2,1)} %copy-done.1, bf16[256,128]{1,0:T(8,128)(2,1)} %copy-done.2, bf16[256,128]{1,0:T(8,128)(2,1)} %copy-done.4, ...), custom_call_target="tpu_custom_call" | custom-call | tf_op jit(solution)/shard_map/coarse_grads/pallas_call | solution.py:496
  34.7 1.4 %constant_dynamic-update-slice_fusion.3 = bf16[7680,128]{1,0:T(8,128)(2,1)S(1)} fusion(bf16[5184,128]{1,0:T(8,128)(2,1)} %get-tuple-element.50), kind=kLoop, calls=%fused_computation.33 | loop fusion | bytes 2654208
  36.2 11.4 %mid_grads.1 = (bf16[1728,256]{1,0:T(8,128)(2,1)}, bf16[1728,128]{1,0:T(8,128)(2,1)}) custom-call(s32[2]{0:T(128)} %pad_add_fusion.parity.refs_0_, bf16[896,128]{1,0:T(8,128)(2,1)} %copy-done, bf16[896,128]{1,0:T(8,128)(2,1)} %copy-done.1, bf16[256,128]{1,0:T(8,128)(2,1)} %copy-done.2, bf16[256,128]{1,0:T(8,128)(2,1)} %copy-done.4, ...), custom_call_target="tpu_custom_call" | custom-call | tf_op jit(solution)/shard_map/mid_grads/pallas_call | solution.py:367
  47.5 1.1 constant_dynamic-update-slice_fusion.2
  48.6 14.7 %fine_grads.1 = (bf16[1632,384]{1,0:T(8,128)(2,1)}, bf16[432,128]{1,0:T(8,128)(2,1)}) custom-call(s32[2]{0:T(128)} %pad_add_fusion.parity.refs_0_, bf16[896,128]{1,0:T(8,128)(2,1)} %copy-done, bf16[896,128]{1,0:T(8,128)(2,1)} %copy-done.1, bf16[256,128]{1,0:T(8,128)(2,1)} %copy-done.2, bf16[256,128]{1,0:T(8,128)(2,1)} %copy-done.4, ...), custom_call_target="tpu_custom_call" | custom-call | tf_op jit(solution)/shard_map/fine_grads/pallas_call | solution.py:367
  63.3 0.9 constant_dynamic-update-slice_fusion.1
  64.5 2.6 %collective-permute-done.8 = bf16[3840,128]{1,0:T(8,128)(2,1)} collective-permute-done((bf16[3840,128]{1,0:T(8,128)(2,1)S(1)}, bf16[3840,128]{1,0:T(8,128)(2,1)}, u32[]{:S(2)}, u32[]{:S(2)}) %collective-permute-start.8) | collective-permute-done | bytes 983072 | tf_op jit(solution)/shard_map/ppermute | solution.py:40
  67.2 1.5 %fusion = bf16[3840,128]{1,0:T(8,128)(2,1)S(1)} fusion(bf16[3840,128]{1,0:T(8,128)(2,1)} %collective-permute-done.8, bf16[2,3840,128]{2,1,0:T(8,128)(2,1)S(1)} %bitcast.63, s32[]{:T(128)S(6)} %select_n.83), kind=kLoop, calls=%fused_computation.2 | loop fusion | flops 1966080 | bytes 2949124 | tf_op jit(solution)/shard_map/convert_element_type | solution.py:81
  68.7 3.4 %collective-permute-start.11 = (bf16[960,128]{1,0:T(8,128)(2,1)S(1)}, bf16[960,128]{1,0:T(8,128)(2,1)S(1)}, u32[]{:S(2)}, u32[]{:S(2)}) collective-permute-start(bf16[960,128]{1,0:T(8,128)(2,1)S(1)} %get-tuple-element.80), channel_id=1, source_target_pairs={{0,3},{1,2},{2,1},{3,0},{4,100},{5,101},{6,102},{7,103},{8,11},{9,... | collective-permute-start | bytes 737288 | tf_op jit(solution)/shard_map/ppermute | solution.py:40
  72.1 0.2 collective-permute-start.10
  72.3 0.5 collective-permute-start.9
  72.9 0.8 reshape.59.refs_2_
  73.6 7.6 %fine_input.1 = bf16[48,32,256]{2,1,0:T(8,128)(2,1)} custom-call(bf16[1536,256]{1,0:T(8,128)(2,1)} %get-tuple-element.53.refs_11_.refs_0_, bf16[1632,384]{1,0:T(8,128)(2,1)} %get-tuple-element.58.refs_1_, bf16[144,144]{1,0:T(8,128)(2,1)} %reshape.59.refs_2_), custom_call_target="tpu_custom_call" | custom-call | tf_op jit(solution)/shard_map/fine_input/pallas_call | solution.py:394
  81.4 3.1 %collective-permute-start.14 = (bf16[240,128]{1,0:T(8,128)(2,1)S(1)}, bf16[240,128]{1,0:T(8,128)(2,1)S(1)}, u32[]{:S(2)}, u32[]{:S(2)}) collective-permute-start(bf16[240,128]{1,0:T(8,128)(2,1)S(1)} %get-tuple-element.83), channel_id=1, source_target_pairs={{0,96},{1,97},{2,98},{3,99},{4,28},{5,29},{6,30},{7,31},{8,104},{9... | collective-permute-start | bytes 184328 | tf_op jit(solution)/shard_map/ppermute | solution.py:40
  84.5 0.6 collective-permute-start.12
  85.1 0.9 collective-permute-done.14
  86.1 3.0 %collective-permute-done.13 = bf16[240,128]{1,0:T(8,128)(2,1)S(1)} collective-permute-done((bf16[240,128]{1,0:T(8,128)(2,1)S(1)}, bf16[240,128]{1,0:T(8,128)(2,1)S(1)}, u32[]{:S(2)}, u32[]{:S(2)}) %collective-permute-start.13) | collective-permute-done | bytes 61472 | tf_op jit(solution)/shard_map/ppermute | solution.py:40
  89.1 1.8 %collective-permute-start.17 = (bf16[240,128]{1,0:T(8,128)(2,1)S(1)}, bf16[240,128]{1,0:T(8,128)(2,1)S(1)}, u32[]{:S(2)}, u32[]{:S(2)}) collective-permute-start(bf16[240,128]{1,0:T(8,128)(2,1)S(1)} %fusion.4), channel_id=1, source_target_pairs={{0,24},{1,25},{2,26},{3,27},{4,7},{5,6},{6,5},{7,4},{8,16},{9,17},... | collective-permute-start | bytes 184328 | tf_op jit(solution)/shard_map/ppermute | solution.py:40
  90.9 4.5 %collective-permute-start.16 = (bf16[240,128]{1,0:T(8,128)(2,1)S(1)}, bf16[240,128]{1,0:T(8,128)(2,1)S(1)}, u32[]{:S(2)}, u32[]{:S(2)}) collective-permute-start(bf16[240,128]{1,0:T(8,128)(2,1)S(1)} %fusion.4), channel_id=1, source_target_pairs={{0,16},{1,17},{2,18},{3,19},{4,6},{5,7},{6,4},{7,5},{8,24},{9,25},... | collective-permute-start | bytes 184328 | tf_op jit(solution)/shard_map/ppermute | solution.py:40
  95.7 0.9 reshape.62.refs_2_
  96.5 0.5 collective-permute-done.16
  97.1 1.5 %collective-permute-done.15 = bf16[240,128]{1,0:T(8,128)(2,1)S(1)} collective-permute-done((bf16[240,128]{1,0:T(8,128)(2,1)S(1)}, bf16[240,128]{1,0:T(8,128)(2,1)S(1)}, u32[]{:S(2)}, u32[]{:S(2)}) %collective-permute-start.15) | collective-permute-done | bytes 61472 | tf_op jit(solution)/shard_map/ppermute | solution.py:40
  98.6 0.9 collective-permute-start.18
  99.5 2.2 %collective-permute-start.19 = (bf16[240,128]{1,0:T(8,128)(2,1)S(1)}, bf16[240,128]{1,0:T(8,128)(2,1)S(1)}, u32[]{:S(2)}, u32[]{:S(2)}) collective-permute-start(bf16[240,128]{1,0:T(8,128)(2,1)S(1)} %add_convert_fusion), channel_id=1, source_target_pairs={{0,64},{1,65},{2,66},{3,67},{4,20},{5,21},{6,22},{7,23},{8,72},{9,... | collective-permute-start | bytes 184328 | tf_op jit(solution)/shard_map/ppermute | solution.py:40
  101.7 0.8 collective-permute-start.20
  102.6 5.5 %mid_input.1 = bf16[96,16,128]{2,1,0:T(8,128)(2,1)} custom-call(bf16[1536,128]{1,0:T(8,128)(2,1)} %get-tuple-element.51.refs_11_.refs_0_, bf16[1728,256]{1,0:T(8,128)(2,1)} %get-tuple-element.63.refs_1_, bf16[288,288]{1,0:T(8,128)(2,1)} %reshape.62.refs_2_), custom_call_target="tpu_custom_call" | custom-call | tf_op jit(solution)/shard_map/mid_input/pallas_call | solution.py:394
  108.1 0.8 collective-permute-start.21
  108.9 3.3 %collective-permute-start.22 = (bf16[960,128]{1,0:T(8,128)(2,1)S(1)}, bf16[960,128]{1,0:T(8,128)(2,1)S(1)}, u32[]{:S(2)}, u32[]{:S(2)}) collective-permute-start(bf16[960,128]{1,0:T(8,128)(2,1)S(1)} %bitcast.73), channel_id=1, source_target_pairs={{0,2},{1,3},{2,0},{3,1},{4,68},{5,69},{6,70},{7,71},{8,10},{9,11},... | collective-permute-start | bytes 737288 | tf_op jit(solution)/shard_map/ppermute | solution.py:40
  112.5 4.7 %coarse_input.1 = bf16[8,64,192]{2,1,0:T(8,128)(2,1)} custom-call(bf16[8,64,192]{2,1,0:T(8,128)(2,1)} %get-tuple-element.49.refs_10_.masked, bf16[3,816,192]{2,1,0:T(8,128)(2,1)} %get-tuple-element.68.px, bf16[3,3,192,192]{3,2,1,0:T(8,128)(2,1)} %first.1), custom_call_target="tpu_custom_call" | custom-call | tf_op jit(solution)/shard_map/coarse_input/pallas_call | solution.py:522
  117.2 1.4 %collective-permute-done.22 = bf16[960,128]{1,0:T(8,128)(2,1)S(1)} collective-permute-done((bf16[960,128]{1,0:T(8,128)(2,1)S(1)}, bf16[960,128]{1,0:T(8,128)(2,1)S(1)}, u32[]{:S(2)}, u32[]{:S(2)}) %collective-permute-start.22) | collective-permute-done | bytes 245792 | tf_op jit(solution)/shard_map/ppermute | solution.py:40
  118.6 2.5 %collective-permute-done.23 = bf16[960,128]{1,0:T(8,128)(2,1)S(1)} collective-permute-done((bf16[960,128]{1,0:T(8,128)(2,1)S(1)}, bf16[960,128]{1,0:T(8,128)(2,1)S(1)}, u32[]{:S(2)}, u32[]{:S(2)}) %collective-permute-start.23) | collective-permute-done | bytes 245792 | tf_op jit(solution)/shard_map/ppermute | solution.py:40
  121.2 6.4 %collective-permute-start.24 = (bf16[3840,128]{1,0:T(8,128)(2,1)S(1)}, bf16[3840,128]{1,0:T(8,128)(2,1)S(1)}, u32[]{:S(2)}, u32[]{:S(2)}) collective-permute-start(bf16[3840,128]{1,0:T(8,128)(2,1)S(1)} %bitcast.66), channel_id=1, source_target_pairs={{0,4},{1,5},{2,6},{3,7},{4,0},{5,1},{6,2},{7,3},{8,12},{9,13},{10,... | collective-permute-start | bytes 2949128 | tf_op jit(solution)/shard_map/ppermute | solution.py:40
  127.6 2.2 %collective-permute-done.24 = bf16[3840,128]{1,0:T(8,128)(2,1)S(1)} collective-permute-done((bf16[3840,128]{1,0:T(8,128)(2,1)S(1)}, bf16[3840,128]{1,0:T(8,128)(2,1)S(1)}, u32[]{:S(2)}, u32[]{:S(2)}) %collective-permute-start.24) | collective-permute-done | bytes 983072 | tf_op jit(solution)/shard_map/ppermute | solution.py:40
  129.7 1.8 %maximum_select_fusion.summed = bf16[7680,128]{1,0:T(8,128)(2,1)} fusion(bf16[3840,128]{1,0:T(8,128)(2,1)S(1)} %collective-permute-done.24, bf16[3840,128]{1,0:T(8,128)(2,1)S(1)} %bitcast.67, pred[]{:T(512)S(6)} %eq.10), kind=kLoop, calls=%fused_computation | loop fusion | flops 8847360 | bytes 3932161 | tf_op jit(solution)/shard_map/jit(_where)/select_n | solution.py:88
  131.6 3.9 %unpack.1 = (f32[3,3,48,48]{3,2,1,0:T(8,128)}, f32[3,3,48,48]{3,2,1,0:T(8,128)}, f32[3,3,96,96]{3,2,1,0:T(8,128)}, f32[3,3,96,96]{3,2,1,0:T(8,128)}, f32[3,3,192...) custom-call(bf16[7680,128]{1,0:T(8,128)(2,1)} %maximum_select_fusion.summed), custom_call_target="tpu_custom_call" | custom-call | tf_op jit(solution)/shard_map/unpack/pallas_call | solution.py:556
  (72 shorter events, 1.7 us)
Async XLA Ops:
  1.2 14.3 %copy-start.8 = (bf16[3,3,96,96]{3,2,1,0:T(8,128)(2,1)S(1)}, bf16[3,3,96,96]{3,2,1,0:T(8,128)(2,1)}, u32[]{:S(2)}) copy-start(bf16[3,3,96,96]{3,2,1,0:T(8,128)(2,1)} %param.34) | copy-start | bytes 497668
  1.3 25.5 %copy-start.10 = (bf16[3,3,48,48]{3,2,1,0:T(8,128)(2,1)S(1)}, bf16[3,3,48,48]{3,2,1,0:T(8,128)(2,1)}, u32[]{:S(2)}) copy-start(bf16[3,3,48,48]{3,2,1,0:T(8,128)(2,1)} %param.32) | copy-start | bytes 124420
  7.7 8.9 %collective-permute-start.2 = (bf16[256,128]{1,0:T(8,128)(2,1)}, bf16[256,128]{1,0:T(8,128)(2,1)S(1)}, u32[]{:S(2)}, u32[]{:S(2)}) collective-permute-start(bf16[256,128]{1,0:T(8,128)(2,1)} %get-tuple-element.47), channel_id=1, source_target_pairs={{0,1},{1,0},{2,3},{3,2},{4,5},{5,4},{6,7},{7,6},{8,9},{9,8},{10,11... | collective-permute-start | bytes 196616 | tf_op jit(solution)/shard_map/ppermute | solution.py:40
  9.9 16.2 %collective-permute-start.4 = (bf16[256,128]{1,0:T(8,128)(2,1)}, bf16[256,128]{1,0:T(8,128)(2,1)S(1)}, u32[]{:S(2)}, u32[]{:S(2)}) collective-permute-start(bf16[256,128]{1,0:T(8,128)(2,1)} %get-tuple-element.47), channel_id=1, source_target_pairs={{0,5},{1,4},{2,7},{3,6},{4,1},{5,0},{6,3},{7,2},{8,13},{9,12},{10,... | collective-permute-start | bytes 196616 | tf_op jit(solution)/shard_map/ppermute | solution.py:40
  10.8 17.4 %collective-permute-start = (bf16[896,128]{1,0:T(8,128)(2,1)}, bf16[896,128]{1,0:T(8,128)(2,1)S(1)}, u32[]{:S(2)}, u32[]{:S(2)}) collective-permute-start(bf16[896,128]{1,0:T(8,128)(2,1)} %get-tuple-element.45), channel_id=1, source_target_pairs={{0,4},{1,5},{2,6},{3,7},{4,0},{5,1},{6,2},{7,3},{8,12},{9,13},{10,... | collective-permute-start | bytes 688136 | tf_op jit(solution)/shard_map/ppermute | solution.py:40
  10.9 17.4 %collective-permute-start.1 = (bf16[896,128]{1,0:T(8,128)(2,1)}, bf16[896,128]{1,0:T(8,128)(2,1)S(1)}, u32[]{:S(2)}, u32[]{:S(2)}) collective-permute-start(bf16[896,128]{1,0:T(8,128)(2,1)} %get-tuple-element.46), channel_id=1, source_target_pairs={{4,8},{5,9},{6,10},{7,11},{8,4},{9,5},{10,6},{11,7},{12,16},{13,17... | collective-permute-start | bytes 688136 | tf_op jit(solution)/shard_map/ppermute | solution.py:40
  14.8 2.4 %collective-permute-start.3 = (bf16[256,128]{1,0:T(8,128)(2,1)}, bf16[256,128]{1,0:T(8,128)(2,1)S(1)}, u32[]{:S(2)}, u32[]{:S(2)}) collective-permute-start(bf16[256,128]{1,0:T(8,128)(2,1)} %get-tuple-element.48), channel_id=1, source_target_pairs={{1,2},{2,1},{5,6},{6,5},{9,10},{10,9},{13,14},{14,13},{17,18},{18,... | collective-permute-start | bytes 196616 | tf_op jit(solution)/shard_map/ppermute | solution.py:40
  16.6 11.7 %copy-start.2 = (bf16[256,128]{1,0:T(8,128)(2,1)}, bf16[256,128]{1,0:T(8,128)(2,1)S(1)}, u32[]{:S(2)}) copy-start(bf16[256,128]{1,0:T(8,128)(2,1)S(1)} %collective-permute-done.2.refs_2_.refs_3_) | copy-start | bytes 196612
  16.6 11.0 %collective-permute-start.5 = (bf16[256,128]{1,0:T(8,128)(2,1)}, bf16[256,128]{1,0:T(8,128)(2,1)S(1)}, u32[]{:S(2)}, u32[]{:S(2)}) collective-permute-start(bf16[256,128]{1,0:T(8,128)(2,1)} %get-tuple-element.48), channel_id=1, source_target_pairs={{1,6},{2,5},{5,2},{6,1},{9,14},{10,13},{13,10},{14,9},{17,22},{18,... | collective-permute-start | bytes 196616 | tf_op jit(solution)/shard_map/ppermute | solution.py:40
  17.3 11.0 %copy-start.4 = (bf16[256,128]{1,0:T(8,128)(2,1)}, bf16[256,128]{1,0:T(8,128)(2,1)S(1)}, u32[]{:S(2)}) copy-start(bf16[256,128]{1,0:T(8,128)(2,1)S(1)} %collective-permute-done.3.refs_3_.refs_4_) | copy-start | bytes 196612
  17.3 10.9 %collective-permute-start.6 = (bf16[256,128]{1,0:T(8,128)(2,1)}, bf16[256,128]{1,0:T(8,128)(2,1)S(1)}, u32[]{:S(2)}, u32[]{:S(2)}) collective-permute-start(bf16[256,128]{1,0:T(8,128)(2,1)} %get-tuple-element.47), channel_id=1, source_target_pairs={{4,9},{5,8},{6,11},{7,10},{8,5},{9,4},{10,7},{11,6},{12,17},{13,16... | collective-permute-start | bytes 196616 | tf_op jit(solution)/shard_map/ppermute | solution.py:40
  26.1 2.2 %copy-start.3 = (bf16[256,128]{1,0:T(8,128)(2,1)}, bf16[256,128]{1,0:T(8,128)(2,1)S(1)}, u32[]{:S(2)}) copy-start(bf16[256,128]{1,0:T(8,128)(2,1)S(1)} %collective-permute-done.4.refs_4_.refs_5_) | copy-start | bytes 196612
  26.1 2.1 %collective-permute-start.7 = (bf16[256,128]{1,0:T(8,128)(2,1)}, bf16[256,128]{1,0:T(8,128)(2,1)S(1)}, u32[]{:S(2)}, u32[]{:S(2)}) collective-permute-start(bf16[256,128]{1,0:T(8,128)(2,1)} %get-tuple-element.48), channel_id=1, source_target_pairs={{5,10},{6,9},{9,6},{10,5},{13,18},{14,17},{17,14},{18,13},{21,26},... | collective-permute-start | bytes 196616 | tf_op jit(solution)/shard_map/ppermute | solution.py:40
  27.6 0.7 copy-start.5
  28.2 0.6 copy-start.6
  28.2 0.6 copy-start.7
  28.2 0.7 copy-start
  28.3 0.8 copy-start.1
  48.6 15.6 %copy-start.12 = (bf16[144,128]{1,0:T(8,128)(2,1)S(1)}, bf16[144,128]{1,0:T(8,128)(2,1)}, u32[]{:S(2)}) copy-start(bf16[144,128]{1,0:T(8,128)(2,1)} %get-tuple-element.55) | copy-start | bytes 110596
  64.4 2.8 %collective-permute-start.8 = (bf16[3840,128]{1,0:T(8,128)(2,1)S(1)}, bf16[3840,128]{1,0:T(8,128)(2,1)}, u32[]{:S(2)}, u32[]{:S(2)}) collective-permute-start(bf16[3840,128]{1,0:T(8,128)(2,1)S(1)} %dynamic-slice_bitcast_fusion), channel_id=1, source_target_pairs={{0,4},{1,5},{2,6},{3,7},{4,0},{5,1},{6,2},{7,3},{8,12},{9,13},{10,... | collective-permute-start | bytes 2949128 | tf_op jit(solution)/shard_map/ppermute | solution.py:40
  64.5 8.3 %copy-start.11 = (bf16[3,3,48,48]{3,2,1,0:T(8,128)(2,1)S(1)}, bf16[3,3,48,48]{3,2,1,0:T(8,128)(2,1)}, u32[]{:S(2)}) copy-start(bf16[3,3,48,48]{3,2,1,0:T(8,128)(2,1)} %param.31) | copy-start | bytes 124420
  68.7 12.5 %collective-permute-start.11 = (bf16[960,128]{1,0:T(8,128)(2,1)S(1)}, bf16[960,128]{1,0:T(8,128)(2,1)S(1)}, u32[]{:S(2)}, u32[]{:S(2)}) collective-permute-start(bf16[960,128]{1,0:T(8,128)(2,1)S(1)} %get-tuple-element.80), channel_id=1, source_target_pairs={{0,3},{1,2},{2,1},{3,0},{4,100},{5,101},{6,102},{7,103},{8,11},{9,... | collective-permute-start | bytes 737288 | tf_op jit(solution)/shard_map/ppermute | solution.py:40
  72.1 9.1 %collective-permute-start.10 = (bf16[960,128]{1,0:T(8,128)(2,1)S(1)}, bf16[960,128]{1,0:T(8,128)(2,1)S(1)}, u32[]{:S(2)}, u32[]{:S(2)}) collective-permute-start(bf16[960,128]{1,0:T(8,128)(2,1)S(1)} %get-tuple-element.81), channel_id=1, source_target_pairs={{0,2},{1,3},{2,0},{3,1},{4,68},{5,69},{6,70},{7,71},{8,10},{9,11},... | collective-permute-start | bytes 737288 | tf_op jit(solution)/shard_map/ppermute | solution.py:40
  72.3 8.9 %collective-permute-start.9 = (bf16[960,128]{1,0:T(8,128)(2,1)S(1)}, bf16[960,128]{1,0:T(8,128)(2,1)S(1)}, u32[]{:S(2)}, u32[]{:S(2)}) collective-permute-start(bf16[960,128]{1,0:T(8,128)(2,1)S(1)} %get-tuple-element.79), channel_id=1, source_target_pairs={{0,1},{1,0},{2,3},{3,2},{4,36},{5,37},{6,38},{7,39},{8,9},{9,8},{1... | collective-permute-start | bytes 737288 | tf_op jit(solution)/shard_map/ppermute | solution.py:40
  73.6 21.8 %copy-start.9 = (bf16[3,3,96,96]{3,2,1,0:T(8,128)(2,1)S(1)}, bf16[3,3,96,96]{3,2,1,0:T(8,128)(2,1)}, u32[]{:S(2)}) copy-start(bf16[3,3,96,96]{3,2,1,0:T(8,128)(2,1)} %param.33) | copy-start | bytes 497668
  81.4 4.7 %collective-permute-start.14 = (bf16[240,128]{1,0:T(8,128)(2,1)S(1)}, bf16[240,128]{1,0:T(8,128)(2,1)S(1)}, u32[]{:S(2)}, u32[]{:S(2)}) collective-permute-start(bf16[240,128]{1,0:T(8,128)(2,1)S(1)} %get-tuple-element.83), channel_id=1, source_target_pairs={{0,96},{1,97},{2,98},{3,99},{4,28},{5,29},{6,30},{7,31},{8,104},{9... | collective-permute-start | bytes 184328 | tf_op jit(solution)/shard_map/ppermute | solution.py:40
  84.5 4.6 %collective-permute-start.13 = (bf16[240,128]{1,0:T(8,128)(2,1)S(1)}, bf16[240,128]{1,0:T(8,128)(2,1)S(1)}, u32[]{:S(2)}, u32[]{:S(2)}) collective-permute-start(bf16[240,128]{1,0:T(8,128)(2,1)S(1)} %get-tuple-element.84), channel_id=1, source_target_pairs={{0,64},{1,65},{2,66},{3,67},{4,20},{5,21},{6,22},{7,23},{8,72},{9,... | collective-permute-start | bytes 184328 | tf_op jit(solution)/shard_map/ppermute | solution.py:40
  84.5 4.5 %collective-permute-start.12 = (bf16[240,128]{1,0:T(8,128)(2,1)S(1)}, bf16[240,128]{1,0:T(8,128)(2,1)S(1)}, u32[]{:S(2)}, u32[]{:S(2)}) collective-permute-start(bf16[240,128]{1,0:T(8,128)(2,1)S(1)} %get-tuple-element.82), channel_id=1, source_target_pairs={{0,32},{1,33},{2,34},{3,35},{4,12},{5,13},{6,14},{7,15},{8,40},{9,... | collective-permute-start | bytes 184328 | tf_op jit(solution)/shard_map/ppermute | solution.py:40
  89.1 7.4 %collective-permute-start.17 = (bf16[240,128]{1,0:T(8,128)(2,1)S(1)}, bf16[240,128]{1,0:T(8,128)(2,1)S(1)}, u32[]{:S(2)}, u32[]{:S(2)}) collective-permute-start(bf16[240,128]{1,0:T(8,128)(2,1)S(1)} %fusion.4), channel_id=1, source_target_pairs={{0,24},{1,25},{2,26},{3,27},{4,7},{5,6},{6,5},{7,4},{8,16},{9,17},... | collective-permute-start | bytes 184328 | tf_op jit(solution)/shard_map/ppermute | solution.py:40
  90.9 6.2 %collective-permute-start.16 = (bf16[240,128]{1,0:T(8,128)(2,1)S(1)}, bf16[240,128]{1,0:T(8,128)(2,1)S(1)}, u32[]{:S(2)}, u32[]{:S(2)}) collective-permute-start(bf16[240,128]{1,0:T(8,128)(2,1)S(1)} %fusion.4), channel_id=1, source_target_pairs={{0,16},{1,17},{2,18},{3,19},{4,6},{5,7},{6,4},{7,5},{8,24},{9,25},... | collective-permute-start | bytes 184328 | tf_op jit(solution)/shard_map/ppermute | solution.py:40
  95.5 3.1 %collective-permute-start.15 = (bf16[240,128]{1,0:T(8,128)(2,1)S(1)}, bf16[240,128]{1,0:T(8,128)(2,1)S(1)}, u32[]{:S(2)}, u32[]{:S(2)}) collective-permute-start(bf16[240,128]{1,0:T(8,128)(2,1)S(1)} %fusion.4), channel_id=1, source_target_pairs={{0,8},{1,9},{2,10},{3,11},{4,5},{5,4},{6,7},{7,6},{8,0},{9,1},{10,... | collective-permute-start | bytes 184328 | tf_op jit(solution)/shard_map/ppermute | solution.py:40
  98.6 9.5 %collective-permute-start.18 = (bf16[240,128]{1,0:T(8,128)(2,1)S(1)}, bf16[240,128]{1,0:T(8,128)(2,1)S(1)}, u32[]{:S(2)}, u32[]{:S(2)}) collective-permute-start(bf16[240,128]{1,0:T(8,128)(2,1)S(1)} %add_convert_fusion), channel_id=1, source_target_pairs={{0,32},{1,33},{2,34},{3,35},{4,12},{5,13},{6,14},{7,15},{8,40},{9,... | collective-permute-start | bytes 184328 | tf_op jit(solution)/shard_map/ppermute | solution.py:40
  99.5 8.6 %collective-permute-start.19 = (bf16[240,128]{1,0:T(8,128)(2,1)S(1)}, bf16[240,128]{1,0:T(8,128)(2,1)S(1)}, u32[]{:S(2)}, u32[]{:S(2)}) collective-permute-start(bf16[240,128]{1,0:T(8,128)(2,1)S(1)} %add_convert_fusion), channel_id=1, source_target_pairs={{0,64},{1,65},{2,66},{3,67},{4,20},{5,21},{6,22},{7,23},{8,72},{9,... | collective-permute-start | bytes 184328 | tf_op jit(solution)/shard_map/ppermute | solution.py:40
  101.7 6.4 %collective-permute-start.20 = (bf16[240,128]{1,0:T(8,128)(2,1)S(1)}, bf16[240,128]{1,0:T(8,128)(2,1)S(1)}, u32[]{:S(2)}, u32[]{:S(2)}) collective-permute-start(bf16[240,128]{1,0:T(8,128)(2,1)S(1)} %add_convert_fusion), channel_id=1, source_target_pairs={{0,96},{1,97},{2,98},{3,99},{4,28},{5,29},{6,30},{7,31},{8,104},{9... | collective-permute-start | bytes 184328 | tf_op jit(solution)/shard_map/ppermute | solution.py:40
  108.1 9.0 %collective-permute-start.21 = (bf16[960,128]{1,0:T(8,128)(2,1)S(1)}, bf16[960,128]{1,0:T(8,128)(2,1)S(1)}, u32[]{:S(2)}, u32[]{:S(2)}) collective-permute-start(bf16[960,128]{1,0:T(8,128)(2,1)S(1)} %bitcast.72), channel_id=1, source_target_pairs={{0,1},{1,0},{2,3},{3,2},{4,36},{5,37},{6,38},{7,39},{8,9},{9,8},{1... | collective-permute-start | bytes 737288 | tf_op jit(solution)/shard_map/ppermute | solution.py:40
  108.9 9.6 %collective-permute-start.22 = (bf16[960,128]{1,0:T(8,128)(2,1)S(1)}, bf16[960,128]{1,0:T(8,128)(2,1)S(1)}, u32[]{:S(2)}, u32[]{:S(2)}) collective-permute-start(bf16[960,128]{1,0:T(8,128)(2,1)S(1)} %bitcast.73), channel_id=1, source_target_pairs={{0,2},{1,3},{2,0},{3,1},{4,68},{5,69},{6,70},{7,71},{8,10},{9,11},... | collective-permute-start | bytes 737288 | tf_op jit(solution)/shard_map/ppermute | solution.py:40
  112.3 8.8 %collective-permute-start.23 = (bf16[960,128]{1,0:T(8,128)(2,1)S(1)}, bf16[960,128]{1,0:T(8,128)(2,1)S(1)}, u32[]{:S(2)}, u32[]{:S(2)}) collective-permute-start(bf16[960,128]{1,0:T(8,128)(2,1)S(1)} %bitcast.74), channel_id=1, source_target_pairs={{0,3},{1,2},{2,1},{3,0},{4,100},{5,101},{6,102},{7,103},{8,11},{9,... | collective-permute-start | bytes 737288 | tf_op jit(solution)/shard_map/ppermute | solution.py:40
  121.2 8.6 %collective-permute-start.24 = (bf16[3840,128]{1,0:T(8,128)(2,1)S(1)}, bf16[3840,128]{1,0:T(8,128)(2,1)S(1)}, u32[]{:S(2)}, u32[]{:S(2)}) collective-permute-start(bf16[3840,128]{1,0:T(8,128)(2,1)S(1)} %bitcast.66), channel_id=1, source_target_pairs={{0,4},{1,5},{2,6},{3,7},{4,0},{5,1},{6,2},{7,3},{8,12},{9,13},{10,... | collective-permute-start | bytes 2949128 | tf_op jit(solution)/shard_map/ppermute | solution.py:40

commit v2 on v1

--- a/solution.py
+++ b/solution.py
@@ -11,6 +11,7 @@
 FINE, MID = 48, 96
 COARSE_ROWS, COARSE_COLS, COARSE = 8, 64, 192
 PITCH = 80
+AT_MID, AT_FINE, AT_LIFT, SUM_ROWS = 5184, 6912, 7344, 7680
 PARAMS = pltpu.CompilerParams(vmem_limit_bytes=56 * 2**20)
 
 AXES = ("row", "col")
@@ -72,21 +73,15 @@
     return lax.optimization_barrier((stage(block), work(*operands)))
 
 
-def all_sum(block, works):
-    core, mine = my_place()
-    half = block.shape[0] // 2
-    halves = block.reshape(2, half, block.shape[1])
-    other = send(lax.dynamic_index_in_dim(halves, 1 - core, 0, keepdims=False), CORE_PAIRS)
-    own = lax.dynamic_index_in_dim(halves, core, 0, keepdims=False)
-    part = (own.astype(jnp.float32) + other.astype(jnp.float32)).astype(jnp.bfloat16)
+def all_sum(kept, given, works):
+    _, mine = my_place()
+    part = (kept.astype(jnp.float32) + send(given, CORE_PAIRS).astype(jnp.float32)).astype(jnp.bfloat16)
     part, out_0 = beside(lambda x: scatter_stage(x, 0, mine[0]), part, *works[0])
     part = scatter_stage(part, 1, mine[1])
     part = reduce_stage(part, 2)
     part, out_1 = beside(lambda x: gather_stage(x, 1, mine[1]), part, *works[1])
     part, out_2 = beside(lambda x: gather_stage(x, 0, mine[0]), part, *works[2])
-    other = send(part, CORE_PAIRS)
-    whole = jnp.where(core == 0, jnp.concatenate([part, other]), jnp.concatenate([other, part]))
-    return whole, out_0, out_1, out_2
+    return part, send(part, CORE_PAIRS), out_0, out_1, out_2
 
 
 def partner(at, count, pairing):
@@ -214,15 +209,57 @@
 
 
 class Halo:
-    def __init__(self, parity, refs):
-        row_0, row_1, col_0, col_1, *corner = [ref[...] for ref in refs]
+    def __init__(self, parity, row_0, row_1, col_0, col_1):
         row_even, col_even = parity[0] == 0, parity[1] == 0
-        self.top, self.bottom = jnp.where(row_even, row_1, row_0), jnp.where(row_even, row_0, row_1)
-        self.left, self.right = jnp.where(col_even, col_1, col_0), jnp.where(col_even, col_0, col_1)
-        left = [jnp.where(col_even, corner[2 * p + 1], corner[2 * p]) for p in range(2)]
-        right = [jnp.where(col_even, corner[2 * p], corner[2 * p + 1]) for p in range(2)]
-        self.top_left, self.bottom_left = jnp.where(row_even, left[1], left[0]), jnp.where(row_even, left[0], left[1])
-        self.top_right, self.bottom_right = jnp.where(row_even, right[1], right[0]), jnp.where(row_even, right[0], right[1])
+        rows, cols = (row_0[...], row_1[...]), (col_0[...], col_1[...])
+        self.top, self.bottom = jnp.where(row_even, rows[1], rows[0]), jnp.where(row_even, rows[0], rows[1])
+        self.left, self.right = jnp.where(col_even, cols[1], cols[0]), jnp.where(col_even, cols[0], cols[1])
+
+
+def corner_kernel(parity, row_0, row_1, side_0, side_1, col_0, col_1):
+    half = jnp.bfloat16
+    row_even = parity[0] == 0
+    halos = (jnp.where(row_even, row_1[...], row_0[...]), jnp.where(row_even, row_0[...], row_1[...]))
+    wide = jnp.concatenate(
+        [
+            jnp.concatenate([jnp.concatenate([rim[576:704, :], rim[768:896, 0:64]], axis=1),
+                             jnp.concatenate([rim[704:768, :], rim[768:832, 64:128]], axis=1)], axis=0)
+            for rim in halos
+        ],
+        axis=0,
+    )
+    sides = []
+    for (first, second, single), starts in (((0, 1, 0), (0, 192)), ((126, 127, 127), (96, 240))):
+        parts = []
+        for rim in halos:
+            edge = (
+                dot(picks((16, 128), ((0, first), (1, second))), rim[starts[0] : starts[0] + 256], 1, 1)
+                + dot(picks((16, 128), ((2, single),)), rim[starts[1] : starts[1] + 256], 1, 1)
+                + dot(picks((16, 128), ((3, first), (4, second))), rim[288:544], 1, 1)
+                + dot(picks((16, 128), ((5, single),)), rim[480:736], 1, 1)
+            ).astype(half)
+            parts += [edge[:, :128], edge[:, 128:]]
+        first, second, single = (0, 1, 0) if first == 0 else (62, 63, 63)
+        pairs = []
+        for index, at in ((0, 0), (5, 192)):
+            pairs += [(index, at + first), (index + 1, at + second), (index + 2, at + 64 + first), (index + 3, at + 64 + second)]
+            pairs.append((index + 4, at + 128 + single))
+        rim = dot(picks((16, 384), pairs), wide).astype(half)
+        parts += [rim[:, :128], jnp.concatenate([rim[:, 128:], jnp.zeros((16, 64), half)], axis=1)]
+        sides.append(jnp.concatenate(parts, axis=0))
+    for out, side, to_right in ((col_0, side_0, parity[1] == 0), (col_1, side_1, parity[1] == 1)):
+        out[0:256, :] = side[...]
+        out[256:352, :] = jnp.where(to_right, sides[1], sides[0])
+
+
+def corners(parity, *messages):
+    return pl.pallas_call(
+        corner_kernel,
+        out_shape=[jax.ShapeDtypeStruct((352, 128), jnp.bfloat16)] * 2,
+        in_specs=[IN_SMEM] + [IN_VMEM] * 4,
+        compiler_params=PARAMS,
+        name="corners",
+    )(parity, *messages)
 
 
 def prep(*args):
@@ -241,15 +278,11 @@
     )(*args)
 
 
-def unit_kernel(
-    parity, *refs, chans, rows, width, edge, fill_rows, write_grads,
-):
-    halo = Halo(parity, refs[:8])
-    source, inner, masked, second, px, grads, mx, ix, sx, acc_first, acc_second = refs[8:]
+def channel_part(halo, second, refs, write_px, *, chans, rows, width, edge, fill_rows):
+    source, inner, px, mx, ix, sx, acc_first, acc_second = refs
     ring = width + 128
     half = jnp.bfloat16
 
-    mx[2 * chans : 2 * chans + CELLS, 0:width] = masked[...]
     ix[chans : chans + CELLS, 0:width] = jnp.transpose(inner[...], (1, 0, 2)).reshape(CELLS, width)
     sx[...] = jnp.transpose(source[...], (1, 0, 2)).reshape(CELLS, width)
     fill_rows(mx, ix, halo.top, 0, 0)
@@ -268,20 +301,13 @@
         cols = columns(halo.right, halo.left, tile)
         mx[2 * chans + tile * 128 : 2 * chans + (tile + 1) * 128, width:ring] = cols[:, :128]
         ix[chans + tile * 128 : chans + (tile + 1) * 128, width:ring] = cols[:, 128:]
-    for tile in range((CELLS - 2 * chans) // 128, 12):
-        cols = columns(halo.top_right, halo.top_left, tile)
-        skip = max(0, CELLS - 2 * chans - tile * 128)
-        at = tile * 128 + skip - (CELLS - 2 * chans)
-        mx[at : at + 128 - skip, width:ring] = cols[skip:, :128]
-        if tile == 11:
-            ix[0:chans, width:ring] = cols[128 - chans :, 128:]
     for tile in range(-(-2 * chans // 128)):
-        cols = columns(halo.bottom_right, halo.bottom_left, tile)
         size = min(128, 2 * chans - tile * 128)
-        at = 2 * chans + CELLS + tile * 128
-        mx[at : at + size, width:ring] = cols[:size, :128]
-        if tile == 0:
-            ix[chans + CELLS :, width:ring] = cols[:chans, 128:]
+        for first_tile, at, inner_at in ((16, 0, 0), (18, 2 * chans + CELLS, chans + CELLS)):
+            cols = columns(halo.right, halo.left, first_tile + tile)
+            mx[at + tile * 128 : at + tile * 128 + size, width:ring] = cols[:size, :128]
+            if tile == 0:
+                ix[inner_at : inner_at + chans, width:ring] = cols[:chans, 128:]
 
     def before(row, carry):
         at = pl.multiple_of(row * chans, 16)
@@ -289,7 +315,8 @@
         px[pl.ds(at, chans), :] = keep(ix[pl.ds(at, chans), :].astype(jnp.float32), inner_grad).astype(half)
         return carry
 
-    lax.fori_loop(0, rows + 2, before, 0, unroll=2)
+    lax.fori_loop(0, rows + 2, before, 0, unroll=True)
+    write_px()
 
     def spread(tile):
         wide = jnp.concatenate([tile.astype(jnp.float32), jnp.zeros((chans, 128), jnp.float32)], axis=1)
@@ -306,8 +333,7 @@
         acc_second[...] += dot(spread(own), mx[pl.ds(pl.multiple_of(at + chans, 16), 3 * chans), :], 1, 1)
         return carry
 
-    lax.fori_loop(0, rows, after, 0, unroll=2)
-    write_grads(grads, acc_first, acc_second)
+    lax.fori_loop(0, rows, after, 0, unroll=True)
 
 
 def ring_taps(weight, window, chans, ring):
@@ -322,7 +348,7 @@
         ox[pl.ds(row, 1), :, :] = (masked[pl.ds(at, chans), :].astype(jnp.float32) + grad).astype(jnp.bfloat16)[None]
         return carry
 
-    lax.fori_loop(0, rows, step, 0, unroll=2)
+    lax.fori_loop(0, rows, step, 0, unroll=True)
     out[...] = jnp.transpose(ox[...], (1, 0, 2))
 
 
@@ -355,34 +381,6 @@
             grads[at : at + 288, :] = part.astype(jnp.bfloat16)
 
 
-def channel_grads(parity, halo, source, inner, masked, second, chans, rows, width, edge, fill_rows, grad_rows, write_grads, name):
-    half = jnp.bfloat16
-    ring = width + 128
-
-    def kernel(*refs):
-        unit_kernel(
-            *refs, chans=chans, rows=rows, width=width, edge=edge, fill_rows=fill_rows, write_grads=write_grads
-        )
-
-    return pl.pallas_call(
-        kernel,
-        out_shape=[
-            jax.ShapeDtypeStruct(((rows + 2) * chans, ring), half),
-            jax.ShapeDtypeStruct((grad_rows, 128), half),
-        ],
-        in_specs=[IN_SMEM] + [IN_VMEM] * 12,
-        scratch_shapes=[
-            pltpu.VMEM(((rows + 4) * chans, ring), half),
-            pltpu.VMEM(((rows + 2) * chans, ring), half),
-            pltpu.VMEM((CELLS, width), half),
-            pltpu.VMEM((3 * chans, 3 * chans), jnp.float32),
-            pltpu.VMEM((3 * chans, 3 * chans), jnp.float32),
-        ],
-        compiler_params=PARAMS,
-        name=name,
-    )(parity, *halo, source, inner, masked, stacked(second, chans))
-
-
 def stacked(weight, chans):
     return jnp.transpose(weight[::-1], (1, 2, 0, 3)).reshape(3 * chans, 3 * chans)
 
@@ -401,17 +399,20 @@
 
 
 def coarse_places():
-    place = np.zeros((2, 13 * 16, 6 * 32), np.float32)
+    place = np.zeros((2, 13 * 16, 96), np.float32)
     for index, first_row, count, sides in ((0, -2, 12, ((0, 0, "r"), (1, 1, "r"), (14, 0, "l"), (15, 1, "l"))), (1, -1, 10, ((0, 2, "r"), (15, 2, "l")))):
         for block in range(count + 1):
             for at, which, side in sides:
                 row = first_row + block - (1 if side == "r" else 0)
                 if row < first_row or row >= first_row + count:
                     continue
-                message = 0 if 0 <= row < 8 else 1 if row < 0 else 2
-                source = 2 * message + (0 if side == "r" else 1)
-                place[index, block * 16 + at, source * 32 + which * 8 + row % 8] = 1
-    return place.reshape(2 * 13 * 16, 6 * 32)
+                if 0 <= row < 8:
+                    source = (0 if side == "r" else 32) + which * 8 + row
+                else:
+                    source = (64 if side == "r" else 80) + (0 if row < 0 else 5)
+                    source += 4 if index else 2 * (row + 2 if row < 0 else row - 8) + which
+                place[index, block * 16 + at, source] = 1
+    return place.reshape(2 * 13 * 16, 96)
 
 
 def coarse_taps(ref, weight, start, size):
@@ -423,16 +424,13 @@
     return total
 
 
-def coarse_kernel(parity, *refs):
-    halo = Halo(parity, refs[:8])
-    source, inner, masked, second, place, px, grads, mx, ix, own, turned, tail = refs[8:]
+def coarse_part(halo, second, place, refs, write_px):
+    source, inner, masked, grads, px, mx, ix, own, turned, tail = refs
     half = jnp.bfloat16
     lead = 16
     rims = jnp.concatenate(
-        [
-            jnp.concatenate([ref[192:224, :], ref[224:256, 0:64]], axis=1)
-            for ref in (halo.right, halo.left, halo.top_right, halo.top_left, halo.bottom_right, halo.bottom_left)
-        ],
+        [jnp.concatenate([rim[192:224, :], rim[224:256, 0:64]], axis=1) for rim in (halo.right, halo.left)]
+        + [jnp.concatenate([rim[320:336, :], rim[336:352, 0:64]], axis=1) for rim in (halo.right, halo.left)],
         axis=0,
     )
     rims = dot(place[...], rims).astype(half)
@@ -465,6 +463,7 @@
             ix[start : start + 272, :].astype(jnp.float32), inner_grad
         ).astype(half)
     shifted(px, 816)
+    write_px()
     def corr(tile, ref, start, write):
         own[...] = jnp.zeros(own.shape, half)
         for row in range(8):
@@ -491,31 +490,140 @@
     corr(source, px, lead, write_first)
 
 
-def coarse_grads(parity, halo, source, inner, masked, second):
+def grads_kernel(parity, *refs):
+    messages, (second_coarse, second_mid, second_fine, place, lift), refs = refs[:4], refs[4:9], refs[9:]
+    arrays, (px_coarse, px_mid, px_fine, kept, given), refs = refs[:9], refs[9:14], refs[14:]
+    held, work, (load_sems, px_sems, sum_sems) = refs[:7], refs[7:28], refs[28:]
+    coarse_work, mid_work, fine_work = work[:7], work[7:14], work[14:21]
+    sum_coarse, sum_mid, sum_fine = coarse_work[0], mid_work[0], fine_work[0]
+    mx_mid, mx_fine = mid_work[2], fine_work[2]
+    core = parity[0]
+
+    places = (
+        *held[:3],
+        held[3], held[4], mx_mid.at[2 * MID : 2 * MID + CELLS, 0:128],
+        held[5], held[6], mx_fine.at[2 * FINE : 2 * FINE + CELLS, 0:256],
+    )
+    loads = [pltpu.make_async_copy(array, to, load_sems.at[k]) for k, (array, to) in enumerate(zip(arrays, places))]
+    for load in loads:
+        load.start()
+    halo = Halo(parity, *messages)
+
+    px_copies = [
+        pltpu.make_async_copy(work[1], out, px_sems.at[k])
+        for k, (work, out) in enumerate(((coarse_work, px_coarse), (mid_work, px_mid), (fine_work, px_fine)))
+    ]
+    half_rows = SUM_ROWS // 2
+
+    def sum_copies(k, source, at, size):
+        start = at % half_rows
+        return [pltpu.make_async_copy(source, out.at[start : start + size, :], sum_sems.at[k]) for out in (kept, given)]
+
+    def write(copies, at):
+        keeps = core == at // half_rows
+
+        @pl.when(keeps)
+        def _():
+            copies[0].start()
+
+        @pl.when(jnp.logical_not(keeps))
+        def _():
+            copies[1].start()
+
+    rest = AT_MID - half_rows
+    pieces = (
+        (sum_coarse.at[0:half_rows, :], 0, half_rows),
+        (sum_coarse.at[half_rows:AT_MID, :], half_rows, rest),
+        (sum_mid, AT_MID, AT_FINE - AT_MID),
+        (sum_fine, AT_FINE, SUM_ROWS - AT_FINE),
+    )
+    sums = [sum_copies(k, *piece) for k, piece in enumerate(pieces)]
+
+    for load in loads[:3]:
+        load.wait()
+    coarse_part(halo, second_coarse, place, (*held[:3], *coarse_work), px_copies[0].start)
+    write(sums[0], pieces[0][1])
+    write(sums[1], pieces[1][1])
+
+    for load in loads[3:6]:
+        load.wait()
+    channel_part(
+        halo, second_mid, (held[3], held[4], *mid_work[1:]), px_copies[1].start,
+        chans=MID, rows=16, width=128, edge=3, fill_rows=mid_rows,
+    )
+    mid_grads(sum_mid, mid_work[5], mid_work[6])
+    write(sums[2], pieces[2][1])
+
+    for load in loads[6:]:
+        load.wait()
+    channel_part(
+        halo, second_fine, (held[5], held[6], *fine_work[1:]), px_copies[2].start,
+        chans=FINE, rows=32, width=256, edge=0, fill_rows=fine_rows,
+    )
+    fine_grads(sum_fine, fine_work[5], fine_work[6])
+    sum_fine[432:576, :] = lift[...]
+    sum_fine[576:, :] = jnp.zeros((SUM_ROWS - AT_LIFT - 144, 128), jnp.bfloat16)
+    write(sums[3], pieces[3][1])
+
+    for copy in px_copies:
+        copy.wait()
+    for copies in sums:
+        copies[0].wait()
+
+
+def grads(parity, messages, seconds, lift, arrays):
     half = jnp.bfloat16
+    any_memory = pl.BlockSpec(memory_space=pl.ANY)
+    full = jnp.float32
+
+    def channel_work(chans, rows, width, sum_rows):
+        ring = width + 128
+        return [
+            ((sum_rows, 128), half),
+            (((rows + 2) * chans, ring), half),
+            (((rows + 4) * chans, ring), half),
+            (((rows + 2) * chans, ring), half),
+            ((CELLS, width), half),
+            ((3 * chans, 3 * chans), full),
+            ((3 * chans, 3 * chans), full),
+        ]
+
+    tile = ((COARSE_ROWS, COARSE_COLS, COARSE), half)
+    held = [tile, tile, tile] + [((MID, 16, 128), half)] * 2 + [((FINE, 32, 256), half)] * 2
+    coarse_work = [
+        ((AT_MID, 128), half),
+        ((3, 816, COARSE), half),
+        ((3, 976, COARSE), half),
+        ((816, COARSE), half),
+        ((8 * PITCH, COARSE), half),
+        ((COARSE, 8 * PITCH), half),
+        ((1728, 64), half),
+    ]
+    scratch = held + coarse_work + channel_work(MID, 16, 128, AT_FINE - AT_MID) + channel_work(FINE, 32, 256, SUM_ROWS - AT_FINE)
     return pl.pallas_call(
-        coarse_kernel,
+        grads_kernel,
         out_shape=[
             jax.ShapeDtypeStruct((3, 816, COARSE), half),
-            jax.ShapeDtypeStruct((5184, 128), half),
+            jax.ShapeDtypeStruct((18 * MID, 256), half),
+            jax.ShapeDtypeStruct((34 * FINE, 384), half),
+            jax.ShapeDtypeStruct((SUM_ROWS // 2, 128), half),
+            jax.ShapeDtypeStruct((SUM_ROWS // 2, 128), half),
         ],
-        in_specs=[IN_SMEM] + [IN_VMEM] * 13,
-        scratch_shapes=[
-            pltpu.VMEM((3, 976, COARSE), half),
-            pltpu.VMEM((816, COARSE), half),
-            pltpu.VMEM((8 * PITCH, COARSE), half),
-            pltpu.VMEM((COARSE, 8 * PITCH), half),
-            pltpu.VMEM((1728, 64), half),
-        ],
+        in_specs=[IN_SMEM] + [IN_VMEM] * 9 + [any_memory] * 9,
+        out_specs=[any_memory] * 5,
+        scratch_shapes=[pltpu.VMEM(*shape) for shape in scratch]
+        + [pltpu.SemaphoreType.DMA((9,)), pltpu.SemaphoreType.DMA((3,)), pltpu.SemaphoreType.DMA((4,))],
         compiler_params=PARAMS,
-        name="coarse_grads",
-    )(parity, *halo, source, inner, masked, second, jnp.asarray(coarse_places(), half))
+        name="grads",
+    )(parity, *messages, *seconds, jnp.asarray(coarse_places(), half), lift, *arrays)
 
 
 def coarse_input_kernel(masked, px, first, out):
-    for row in range(8):
-        grad = coarse_taps(px, first, 16 + row * PITCH, 64)
-        out[row] = (masked[row].astype(jnp.float32) + grad).astype(jnp.bfloat16)
+    for start in range(0, 8, 4):
+        grad = coarse_taps(px, first, 16 + start * PITCH, 4 * PITCH)
+        for row in range(start, start + 4):
+            at = (row - start) * PITCH
+            out[row] = (masked[row].astype(jnp.float32) + grad[at : at + 64]).astype(jnp.bfloat16)
 
 
 def coarse_input(masked, px, first):
@@ -527,12 +635,23 @@
     )(masked, px, first)
 
 
-AT_MID, AT_FINE, AT_LIFT, SUM_ROWS = 5184, 6912, 7344, 7680
-
-
-def unpack_kernel(summed, first_fine, second_fine, first_mid, second_mid, first_coarse, second_coarse, lift_mid, lift_coarse):
+def unpack_kernel(parity, kept, other, *refs):
+    outs, tiles, sems = refs[:8], refs[8:16], refs[16]
+    mine, theirs = kept[...], other[...]
+    first_half = parity[0] == 0
+    halves = (jnp.where(first_half, mine, theirs), jnp.where(first_half, theirs, mine))
+    first_fine, second_fine, first_mid, second_mid, first_coarse, second_coarse, lift_mid, lift_coarse = tiles
+
     def part(start, size, lanes=slice(0, 128)):
-        return summed[start : start + size, lanes].astype(jnp.float32)
+        at = start % 3840
+        return halves[start // 3840][at : at + size, lanes].astype(jnp.float32)
+
+    copies = []
+
+    def leave(tile, out):
+        copy = pltpu.make_async_copy(tile, out, sems.at[len(copies)])
+        copy.start()
+        copies.append(copy)
 
     for tap in range(9):
         row_tap, col_tap = tap // 3, tap % 3
@@ -541,24 +660,42 @@
         second_coarse[row_tap, col_tap, :, 128:192] = tails[:, :64]
         first_coarse[row_tap, col_tap, :, 0:128] = part(1728 + tap * COARSE, COARSE)
         first_coarse[row_tap, col_tap, :, 128:192] = tails[:, 64:]
+        if col_tap == 2:
+            leave(second_coarse.at[row_tap], outs[5].at[row_tap])
+            leave(first_coarse.at[row_tap], outs[4].at[row_tap])
+    for tap in range(9):
+        row_tap, col_tap = tap // 3, tap % 3
+        second_mid[row_tap, col_tap] = part(AT_MID + tap * MID, MID, slice(0, 96))
+        first_mid[row_tap, col_tap] = part(AT_MID + 864 + tap * MID, MID, slice(0, 96))
+    leave(second_mid, outs[3])
+    leave(first_mid, outs[2])
+    for tap in range(9):
+        row_tap, col_tap = tap // 3, tap % 3
         pair = part(AT_FINE + tap * FINE, FINE)
         second_fine[row_tap, col_tap] = pair[:, 0:48]
         first_fine[row_tap, col_tap] = pair[:, 48:96]
-        second_mid[row_tap, col_tap] = part(AT_MID + tap * MID, MID, slice(0, 96))
-        first_mid[row_tap, col_tap] = part(AT_MID + 864 + tap * MID, MID, slice(0, 96))
+    leave(second_fine, outs[1])
+    leave(first_fine, outs[0])
     lift_mid[...] = part(AT_LIFT, 48, slice(0, 96))
     lift_coarse[:, 0:128] = part(AT_LIFT + 96, 48)
     lift_coarse[:, 128:192] = part(AT_LIFT + 48, 48, slice(0, 64))
-
-
-def unpack(summed):
+    leave(lift_mid, outs[6])
+    leave(lift_coarse, outs[7])
+    for copy in copies:
+        copy.wait()
+
+
+def unpack(parity, kept, other):
     shapes = ((3, 3, 48, 48),) * 2 + ((3, 3, 96, 96),) * 2 + ((3, 3, 192, 192),) * 2 + ((48, 96), (48, 192))
     *taps, lift_mid, lift_coarse = pl.pallas_call(
         unpack_kernel,
         out_shape=[jax.ShapeDtypeStruct(shape, jnp.float32) for shape in shapes],
+        in_specs=[IN_SMEM, IN_VMEM, IN_VMEM],
+        out_specs=[pl.BlockSpec(memory_space=pl.ANY)] * 8,
+        scratch_shapes=[pltpu.VMEM(shape, jnp.float32) for shape in shapes] + [pltpu.SemaphoreType.DMA((12,))],
         compiler_params=PARAMS,
         name="unpack",
-    )(summed)
+    )(parity, kept, other)
     return *taps, jnp.transpose(lift_mid), jnp.transpose(lift_coarse)
 
 
@@ -575,33 +712,26 @@
         parity, grad_joined, joined_fine, unit_fine, inner_fine, unit_mid, inner_mid, unit_coarse, inner_coarse,
         jnp.transpose(lift_mid), jnp.transpose(lift_coarse),
     )
-    halo = (
-        send(row_0, swap_pairs(0, None)),
-        send(row_1, swap_pairs(1, None)),
-        send(col_0, swap_pairs(None, 0)),
-        send(col_1, swap_pairs(None, 1)),
-        send(col_0, swap_pairs(0, 0)),
-        send(col_1, swap_pairs(0, 1)),
-        send(col_0, swap_pairs(1, 0)),
-        send(col_1, swap_pairs(1, 1)),
-    )
-    coarse_px, coarse_part = coarse_grads(parity, halo, input_coarse, inner_coarse, coarse, second_coarse)
-    mid_px, mid_part = channel_grads(
-        parity, halo, input_mid, inner_mid, mid, second_mid, MID, 16, 128, 3, mid_rows, 1728, mid_grads, "mid_grads"
-    )
-    fine_px, fine_part = channel_grads(
-        parity, halo, input_fine, inner_fine, fine, second_fine, FINE, 32, 256, 0, fine_rows, 432, fine_grads, "fine_grads"
-    )
-    unused = jnp.zeros((SUM_ROWS - AT_LIFT - 144, 128), jnp.bfloat16)
-    summed, fine_input, mid_input, input_grad = all_sum(
-        jnp.concatenate([coarse_part, mid_part, fine_part, lift, unused]),
+    row_0, row_1 = send(row_0, swap_pairs(0, None)), send(row_1, swap_pairs(1, None))
+    col_0, col_1 = corners(parity, row_0, row_1, col_0, col_1)
+    col_0, col_1 = send(col_0, swap_pairs(None, 0)), send(col_1, swap_pairs(None, 1))
+    coarse_px, mid_px, fine_px, kept, given = grads(
+        parity,
+        (row_0, row_1, col_0, col_1),
+        (second_coarse, stacked(second_mid, MID), stacked(second_fine, FINE)),
+        lift,
+        (input_coarse, inner_coarse, coarse, input_mid, inner_mid, mid, input_fine, inner_fine, fine),
+    )
+    kept, other, fine_input, mid_input, input_grad = all_sum(
+        kept,
+        given,
         (
             (lambda px: channel_input(fine, px, first_fine, FINE, 32, 256, "fine_input"), fine_px),
             (lambda px: channel_input(mid, px, first_mid, MID, 16, 128, "mid_input"), mid_px),
             (lambda px: coarse_input(coarse, px, first_coarse), coarse_px),
         ),
     )
-    return (fine_input, mid_input, jnp.transpose(input_grad, (2, 0, 1)), *unpack(summed))
+    return (fine_input, mid_input, jnp.transpose(input_grad, (2, 0, 1)), *unpack(parity, kept, other))
 
 
 def solution(mesh):

time: 136 us -> 109 us (0.80)
  Pallas kernels: 59.9 us -> 39.4 us
  starting transfers between devices: 46.7 us -> 38.8 us
  waiting for transfers between devices: 15.3 us -> 20.1 us
  local copies, waits for them, and re-layouts: 8.46 us -> 6.5 us
  other arithmetic: 4.09 us -> 2.31 us
    pallas_call x3 -> x2, Pallas kernels: 31.8 us -> 18.3 us  [the longest x1 16 us: grads(): pl.pallas_call(grads_kernel, out_shape=[jax.ShapeDtypeStruct((3, 816, COA...]
    ppermute x25 -> x21, starting transfers between devices: 46.7 us -> 38.8 us  [send(): return lax.ppermute(block, AXES, pairs)]
    pallas_call x2, Pallas kernels: 13 us -> 7.55 us  [channel_input(): pl.pallas_call(kernel, out_shape=jax.ShapeDtypeStruct((chans, rows, width...]
    ppermute x25 -> x21, waiting for transfers between devices: 15.3 us -> 20.1 us  [send(): return lax.ppermute(block, AXES, pairs)]
    unnamed x30 -> x20, local copies, waits for them, and re-layouts: 4.17 us -> 2.31 us
    select_n x1 -> x0, other arithmetic: 1.84 us -> none  [all_sum(): jnp.where(core == 0, jnp.concatenate([part, other]), jnp.concatenate([oth...]
    pallas_call x1, Pallas kernels: 4.67 us -> 3.27 us  [coarse_input(): pl.pallas_call(coarse_input_kernel, out_shape=jax.ShapeDtypeStruct((COARS...]
  transfers between devices with their start and end apart: 25 -> 21, of which waited for: 9 -> 13; matrix products, arithmetic and copies ran while one was open for 3% -> 4% of each run, Pallas kernels for 13% -> 10%
where the time goes in v2:
time: 109 us; the launch traced here: 108 us
  Pallas kernels  39.4 us (36%)
  starting transfers between devices  38.8 us (36%)
  waiting for transfers between devices  20.1 us (18%)
  local copies, waits for them, and re-layouts  6.5 us (6%)
  other arithmetic  2.31 us (2%)
  between operations  1.12 us (1%)
    ppermute x21, starting transfers between devices, send(): return lax.ppermute(block, AXES, pairs)  38.8 us
    ppermute x21, waiting for transfers between devices, send(): return lax.ppermute(block, AXES, pairs)  20.1 us
    pallas_call x1, Pallas kernels, grads(): pl.pallas_call(grads_kernel, out_shape=[jax.ShapeDtypeStruct((3, 816, COA...  16 us
    pallas_call x2, Pallas kernels, channel_input(): pl.pallas_call(kernel, out_shape=jax.ShapeDtypeStruct((chans, rows, width...  7.55 us
    pallas_call x1, Pallas kernels, prep(): pl.pallas_call(prep_kernel, out_shape=[jax.ShapeDtypeStruct(shape, half)...  6.46 us
    pallas_call x1, Pallas kernels, unpack(): pl.pallas_call(unpack_kernel, out_shape=[jax.ShapeDtypeStruct(shape, jnp....  3.9 us
    pallas_call x1, Pallas kernels, coarse_input(): pl.pallas_call(coarse_input_kernel, out_shape=jax.ShapeDtypeStruct((COARS...  3.27 us
    reshape x4, local copies, waits for them, and re-layouts, stacked(): jnp.transpose(weight[::-1], (1, 2, 0, 3)).reshape(3 * chans, 3 * chans)  3.27 us
  transfers between devices with their start and end apart: 21, of which 13 were waited for; matrix products, arithmetic and copies ran while one was open for 4% of the time, Pallas kernels for 10%

profile of v2, /device:TPU:1, one launch (start us, length us, event | category | flops | bytes accessed | tf_op | source)
XLA Modules:
  0.0 108.3 jit_solution(4541439254225631635)
XLA Ops:
  0.7 0.6 pad_add_fusion.parity
  1.3 6.5 %prep.1 = (bf16[1536,256]{1,0:T(8,128)(2,1)}, bf16[1536,128]{1,0:T(8,128)(2,1)}, bf16[8,64,192]{2,1,0:T(8,128)(2,1)}, bf16[896,128]{1,0:T(8,128)(2,1)}, bf16[896...) custom-call(s32[2]{0:T(128)} %pad_add_fusion.parity, ...), custom_call_target="tpu_custom_call" | custom-call | tf_op jit(solution)/shard_map/prep/pallas_call | solution.py:271
  7.7 1.5 %collective-permute-start = (bf16[896,128]{1,0:T(8,128)(2,1)}, bf16[896,128]{1,0:T(8,128)(2,1)S(1)}, u32[]{:S(2)}, u32[]{:S(2)}) collective-permute-start(bf16[896,128]{1,0:T(8,128)(2,1)} %get-tuple-element.46), channel_id=1, source_target_pairs={{0,4},{1,5},{2,6},{3,7},{4,0},{5,1},{6,2},{7,3},{8,12},{9,13},{10,... | collective-permute-start | bytes 688136 | tf_op jit(solution)/shard_map/ppermute | solution.py:41
  9.3 3.5 %collective-permute-start.1 = (bf16[896,128]{1,0:T(8,128)(2,1)}, bf16[896,128]{1,0:T(8,128)(2,1)S(1)}, u32[]{:S(2)}, u32[]{:S(2)}) collective-permute-start(bf16[896,128]{1,0:T(8,128)(2,1)} %get-tuple-element.47), channel_id=1, source_target_pairs={{4,8},{5,9},{6,10},{7,11},{8,4},{9,5},{10,6},{11,7},{12,16},{13,17... | collective-permute-start | bytes 688136 | tf_op jit(solution)/shard_map/ppermute | solution.py:41
  12.8 0.2 copy.35
  13.0 0.9 reshape.50.refs_5_
  13.9 2.9 %collective-permute-done.1.row_1.refs_1_ = bf16[896,128]{1,0:T(8,128)(2,1)S(1)} collective-permute-done((bf16[896,128]{1,0:T(8,128)(2,1)}, bf16[896,128]{1,0:T(8,128)(2,1)S(1)}, u32[]{:S(2)}, u32[]{:S(2)}) %collective-permute-start.1) | collective-permute-done | bytes 229408 | tf_op jit(solution)/shard_map/ppermute | solution.py:41
  16.8 0.7 copy-done.3
  17.5 2.2 %corners.1 = (bf16[352,128]{1,0:T(8,128)(2,1)}, bf16[352,128]{1,0:T(8,128)(2,1)}) custom-call(s32[2]{0:T(128)} %pad_add_fusion.parity, bf16[896,128]{1,0:T(8,128)(2,1)} %copy-done.2, bf16[896,128]{1,0:T(8,128)(2,1)} %copy-done.3, bf16[256,128]{1,0:T(8,128)(2,1)} %get-tuple-element.48.side_0, bf16[256,128]{1,0:T(8,128)(2,1)} %get-tuple-element.49.side_1), custom_call_target="tpu_custom_call" | custom-call | tf_op jit(solution)/shard_map/corners/pallas_call | solution.py:256
  19.7 1.4 %collective-permute-start.2 = (bf16[352,128]{1,0:T(8,128)(2,1)}, bf16[352,128]{1,0:T(8,128)(2,1)S(1)}, u32[]{:S(2)}, u32[]{:S(2)}) collective-permute-start(bf16[352,128]{1,0:T(8,128)(2,1)} %get-tuple-element.50), channel_id=1, source_target_pairs={{0,1},{1,0},{2,3},{3,2},{4,5},{5,4},{6,7},{7,6},{8,9},{9,8},{10,11... | collective-permute-start | bytes 270344 | tf_op jit(solution)/shard_map/ppermute | solution.py:41
  21.1 0.8 collective-permute-start.3
  22.0 0.7 reshape.51.refs_6_
  22.8 0.5 collective-permute-done.2.refs_2_
  23.3 0.6 copy-done.8
  24.0 16.0 %grads.1 = (bf16[3,816,192]{2,1,0:T(8,128)(2,1)}, bf16[1728,256]{1,0:T(8,128)(2,1)}, bf16[1632,384]{1,0:T(8,128)(2,1)}, bf16[3840,128]{1,0:T(8,128)(2,1)}, bf16[3840,128]{1,0:T(8,128)(2,1)}) custom-call(s32[2]{0:T(128)} %pad_add_fusion.parity, bf16[896,128]{1,0:T(8,128)(2,1)} %copy-done.2, bf16[896,128]{1,0:T(8,128)(2,1)} %copy-done.3, ...), custom_call_target="tpu_custom_call" | custom-call | tf_op jit(solution)/shard_map/grads/pallas_call | solution.py:603
  40.1 2.7 %collective-permute-done.4 = bf16[3840,128]{1,0:T(8,128)(2,1)S(1)} collective-permute-done((bf16[3840,128]{1,0:T(8,128)(2,1)}, bf16[3840,128]{1,0:T(8,128)(2,1)S(1)}, u32[]{:S(2)}, u32[]{:S(2)}) %collective-permute-start.4) | collective-permute-done | bytes 983072 | tf_op jit(solution)/shard_map/ppermute | solution.py:41
  42.9 1.5 %add_convert_fusion = bf16[3840,128]{1,0:T(8,128)(2,1)S(1)} fusion(bf16[3840,128]{1,0:T(8,128)(2,1)S(1)} %collective-permute-done.4, bf16[3840,128]{1,0:T(8,128)(2,1)} %get-tuple-element.56), kind=kLoop, calls=%fused_computation | loop fusion | flops 1966080 | bytes 2949120 | tf_op jit(solution)/shard_map/convert_element_type | solution.py:78
  44.4 6.1 %collective-permute-start.7 = (bf16[960,128]{1,0:T(8,128)(2,1)S(1)}, bf16[960,128]{1,0:T(8,128)(2,1)S(1)}, u32[]{:S(2)}, u32[]{:S(2)}) collective-permute-start(bf16[960,128]{1,0:T(8,128)(2,1)S(1)} %get-tuple-element.82), channel_id=1, source_target_pairs={{0,3},{1,2},{2,1},{3,0},{4,100},{5,101},{6,102},{7,103},{8,11},{9,... | collective-permute-start | bytes 737288 | tf_op jit(solution)/shard_map/ppermute | solution.py:41
  50.5 0.2 collective-permute-start.6
  50.7 0.4 collective-permute-start.5
  51.2 0.8 reshape.53.refs_2_
  52.0 4.0 %fine_input.1 = bf16[48,32,256]{2,1,0:T(8,128)(2,1)} custom-call(bf16[1536,256]{1,0:T(8,128)(2,1)} %get-tuple-element.55.refs_17_.refs_0_, bf16[1632,384]{1,0:T(8,128)(2,1)} %get-tuple-element.60.refs_1_, bf16[144,144]{1,0:T(8,128)(2,1)} %reshape.53.refs_2_), custom_call_target="tpu_custom_call" | custom-call | tf_op jit(solution)/shard_map/fine_input/pallas_call | solution.py:392
  56.0 0.3 collective-permute-done.7
  56.3 0.8 collective-permute-done.6
  57.0 0.4 collective-permute-done.5
  57.6 2.9 %collective-permute-start.10 = (bf16[240,128]{1,0:T(8,128)(2,1)S(1)}, bf16[240,128]{1,0:T(8,128)(2,1)S(1)}, u32[]{:S(2)}, u32[]{:S(2)}) collective-permute-start(bf16[240,128]{1,0:T(8,128)(2,1)S(1)} %get-tuple-element.85), channel_id=1, source_target_pairs={{0,96},{1,97},{2,98},{3,99},{4,28},{5,29},{6,30},{7,31},{8,104},{9... | collective-permute-start | bytes 184328 | tf_op jit(solution)/shard_map/ppermute | solution.py:41
  60.5 0.7 collective-permute-start.8
  61.2 0.9 collective-permute-done.10
  62.1 3.0 %collective-permute-done.9 = bf16[240,128]{1,0:T(8,128)(2,1)S(1)} collective-permute-done((bf16[240,128]{1,0:T(8,128)(2,1)S(1)}, bf16[240,128]{1,0:T(8,128)(2,1)S(1)}, u32[]{:S(2)}, u32[]{:S(2)}) %collective-permute-start.9) | collective-permute-done | bytes 61472 | tf_op jit(solution)/shard_map/ppermute | solution.py:41
  65.1 2.8 %collective-permute-start.13 = (bf16[240,128]{1,0:T(8,128)(2,1)S(1)}, bf16[240,128]{1,0:T(8,128)(2,1)S(1)}, u32[]{:S(2)}, u32[]{:S(2)}) collective-permute-start(bf16[240,128]{1,0:T(8,128)(2,1)S(1)} %fusion.3), channel_id=1, source_target_pairs={{0,24},{1,25},{2,26},{3,27},{4,7},{5,6},{6,5},{7,4},{8,16},{9,17},... | collective-permute-start | bytes 184328 | tf_op jit(solution)/shard_map/ppermute | solution.py:41
  67.9 3.1 %collective-permute-start.12 = (bf16[240,128]{1,0:T(8,128)(2,1)S(1)}, bf16[240,128]{1,0:T(8,128)(2,1)S(1)}, u32[]{:S(2)}, u32[]{:S(2)}) collective-permute-start(bf16[240,128]{1,0:T(8,128)(2,1)S(1)} %fusion.3), channel_id=1, source_target_pairs={{0,16},{1,17},{2,18},{3,19},{4,6},{5,7},{6,4},{7,5},{8,24},{9,25},... | collective-permute-start | bytes 184328 | tf_op jit(solution)/shard_map/ppermute | solution.py:41
  71.1 0.2 copy.38
  71.3 0.9 reshape.56.refs_2_
  72.1 0.5 collective-permute-done.12
  72.7 1.5 %collective-permute-done.11 = bf16[240,128]{1,0:T(8,128)(2,1)S(1)} collective-permute-done((bf16[240,128]{1,0:T(8,128)(2,1)S(1)}, bf16[240,128]{1,0:T(8,128)(2,1)S(1)}, u32[]{:S(2)}, u32[]{:S(2)}) %collective-permute-start.11) | collective-permute-done | bytes 61472 | tf_op jit(solution)/shard_map/ppermute | solution.py:41
  74.3 2.4 %collective-permute-start.15 = (bf16[240,128]{1,0:T(8,128)(2,1)S(1)}, bf16[240,128]{1,0:T(8,128)(2,1)S(1)}, u32[]{:S(2)}, u32[]{:S(2)}) collective-permute-start(bf16[240,128]{1,0:T(8,128)(2,1)S(1)} %add_convert_fusion.1), channel_id=1, source_target_pairs={{0,64},{1,65},{2,66},{3,67},{4,20},{5,21},{6,22},{7,23},{8,72},{9,... | collective-permute-start | bytes 184328 | tf_op jit(solution)/shard_map/ppermute | solution.py:41
  76.7 1.4 %collective-permute-start.16 = (bf16[240,128]{1,0:T(8,128)(2,1)S(1)}, bf16[240,128]{1,0:T(8,128)(2,1)S(1)}, u32[]{:S(2)}, u32[]{:S(2)}) collective-permute-start(bf16[240,128]{1,0:T(8,128)(2,1)S(1)} %add_convert_fusion.1), channel_id=1, source_target_pairs={{0,96},{1,97},{2,98},{3,99},{4,28},{5,29},{6,30},{7,31},{8,104},{9... | collective-permute-start | bytes 184328 | tf_op jit(solution)/shard_map/ppermute | solution.py:41
  78.2 3.6 %mid_input.1 = bf16[96,16,128]{2,1,0:T(8,128)(2,1)} custom-call(bf16[1536,128]{1,0:T(8,128)(2,1)} %get-tuple-element.54.refs_14_.refs_0_, bf16[1728,256]{1,0:T(8,128)(2,1)} %get-tuple-element.65.refs_1_, bf16[288,288]{1,0:T(8,128)(2,1)} %reshape.56.refs_2_), custom_call_target="tpu_custom_call" | custom-call | tf_op jit(solution)/shard_map/mid_input/pallas_call | solution.py:392
  81.8 1.3 %collective-permute-start.17 = (bf16[960,128]{1,0:T(8,128)(2,1)S(1)}, bf16[960,128]{1,0:T(8,128)(2,1)S(1)}, u32[]{:S(2)}, u32[]{:S(2)}) collective-permute-start(bf16[960,128]{1,0:T(8,128)(2,1)S(1)} %bitcast.64), channel_id=1, source_target_pairs={{0,1},{1,0},{2,3},{3,2},{4,36},{5,37},{6,38},{7,39},{8,9},{9,8},{1... | collective-permute-start | bytes 737288 | tf_op jit(solution)/shard_map/ppermute | solution.py:41
  83.1 1.8 %collective-permute-start.18 = (bf16[960,128]{1,0:T(8,128)(2,1)S(1)}, bf16[960,128]{1,0:T(8,128)(2,1)S(1)}, u32[]{:S(2)}, u32[]{:S(2)}) collective-permute-start(bf16[960,128]{1,0:T(8,128)(2,1)S(1)} %bitcast.65), channel_id=1, source_target_pairs={{0,2},{1,3},{2,0},{3,1},{4,68},{5,69},{6,70},{7,71},{8,10},{9,11},... | collective-permute-start | bytes 737288 | tf_op jit(solution)/shard_map/ppermute | solution.py:41
  85.0 0.8 collective-permute-start.19
  85.9 3.3 %coarse_input.1 = bf16[8,64,192]{2,1,0:T(8,128)(2,1)} custom-call(bf16[8,64,192]{2,1,0:T(8,128)(2,1)} %get-tuple-element.53.refs_11_.masked, bf16[3,816,192]{2,1,0:T(8,128)(2,1)} %get-tuple-element.70.px, bf16[3,3,192,192]{3,2,1,0:T(8,128)(2,1)} %first.1), custom_call_target="tpu_custom_call" | custom-call | tf_op jit(solution)/shard_map/coarse_input/pallas_call | solution.py:630
  89.2 1.9 %collective-permute-done.18 = bf16[960,128]{1,0:T(8,128)(2,1)S(1)} collective-permute-done((bf16[960,128]{1,0:T(8,128)(2,1)S(1)}, bf16[960,128]{1,0:T(8,128)(2,1)S(1)}, u32[]{:S(2)}, u32[]{:S(2)}) %collective-permute-start.18) | collective-permute-done | bytes 245792 | tf_op jit(solution)/shard_map/ppermute | solution.py:41
  91.2 2.5 %collective-permute-done.19 = bf16[960,128]{1,0:T(8,128)(2,1)S(1)} collective-permute-done((bf16[960,128]{1,0:T(8,128)(2,1)S(1)}, bf16[960,128]{1,0:T(8,128)(2,1)S(1)}, u32[]{:S(2)}, u32[]{:S(2)}) %collective-permute-start.19) | collective-permute-done | bytes 245792 | tf_op jit(solution)/shard_map/ppermute | solution.py:41
  93.8 7.4 %collective-permute-start.20 = (bf16[3840,128]{1,0:T(8,128)(2,1)S(1)}, bf16[3840,128]{1,0:T(8,128)(2,1)S(1)}, u32[]{:S(2)}, u32[]{:S(2)}) collective-permute-start(bf16[3840,128]{1,0:T(8,128)(2,1)S(1)} %bitcast.58), channel_id=1, source_target_pairs={{0,4},{1,5},{2,6},{3,7},{4,0},{5,1},{6,2},{7,3},{8,12},{9,13},{10,... | collective-permute-start | bytes 2949128 | tf_op jit(solution)/shard_map/ppermute | solution.py:41
  101.1 2.2 %collective-permute-done.20.other = bf16[3840,128]{1,0:T(8,128)(2,1)S(1)} collective-permute-done((bf16[3840,128]{1,0:T(8,128)(2,1)S(1)}, bf16[3840,128]{1,0:T(8,128)(2,1)S(1)}, u32[]{:S(2)}, u32[]{:S(2)}) %collective-permute-start.20) | collective-permute-done | bytes 983072 | tf_op jit(solution)/shard_map/ppermute | solution.py:41
  103.3 0.9 copy-done.1
  104.3 3.9 %unpack.1 = (f32[3,3,48,48]{3,2,1,0:T(8,128)}, f32[3,3,48,48]{3,2,1,0:T(8,128)}, f32[3,3,96,96]{3,2,1,0:T(8,128)}, f32[3,3,96,96]{3,2,1,0:T(8,128)}, f32[3,3,192...) custom-call(s32[2]{0:T(128)} %pad_add_fusion.parity, ...), custom_call_target="tpu_custom_call" | custom-call | tf_op jit(solution)/shard_map/unpack/pallas_call | solution.py:690
  (50 shorter events, 1.1 us)
Async XLA Ops:
  1.3 11.5 %copy-start.4 = (bf16[3,3,96,96]{3,2,1,0:T(8,128)(2,1)S(1)}, bf16[3,3,96,96]{3,2,1,0:T(8,128)(2,1)}, u32[]{:S(2)}) copy-start(bf16[3,3,96,96]{3,2,1,0:T(8,128)(2,1)} %param.34) | copy-start | bytes 497668
  7.7 14.2 %copy-start.6 = (bf16[3,3,48,48]{3,2,1,0:T(8,128)(2,1)S(1)}, bf16[3,3,48,48]{3,2,1,0:T(8,128)(2,1)}, u32[]{:S(2)}) copy-start(bf16[3,3,48,48]{3,2,1,0:T(8,128)(2,1)} %param.32) | copy-start | bytes 124420
  7.7 6.1 %collective-permute-start = (bf16[896,128]{1,0:T(8,128)(2,1)}, bf16[896,128]{1,0:T(8,128)(2,1)S(1)}, u32[]{:S(2)}, u32[]{:S(2)}) collective-permute-start(bf16[896,128]{1,0:T(8,128)(2,1)} %get-tuple-element.46), channel_id=1, source_target_pairs={{0,4},{1,5},{2,6},{3,7},{4,0},{5,1},{6,2},{7,3},{8,12},{9,13},{10,... | collective-permute-start | bytes 688136 | tf_op jit(solution)/shard_map/ppermute | solution.py:41
  9.3 7.5 %collective-permute-start.1 = (bf16[896,128]{1,0:T(8,128)(2,1)}, bf16[896,128]{1,0:T(8,128)(2,1)S(1)}, u32[]{:S(2)}, u32[]{:S(2)}) collective-permute-start(bf16[896,128]{1,0:T(8,128)(2,1)} %get-tuple-element.47), channel_id=1, source_target_pairs={{4,8},{5,9},{6,10},{7,11},{8,4},{9,5},{10,6},{11,7},{12,16},{13,17... | collective-permute-start | bytes 688136 | tf_op jit(solution)/shard_map/ppermute | solution.py:41
  13.9 2.9 %copy-start.2 = (bf16[896,128]{1,0:T(8,128)(2,1)}, bf16[896,128]{1,0:T(8,128)(2,1)S(1)}, u32[]{:S(2)}) copy-start(bf16[896,128]{1,0:T(8,128)(2,1)S(1)} %collective-permute-done.row_0.refs_0_) | copy-start | bytes 688132
  16.8 0.7 copy-start.3
  19.7 3.6 %collective-permute-start.2 = (bf16[352,128]{1,0:T(8,128)(2,1)}, bf16[352,128]{1,0:T(8,128)(2,1)S(1)}, u32[]{:S(2)}, u32[]{:S(2)}) collective-permute-start(bf16[352,128]{1,0:T(8,128)(2,1)} %get-tuple-element.50), channel_id=1, source_target_pairs={{0,1},{1,0},{2,3},{3,2},{4,5},{5,4},{6,7},{7,6},{8,9},{9,8},{10,11... | collective-permute-start | bytes 270344 | tf_op jit(solution)/shard_map/ppermute | solution.py:41
  21.1 2.2 %collective-permute-start.3 = (bf16[352,128]{1,0:T(8,128)(2,1)}, bf16[352,128]{1,0:T(8,128)(2,1)S(1)}, u32[]{:S(2)}, u32[]{:S(2)}) collective-permute-start(bf16[352,128]{1,0:T(8,128)(2,1)} %get-tuple-element.51), channel_id=1, source_target_pairs={{1,2},{2,1},{5,6},{6,5},{9,10},{10,9},{13,14},{14,13},{17,18},{18,... | collective-permute-start | bytes 270344 | tf_op jit(solution)/shard_map/ppermute | solution.py:41
  23.3 0.6 copy-start.8
  23.3 0.7 copy-start.9
  40.0 2.9 %collective-permute-start.4 = (bf16[3840,128]{1,0:T(8,128)(2,1)}, bf16[3840,128]{1,0:T(8,128)(2,1)S(1)}, u32[]{:S(2)}, u32[]{:S(2)}) collective-permute-start(bf16[3840,128]{1,0:T(8,128)(2,1)} %get-tuple-element.57), channel_id=1, source_target_pairs={{0,4},{1,5},{2,6},{3,7},{4,0},{5,1},{6,2},{7,3},{8,12},{9,13},{10,... | collective-permute-start | bytes 2949128 | tf_op jit(solution)/shard_map/ppermute | solution.py:41
  42.9 8.3 %copy-start.7 = (bf16[3,3,48,48]{3,2,1,0:T(8,128)(2,1)S(1)}, bf16[3,3,48,48]{3,2,1,0:T(8,128)(2,1)}, u32[]{:S(2)}) copy-start(bf16[3,3,48,48]{3,2,1,0:T(8,128)(2,1)} %param.31) | copy-start | bytes 124420
  44.4 11.8 %collective-permute-start.7 = (bf16[960,128]{1,0:T(8,128)(2,1)S(1)}, bf16[960,128]{1,0:T(8,128)(2,1)S(1)}, u32[]{:S(2)}, u32[]{:S(2)}) collective-permute-start(bf16[960,128]{1,0:T(8,128)(2,1)S(1)} %get-tuple-element.82), channel_id=1, source_target_pairs={{0,3},{1,2},{2,1},{3,0},{4,100},{5,101},{6,102},{7,103},{8,11},{9,... | collective-permute-start | bytes 737288 | tf_op jit(solution)/shard_map/ppermute | solution.py:41
  50.5 6.6 %collective-permute-start.6 = (bf16[960,128]{1,0:T(8,128)(2,1)S(1)}, bf16[960,128]{1,0:T(8,128)(2,1)S(1)}, u32[]{:S(2)}, u32[]{:S(2)}) collective-permute-start(bf16[960,128]{1,0:T(8,128)(2,1)S(1)} %get-tuple-element.83), channel_id=1, source_target_pairs={{0,2},{1,3},{2,0},{3,1},{4,68},{5,69},{6,70},{7,71},{8,10},{9,11},... | collective-permute-start | bytes 737288 | tf_op jit(solution)/shard_map/ppermute | solution.py:41
  50.7 6.7 %collective-permute-start.5 = (bf16[960,128]{1,0:T(8,128)(2,1)S(1)}, bf16[960,128]{1,0:T(8,128)(2,1)S(1)}, u32[]{:S(2)}, u32[]{:S(2)}) collective-permute-start(bf16[960,128]{1,0:T(8,128)(2,1)S(1)} %get-tuple-element.81), channel_id=1, source_target_pairs={{0,1},{1,0},{2,3},{3,2},{4,36},{5,37},{6,38},{7,39},{8,9},{9,8},{1... | collective-permute-start | bytes 737288 | tf_op jit(solution)/shard_map/ppermute | solution.py:41
  52.0 19.1 %copy-start.5 = (bf16[3,3,96,96]{3,2,1,0:T(8,128)(2,1)S(1)}, bf16[3,3,96,96]{3,2,1,0:T(8,128)(2,1)}, u32[]{:S(2)}) copy-start(bf16[3,3,96,96]{3,2,1,0:T(8,128)(2,1)} %param.33) | copy-start | bytes 497668
  57.6 4.5 %collective-permute-start.10 = (bf16[240,128]{1,0:T(8,128)(2,1)S(1)}, bf16[240,128]{1,0:T(8,128)(2,1)S(1)}, u32[]{:S(2)}, u32[]{:S(2)}) collective-permute-start(bf16[240,128]{1,0:T(8,128)(2,1)S(1)} %get-tuple-element.85), channel_id=1, source_target_pairs={{0,96},{1,97},{2,98},{3,99},{4,28},{5,29},{6,30},{7,31},{8,104},{9... | collective-permute-start | bytes 184328 | tf_op jit(solution)/shard_map/ppermute | solution.py:41
  60.5 4.6 %collective-permute-start.9 = (bf16[240,128]{1,0:T(8,128)(2,1)S(1)}, bf16[240,128]{1,0:T(8,128)(2,1)S(1)}, u32[]{:S(2)}, u32[]{:S(2)}) collective-permute-start(bf16[240,128]{1,0:T(8,128)(2,1)S(1)} %get-tuple-element.86), channel_id=1, source_target_pairs={{0,64},{1,65},{2,66},{3,67},{4,20},{5,21},{6,22},{7,23},{8,72},{9,... | collective-permute-start | bytes 184328 | tf_op jit(solution)/shard_map/ppermute | solution.py:41
  60.5 4.6 %collective-permute-start.8 = (bf16[240,128]{1,0:T(8,128)(2,1)S(1)}, bf16[240,128]{1,0:T(8,128)(2,1)S(1)}, u32[]{:S(2)}, u32[]{:S(2)}) collective-permute-start(bf16[240,128]{1,0:T(8,128)(2,1)S(1)} %get-tuple-element.84), channel_id=1, source_target_pairs={{0,32},{1,33},{2,34},{3,35},{4,12},{5,13},{6,14},{7,15},{8,40},{9,... | collective-permute-start | bytes 184328 | tf_op jit(solution)/shard_map/ppermute | solution.py:41
  65.1 7.0 %collective-permute-start.13 = (bf16[240,128]{1,0:T(8,128)(2,1)S(1)}, bf16[240,128]{1,0:T(8,128)(2,1)S(1)}, u32[]{:S(2)}, u32[]{:S(2)}) collective-permute-start(bf16[240,128]{1,0:T(8,128)(2,1)S(1)} %fusion.3), channel_id=1, source_target_pairs={{0,24},{1,25},{2,26},{3,27},{4,7},{5,6},{6,5},{7,4},{8,16},{9,17},... | collective-permute-start | bytes 184328 | tf_op jit(solution)/shard_map/ppermute | solution.py:41
  67.9 4.7 %collective-permute-start.12 = (bf16[240,128]{1,0:T(8,128)(2,1)S(1)}, bf16[240,128]{1,0:T(8,128)(2,1)S(1)}, u32[]{:S(2)}, u32[]{:S(2)}) collective-permute-start(bf16[240,128]{1,0:T(8,128)(2,1)S(1)} %fusion.3), channel_id=1, source_target_pairs={{0,16},{1,17},{2,18},{3,19},{4,6},{5,7},{6,4},{7,5},{8,24},{9,25},... | collective-permute-start | bytes 184328 | tf_op jit(solution)/shard_map/ppermute | solution.py:41
  71.1 3.1 %collective-permute-start.11 = (bf16[240,128]{1,0:T(8,128)(2,1)S(1)}, bf16[240,128]{1,0:T(8,128)(2,1)S(1)}, u32[]{:S(2)}, u32[]{:S(2)}) collective-permute-start(bf16[240,128]{1,0:T(8,128)(2,1)S(1)} %fusion.3), channel_id=1, source_target_pairs={{0,8},{1,9},{2,10},{3,11},{4,5},{5,4},{6,7},{7,6},{8,0},{9,1},{10,... | collective-permute-start | bytes 184328 | tf_op jit(solution)/shard_map/ppermute | solution.py:41
  74.2 7.6 %collective-permute-start.14 = (bf16[240,128]{1,0:T(8,128)(2,1)S(1)}, bf16[240,128]{1,0:T(8,128)(2,1)S(1)}, u32[]{:S(2)}, u32[]{:S(2)}) collective-permute-start(bf16[240,128]{1,0:T(8,128)(2,1)S(1)} %add_convert_fusion.1), channel_id=1, source_target_pairs={{0,32},{1,33},{2,34},{3,35},{4,12},{5,13},{6,14},{7,15},{8,40},{9,... | collective-permute-start | bytes 184328 | tf_op jit(solution)/shard_map/ppermute | solution.py:41
  74.3 7.5 %collective-permute-start.15 = (bf16[240,128]{1,0:T(8,128)(2,1)S(1)}, bf16[240,128]{1,0:T(8,128)(2,1)S(1)}, u32[]{:S(2)}, u32[]{:S(2)}) collective-permute-start(bf16[240,128]{1,0:T(8,128)(2,1)S(1)} %add_convert_fusion.1), channel_id=1, source_target_pairs={{0,64},{1,65},{2,66},{3,67},{4,20},{5,21},{6,22},{7,23},{8,72},{9,... | collective-permute-start | bytes 184328 | tf_op jit(solution)/shard_map/ppermute | solution.py:41
  76.7 5.1 %collective-permute-start.16 = (bf16[240,128]{1,0:T(8,128)(2,1)S(1)}, bf16[240,128]{1,0:T(8,128)(2,1)S(1)}, u32[]{:S(2)}, u32[]{:S(2)}) collective-permute-start(bf16[240,128]{1,0:T(8,128)(2,1)S(1)} %add_convert_fusion.1), channel_id=1, source_target_pairs={{0,96},{1,97},{2,98},{3,99},{4,28},{5,29},{6,30},{7,31},{8,104},{9... | collective-permute-start | bytes 184328 | tf_op jit(solution)/shard_map/ppermute | solution.py:41
  81.8 7.4 %collective-permute-start.17 = (bf16[960,128]{1,0:T(8,128)(2,1)S(1)}, bf16[960,128]{1,0:T(8,128)(2,1)S(1)}, u32[]{:S(2)}, u32[]{:S(2)}) collective-permute-start(bf16[960,128]{1,0:T(8,128)(2,1)S(1)} %bitcast.64), channel_id=1, source_target_pairs={{0,1},{1,0},{2,3},{3,2},{4,36},{5,37},{6,38},{7,39},{8,9},{9,8},{1... | collective-permute-start | bytes 737288 | tf_op jit(solution)/shard_map/ppermute | solution.py:41
  83.1 8.1 %collective-permute-start.18 = (bf16[960,128]{1,0:T(8,128)(2,1)S(1)}, bf16[960,128]{1,0:T(8,128)(2,1)S(1)}, u32[]{:S(2)}, u32[]{:S(2)}) collective-permute-start(bf16[960,128]{1,0:T(8,128)(2,1)S(1)} %bitcast.65), channel_id=1, source_target_pairs={{0,2},{1,3},{2,0},{3,1},{4,68},{5,69},{6,70},{7,71},{8,10},{9,11},... | collective-permute-start | bytes 737288 | tf_op jit(solution)/shard_map/ppermute | solution.py:41
  85.0 8.8 %collective-permute-start.19 = (bf16[960,128]{1,0:T(8,128)(2,1)S(1)}, bf16[960,128]{1,0:T(8,128)(2,1)S(1)}, u32[]{:S(2)}, u32[]{:S(2)}) collective-permute-start(bf16[960,128]{1,0:T(8,128)(2,1)S(1)} %bitcast.66), channel_id=1, source_target_pairs={{0,3},{1,2},{2,1},{3,0},{4,100},{5,101},{6,102},{7,103},{8,11},{9,... | collective-permute-start | bytes 737288 | tf_op jit(solution)/shard_map/ppermute | solution.py:41
  93.7 9.6 %copy-start = (bf16[4,960,128]{2,1,0:T(8,128)(2,1)}, bf16[4,960,128]{2,1,0:T(8,128)(2,1)S(1)}, u32[]{:S(2)}) copy-start(bf16[4,960,128]{2,1,0:T(8,128)(2,1)S(1)} %bitcast_dynamic-update-slice_fusion) | copy-start | bytes 2949124
  93.8 9.6 %collective-permute-start.20 = (bf16[3840,128]{1,0:T(8,128)(2,1)S(1)}, bf16[3840,128]{1,0:T(8,128)(2,1)S(1)}, u32[]{:S(2)}, u32[]{:S(2)}) collective-permute-start(bf16[3840,128]{1,0:T(8,128)(2,1)S(1)} %bitcast.58), channel_id=1, source_target_pairs={{0,4},{1,5},{2,6},{3,7},{4,0},{5,1},{6,2},{7,3},{8,12},{9,13},{10,... | collective-permute-start | bytes 2949128 | tf_op jit(solution)/shard_map/ppermute | solution.py:41
  103.3 0.9 copy-start.1

commit v3 on v2

--- a/solution.py
+++ b/solution.py
@@ -11,7 +11,7 @@
 FINE, MID = 48, 96
 COARSE_ROWS, COARSE_COLS, COARSE = 8, 64, 192
 PITCH = 80
-AT_MID, AT_FINE, AT_LIFT, SUM_ROWS = 5184, 6912, 7344, 7680
+AT_TAIL, AT_MID, AT_FINE, AT_LIFT, HALF_ROWS = 1728, 2592, 3456, 3744, 3840
 PARAMS = pltpu.CompilerParams(vmem_limit_bytes=56 * 2**20)
 
 AXES = ("row", "col")
@@ -73,7 +73,7 @@
     return lax.optimization_barrier((stage(block), work(*operands)))
 
 
-def all_sum(kept, given, works):
+def all_sum(kept, given, works, last_work):
     _, mine = my_place()
     part = (kept.astype(jnp.float32) + send(given, CORE_PAIRS).astype(jnp.float32)).astype(jnp.bfloat16)
     part, out_0 = beside(lambda x: scatter_stage(x, 0, mine[0]), part, *works[0])
@@ -81,7 +81,8 @@
     part = reduce_stage(part, 2)
     part, out_1 = beside(lambda x: gather_stage(x, 1, mine[1]), part, *works[1])
     part, out_2 = beside(lambda x: gather_stage(x, 0, mine[0]), part, *works[2])
-    return part, send(part, CORE_PAIRS), out_0, out_1, out_2
+    other, out_3 = beside(lambda x: send(x, CORE_PAIRS), part, last_work, part)
+    return other, out_3, out_0, out_1, out_2
 
 
 def partner(at, count, pairing):
@@ -122,41 +123,105 @@
     return jnp.where(gate > 0, value, jnp.zeros_like(value))
 
 
+def my_parity():
+    return lax.axis_index("row") % 2, lax.axis_index("col") % 2
+
+
 def prep_kernel(
-    parity, grad, joined, unit_fine, inner_fine, unit_mid, inner_mid, unit_coarse, inner_coarse, lift_mid, lift_coarse,
-    fine, mid, coarse, row_0, row_1, col_0, col_1, lift, upstream, gate_mid, in_fine, in_mid,
+    grad, joined, unit_fine, inner_fine, unit_mid, inner_mid, unit_coarse, inner_coarse, lift_mid, lift_coarse,
+    fine, mid, coarse, row_0, row_1, pooled_mid, pooled_coarse, upstream, gate_mid, in_fine, in_mid,
 ):
+    step = pl.program_id(0)
+    cells = CELLS // 2
     above = keep(joined[...], grad[...])
-    upstream[...] = jnp.transpose(above, (1, 0, 2)).reshape(CELLS, 256)
-    fine[...] = jnp.transpose(keep(unit_fine[...], above), (1, 0, 2)).reshape(CELLS, 256)
-    gate_mid[...] = jnp.transpose(unit_mid[...], (1, 0, 2)).reshape(CELLS, 128)
-    in_fine[...] = jnp.transpose(inner_fine[...], (1, 0, 2)).reshape(CELLS, 256)
-    in_mid[...] = jnp.transpose(inner_mid[...], (1, 0, 2)).reshape(CELLS, 128)
-
-    cells, target = iota((256, 192), 0), iota((256, 192), 1)
-    pooling = jnp.where(target < 128, cells // 2, cells // 4 + 128) == target
+    upstream[...] = jnp.transpose(above, (1, 0, 2)).reshape(cells, 256)
+    fine[...] = jnp.transpose(keep(unit_fine[...], above), (1, 0, 2)).reshape(cells, 256)
+    in_fine[...] = jnp.transpose(inner_fine[...], (1, 0, 2)).reshape(cells, 256)
+
+    @pl.when(step == 0)
+    def _():
+        gate_mid[...] = jnp.transpose(unit_mid[...], (1, 0, 2)).reshape(CELLS, 128)
+        in_mid[...] = jnp.transpose(inner_mid[...], (1, 0, 2)).reshape(CELLS, 128)
+
+    source, target = iota((256, 192), 0), iota((256, 192), 1)
+    pooling = jnp.where(target < 128, source // 2, source // 4 + 128) == target
     pooling = pooling.astype(jnp.float32).astype(jnp.bfloat16)
-    sum_mid = jnp.zeros((FINE, MID), jnp.float32)
-    sum_coarse = jnp.zeros((FINE, COARSE), jnp.float32)
-    for row in range(COARSE_ROWS):
+    for row in range(COARSE_ROWS // 2):
         pooled = dot(upstream[row * 192 : (row + 1) * 192, :], pooling)
         quarter = [pooled[k * FINE : (k + 1) * FINE] for k in range(4)]
         for half in range(2):
+            at = 2 * row + half
             cell = (quarter[2 * half] + quarter[2 * half + 1])[:, :128].astype(jnp.bfloat16)
-            rows = slice((2 * row + half) * MID, (2 * row + half + 1) * MID)
-            gate = gate_mid[rows, :]
-            mid[rows, :] = keep(gate, dot(lift_mid[...], cell, 0, 0).astype(jnp.bfloat16))
-            sum_mid += dot(cell, gate, 1, 1)
+            pooled_mid[at * FINE : (at + 1) * FINE, :] = cell
+            gate = gate_mid[pl.ds(pl.multiple_of(step * cells + at * MID, 16), MID), :]
+            mid[at * MID : (at + 1) * MID, :] = keep(gate, dot(lift_mid[...], cell, 0, 0).astype(jnp.bfloat16))
         cell = ((quarter[0] + quarter[1]) + (quarter[2] + quarter[3]))[:, 128:].astype(jnp.bfloat16)
-        gate = unit_coarse[row]
-        coarse[row] = keep(gate, dot(cell, lift_coarse[...], 0, 0).astype(jnp.bfloat16))
-        sum_coarse += dot(cell, gate)
-
-    lift[...] = jnp.zeros(lift.shape, lift.dtype)
-    lift[0:48, 0:96] = sum_mid.astype(jnp.bfloat16)
-    lift[48:96, 0:64] = sum_coarse[:, 128:].astype(jnp.bfloat16)
-    lift[96:144, :] = sum_coarse[:, :128].astype(jnp.bfloat16)
-
+        pooled_coarse[row * FINE : (row + 1) * FINE, :] = cell
+        coarse[row] = keep(unit_coarse[row], dot(cell, lift_coarse[...], 0, 0).astype(jnp.bfloat16))
+
+    row_parity, _ = my_parity()
+    for out, last in ((row_0, row_parity == 0), (row_1, row_parity == 1)):
+
+        @pl.when(step == last.astype(jnp.int32))
+        def _(out=out, last=last):
+            def rim_rows(size, whole=cells):
+                return pl.ds(pl.multiple_of(jnp.where(last, whole - size, 0), 16), size)
+
+            out[0:96, :] = fine[rim_rows(2 * FINE), 0:128]
+            out[96:192, :] = fine[rim_rows(2 * FINE), 128:256]
+            out[192:240, :] = in_fine[rim_rows(FINE), 0:128]
+            out[240:288, :] = in_fine[rim_rows(FINE), 128:256]
+            out[288:480, :] = mid[rim_rows(2 * MID), :]
+            out[480:576, :] = in_mid[rim_rows(MID, CELLS), :]
+            pair = coarse[pl.ds(jnp.where(last, 2, 0), 2)].reshape(128, COARSE)
+            out[576:704, :] = pair[:, :128]
+            single = inner_coarse[pl.ds(jnp.where(last, 3, 0), 1)].reshape(64, COARSE)
+            out[704:768, :] = single[:, :128]
+            out[768:896, :] = jnp.zeros((128, 128), jnp.bfloat16)
+            out[768:896, 0:64] = pair[:, 128:]
+            out[768:832, 64:128] = single[:, 128:]
+
+
+def prep(*args):
+    half = jnp.bfloat16
+    steps = [
+        ((CELLS, 256), (CELLS // 2, 256)),
+        ((CELLS, 128), (CELLS // 2, 128)),
+        ((COARSE_ROWS, COARSE_COLS, COARSE), (COARSE_ROWS // 2, COARSE_COLS, COARSE)),
+        ((896, 128), None),
+        ((896, 128), None),
+        ((16 * FINE, 128), (8 * FINE, 128)),
+        ((8 * FINE, 64), (4 * FINE, 64)),
+    ]
+
+    def whole(shape):
+        return pl.BlockSpec(shape, lambda i: (0,) * len(shape))
+
+    def leading(shape):
+        return pl.BlockSpec(shape, lambda i: (i,) + (0,) * (len(shape) - 1))
+
+    tall = pl.BlockSpec((FINE, 16, 256), lambda i: (0, i, 0))
+    wide = whole((MID, 16, 128))
+    deep = leading((COARSE_ROWS // 2, COARSE_COLS, COARSE))
+    return pl.pallas_call(
+        prep_kernel,
+        grid=(2,),
+        out_shape=[jax.ShapeDtypeStruct(shape, half) for shape, _ in steps],
+        in_specs=[tall] * 4 + [wide] * 2 + [deep] * 2 + [whole((FINE, MID)), whole((FINE, COARSE))],
+        out_specs=[leading(block) if block else whole(shape) for shape, block in steps],
+        scratch_shapes=[pltpu.VMEM(shape, half) for shape in ((CELLS // 2, 256), (CELLS, 128), (CELLS // 2, 256), (CELLS, 128))],
+        compiler_params=PARAMS,
+        name="prep",
+    )(*args)
+
+
+def side_kernel(
+    fine, mid, coarse, inner_fine, inner_mid, inner_coarse, unit_mid, unit_coarse, pooled_mid, pooled_coarse,
+    side_0, side_1, lift, in_fine, in_mid, gate_mid,
+):
+    in_fine[...] = jnp.transpose(inner_fine[...], (1, 0, 2)).reshape(CELLS, 256)
+    in_mid[...] = jnp.transpose(inner_mid[...], (1, 0, 2)).reshape(CELLS, 128)
+    gate_mid[...] = jnp.transpose(unit_mid[...], (1, 0, 2)).reshape(CELLS, 128)
     edges = (
         dot(picks((32, 256), ((0, 0), (1, 1), (16, 254), (17, 255))), fine[...], 1, 1)
         + dot(picks((32, 256), ((2, 0), (18, 255))), in_fine[...], 1, 1)
@@ -175,7 +240,8 @@
             second.astype(jnp.float32).astype(jnp.bfloat16), inner
         )
         sides.append((edges[side * 16 : (side + 1) * 16], rim.astype(jnp.bfloat16)))
-    for out, to_right in ((col_0, parity[1] == 0), (col_1, parity[1] == 1)):
+    _, col_parity = my_parity()
+    for out, to_right in ((side_0, col_parity == 0), (side_1, col_parity == 1)):
         edge = jnp.where(to_right, sides[1][0], sides[0][0])
         rim = jnp.where(to_right, sides[1][1], sides[0][1])
         for tile in range(12):
@@ -184,41 +250,49 @@
         out[224:256, :] = jnp.zeros((32, 128), jnp.bfloat16)
         out[224:256, 0:64] = rim[:, 128:]
 
-    for out, last in ((row_0, parity[0] == 0), (row_1, parity[0] == 1)):
-
-        def rim_rows(size):
-            return pl.ds(pl.multiple_of(jnp.where(last, CELLS - size, 0), 16), size)
-
-        out[0:96, :] = fine[rim_rows(2 * FINE), 0:128]
-        out[96:192, :] = fine[rim_rows(2 * FINE), 128:256]
-        out[192:240, :] = in_fine[rim_rows(FINE), 0:128]
-        out[240:288, :] = in_fine[rim_rows(FINE), 128:256]
-        out[288:480, :] = mid[rim_rows(2 * MID), :]
-        out[480:576, :] = in_mid[rim_rows(MID), :]
-        pair = coarse[pl.ds(jnp.where(last, 6, 0), 2)].reshape(128, COARSE)
-        out[576:704, :] = pair[:, :128]
-        single = inner_coarse[pl.ds(jnp.where(last, 7, 0), 1)].reshape(64, COARSE)
-        out[704:768, :] = single[:, :128]
-        out[768:896, :] = jnp.zeros((128, 128), jnp.bfloat16)
-        out[768:896, 0:64] = pair[:, 128:]
-        out[768:832, 64:128] = single[:, 128:]
-
-
-IN_SMEM = pl.BlockSpec(memory_space=pltpu.SMEM)
+    sum_mid = jnp.zeros((FINE, MID), jnp.float32)
+    for row in range(16):
+        sum_mid += dot(pooled_mid[row * FINE : (row + 1) * FINE, :], gate_mid[row * MID : (row + 1) * MID, :], 1, 1)
+    sum_coarse = jnp.zeros((FINE, COARSE), jnp.float32)
+    for row in range(COARSE_ROWS):
+        sum_coarse += dot(pooled_coarse[row * FINE : (row + 1) * FINE, :], unit_coarse[row])
+    lift[...] = jnp.zeros(lift.shape, lift.dtype)
+    lift[0:48, 0:96] = sum_mid.astype(jnp.bfloat16)
+    lift[48:96, 64:128] = sum_coarse[:, 128:].astype(jnp.bfloat16)
+    lift[96:144, :] = sum_coarse[:, :128].astype(jnp.bfloat16)
+
+
+def side(*args):
+    half = jnp.bfloat16
+    return pl.pallas_call(
+        side_kernel,
+        out_shape=[jax.ShapeDtypeStruct(shape, half) for shape in ((256, 128), (256, 128), (144, 128))],
+        scratch_shapes=[pltpu.VMEM((CELLS, width), half) for width in (256, 128, 128)],
+        compiler_params=PARAMS,
+        name="side",
+    )(*args)
+
+
 IN_VMEM = pl.BlockSpec(memory_space=pltpu.VMEM)
 
 
+def near(*arrays):
+    return [pltpu.with_memory_space_constraint(array, pltpu.VMEM) for array in arrays]
+
+
 class Halo:
-    def __init__(self, parity, row_0, row_1, col_0, col_1):
-        row_even, col_even = parity[0] == 0, parity[1] == 0
+    def __init__(self, row_0, row_1, col_0, col_1):
+        row_parity, col_parity = my_parity()
+        row_even, col_even = row_parity == 0, col_parity == 0
         rows, cols = (row_0[...], row_1[...]), (col_0[...], col_1[...])
         self.top, self.bottom = jnp.where(row_even, rows[1], rows[0]), jnp.where(row_even, rows[0], rows[1])
         self.left, self.right = jnp.where(col_even, cols[1], cols[0]), jnp.where(col_even, cols[0], cols[1])
 
 
-def corner_kernel(parity, row_0, row_1, side_0, side_1, col_0, col_1):
+def corner_kernel(row_0, row_1, side_0, side_1, col_0, col_1):
     half = jnp.bfloat16
-    row_even = parity[0] == 0
+    row_parity, col_parity = my_parity()
+    row_even = row_parity == 0
     halos = (jnp.where(row_even, row_1[...], row_0[...]), jnp.where(row_even, row_0[...], row_1[...]))
     wide = jnp.concatenate(
         [
@@ -247,35 +321,20 @@
         rim = dot(picks((16, 384), pairs), wide).astype(half)
         parts += [rim[:, :128], jnp.concatenate([rim[:, 128:], jnp.zeros((16, 64), half)], axis=1)]
         sides.append(jnp.concatenate(parts, axis=0))
-    for out, side, to_right in ((col_0, side_0, parity[1] == 0), (col_1, side_1, parity[1] == 1)):
+    for out, side, to_right in ((col_0, side_0, col_parity == 0), (col_1, side_1, col_parity == 1)):
         out[0:256, :] = side[...]
         out[256:352, :] = jnp.where(to_right, sides[1], sides[0])
 
 
-def corners(parity, *messages):
+def corners(*messages):
     return pl.pallas_call(
         corner_kernel,
-        out_shape=[jax.ShapeDtypeStruct((352, 128), jnp.bfloat16)] * 2,
-        in_specs=[IN_SMEM] + [IN_VMEM] * 4,
+        out_shape=[pltpu.VMEM((352, 128), jnp.bfloat16)] * 2,
+        out_specs=[IN_VMEM] * 2,
+        in_specs=[IN_VMEM] * 4,
         compiler_params=PARAMS,
         name="corners",
-    )(parity, *messages)
-
-
-def prep(*args):
-    half = jnp.bfloat16
-    shapes = (
-        (CELLS, 256), (CELLS, 128), (COARSE_ROWS, COARSE_COLS, COARSE),
-        (896, 128), (896, 128), (256, 128), (256, 128), (144, 128),
-    )
-    return pl.pallas_call(
-        prep_kernel,
-        out_shape=[jax.ShapeDtypeStruct(shape, half) for shape in shapes],
-        in_specs=[IN_SMEM] + [IN_VMEM] * 10,
-        scratch_shapes=[pltpu.VMEM((CELLS, width), half) for width in (256, 128, 256, 128)],
-        compiler_params=PARAMS,
-        name="prep",
-    )(*args)
+    )(*near(*messages[:2]), *messages[2:])
 
 
 def channel_part(halo, second, refs, write_px, *, chans, rows, width, edge, fill_rows):
@@ -364,21 +423,24 @@
     ix[inner_at : inner_at + 96, 0:128] = halo[480:576, :]
 
 
-def fine_grads(grads, acc_first, acc_second):
-    for tap in range(3):
-        cols = slice((2 - tap) * FINE, (3 - tap) * FINE)
-        pair = jnp.concatenate([acc_second[:, cols], acc_first[:, cols], jnp.zeros((144, 32), jnp.float32)], axis=1)
-        grads[tap * 144 : (tap + 1) * 144, :] = pair.astype(jnp.bfloat16)
-
-
-def mid_grads(grads, acc_first, acc_second):
+def fine_grads(sums, acc_first, acc_second, lift):
+    full, half = jnp.float32, jnp.bfloat16
+    for index, acc in enumerate((acc_second, acc_first)):
+        taps = [acc[:, (2 - tap) * FINE : (3 - tap) * FINE] for tap in range(3)]
+        gap = jnp.zeros((144, 16), full)
+        sums[index, 0:144, :] = jnp.concatenate([taps[0], gap, taps[1], gap], axis=1).astype(half)
+        sums[index, 144:288, :] = jnp.concatenate([taps[2], jnp.zeros((144, 80), full)], axis=1).astype(half)
+        sums[index, 288:384, :] = jnp.zeros((96, 128), half)
+    sums[0, 288:336, :] = lift[0:48, :]
+    sums[1, 288:336, :] = lift[96:144, :]
+    sums[1, 144:192, 64:128] = lift[48:96, 64:128]
+
+
+def mid_grads(sums, acc_first, acc_second):
     for index, acc in enumerate((acc_second, acc_first)):
         for tap in range(3):
-            part = jnp.concatenate(
-                [acc[:, (2 - tap) * MID : (3 - tap) * MID], jnp.zeros((288, 32), jnp.float32)], axis=1
-            )
-            at = (3 * index + tap) * 288
-            grads[at : at + 288, :] = part.astype(jnp.bfloat16)
+            part = jnp.concatenate([acc[:, (2 - tap) * MID : (3 - tap) * MID], jnp.zeros((288, 32), jnp.float32)], axis=1)
+            sums[index, tap * 288 : (tap + 1) * 288, :] = part.astype(jnp.bfloat16)
 
 
 def stacked(weight, chans):
@@ -425,7 +487,7 @@
 
 
 def coarse_part(halo, second, place, refs, write_px):
-    source, inner, masked, grads, px, mx, ix, own, turned, tail = refs
+    source, inner, masked, sums, px, mx, ix, own, turned = refs
     half = jnp.bfloat16
     lead = 16
     rims = jnp.concatenate(
@@ -474,30 +536,26 @@
                 at = start + (2 - row_tap) * PITCH
                 write(row_tap * 3 + col_tap, dot(turned[...], ref[col_tap, at : at + 8 * PITCH, :]))
 
-    def write_second(tap, value):
-        grads[tap * COARSE : (tap + 1) * COARSE, :] = value[:, :128].astype(half)
-        tail[tap * COARSE : (tap + 1) * COARSE, :] = value[:, 128:].astype(half)
-
-    def write_first(tap, value):
-        at = 1728 + tap * COARSE
-        grads[at : at + COARSE, :] = value[:, :128].astype(half)
-        rows = slice(3456 + tap * COARSE, 3456 + (tap + 1) * COARSE)
-        grads[rows, :] = jnp.concatenate(
-            [tail[tap * COARSE : (tap + 1) * COARSE, :], value[:, 128:].astype(half)], axis=1
-        )
-
-    corr(inner, mx, lead + PITCH, write_second)
-    corr(source, px, lead, write_first)
-
-
-def grads_kernel(parity, *refs):
+    def writer(index):
+        def write(tap, value):
+            sums[index, tap * COARSE : (tap + 1) * COARSE, :] = value[:, :128].astype(half)
+            tail = jnp.concatenate([value[:96, 128:], value[96:, 128:]], axis=1)
+            sums[index, AT_TAIL + tap * 96 : AT_TAIL + (tap + 1) * 96, :] = tail.astype(half)
+
+        return write
+
+    corr(inner, mx, lead + PITCH, writer(0))
+    corr(source, px, lead, writer(1))
+
+
+def grads_kernel(*refs):
     messages, (second_coarse, second_mid, second_fine, place, lift), refs = refs[:4], refs[4:9], refs[9:]
     arrays, (px_coarse, px_mid, px_fine, kept, given), refs = refs[:9], refs[9:14], refs[14:]
-    held, work, (load_sems, px_sems, sum_sems) = refs[:7], refs[7:28], refs[28:]
-    coarse_work, mid_work, fine_work = work[:7], work[7:14], work[14:21]
+    held, work, (load_sems, px_sems, sum_sems) = refs[:7], refs[7:27], refs[27:]
+    coarse_work, mid_work, fine_work = work[:6], work[6:13], work[13:20]
     sum_coarse, sum_mid, sum_fine = coarse_work[0], mid_work[0], fine_work[0]
     mx_mid, mx_fine = mid_work[2], fine_work[2]
-    core = parity[0]
+    core, _ = my_parity()
 
     places = (
         *held[:3],
@@ -507,43 +565,37 @@
     loads = [pltpu.make_async_copy(array, to, load_sems.at[k]) for k, (array, to) in enumerate(zip(arrays, places))]
     for load in loads:
         load.start()
-    halo = Halo(parity, *messages)
+    halo = Halo(*messages)
 
     px_copies = [
         pltpu.make_async_copy(work[1], out, px_sems.at[k])
         for k, (work, out) in enumerate(((coarse_work, px_coarse), (mid_work, px_mid), (fine_work, px_fine)))
     ]
-    half_rows = SUM_ROWS // 2
-
-    def sum_copies(k, source, at, size):
-        start = at % half_rows
-        return [pltpu.make_async_copy(source, out.at[start : start + size, :], sum_sems.at[k]) for out in (kept, given)]
-
-    def write(copies, at):
-        keeps = core == at // half_rows
-
-        @pl.when(keeps)
-        def _():
-            copies[0].start()
-
-        @pl.when(jnp.logical_not(keeps))
-        def _():
-            copies[1].start()
-
-    rest = AT_MID - half_rows
-    pieces = (
-        (sum_coarse.at[0:half_rows, :], 0, half_rows),
-        (sum_coarse.at[half_rows:AT_MID, :], half_rows, rest),
-        (sum_mid, AT_MID, AT_FINE - AT_MID),
-        (sum_fine, AT_FINE, SUM_ROWS - AT_FINE),
-    )
-    sums = [sum_copies(k, *piece) for k, piece in enumerate(pieces)]
+    def sum_copies(work, start, size, k):
+        return [
+            [pltpu.make_async_copy(work.at[half], out.at[start : start + size, :], sum_sems.at[2 * k + half]) for out in (kept, given)]
+            for half in range(2)
+        ]
+
+    def write(copies):
+        for half in range(2):
+            keeps = core == half
+
+            @pl.when(keeps)
+            def _(half=half):
+                copies[half][0].start()
+
+            @pl.when(jnp.logical_not(keeps))
+            def _(half=half):
+                copies[half][1].start()
+
+    pieces = ((sum_coarse, 0, AT_MID), (sum_mid, AT_MID, AT_FINE - AT_MID), (sum_fine, AT_FINE, HALF_ROWS - AT_FINE))
+    sums = [sum_copies(*piece, k) for k, piece in enumerate(pieces)]
 
     for load in loads[:3]:
         load.wait()
     coarse_part(halo, second_coarse, place, (*held[:3], *coarse_work), px_copies[0].start)
-    write(sums[0], pieces[0][1])
-    write(sums[1], pieces[1][1])
+    write(sums[0])
 
     for load in loads[3:6]:
         load.wait()
@@ -552,7 +604,7 @@
         chans=MID, rows=16, width=128, edge=3, fill_rows=mid_rows,
     )
     mid_grads(sum_mid, mid_work[5], mid_work[6])
-    write(sums[2], pieces[2][1])
+    write(sums[1])
 
     for load in loads[6:]:
         load.wait()
@@ -560,18 +612,17 @@
         halo, second_fine, (held[5], held[6], *fine_work[1:]), px_copies[2].start,
         chans=FINE, rows=32, width=256, edge=0, fill_rows=fine_rows,
     )
-    fine_grads(sum_fine, fine_work[5], fine_work[6])
-    sum_fine[432:576, :] = lift[...]
-    sum_fine[576:, :] = jnp.zeros((SUM_ROWS - AT_LIFT - 144, 128), jnp.bfloat16)
-    write(sums[3], pieces[3][1])
+    fine_grads(sum_fine, fine_work[5], fine_work[6], lift)
+    write(sums[2])
 
     for copy in px_copies:
         copy.wait()
-    for copies in sums:
-        copies[0].wait()
-
-
-def grads(parity, messages, seconds, lift, arrays):
+    for halves in sums:
+        for copies in halves:
+            copies[0].wait()
+
+
+def grads(messages, seconds, lift, arrays):
     half = jnp.bfloat16
     any_memory = pl.BlockSpec(memory_space=pl.ANY)
     full = jnp.float32
@@ -579,7 +630,7 @@
     def channel_work(chans, rows, width, sum_rows):
         ring = width + 128
         return [
-            ((sum_rows, 128), half),
+            ((2, sum_rows, 128), half),
             (((rows + 2) * chans, ring), half),
             (((rows + 4) * chans, ring), half),
             (((rows + 2) * chans, ring), half),
@@ -591,31 +642,30 @@
     tile = ((COARSE_ROWS, COARSE_COLS, COARSE), half)
     held = [tile, tile, tile] + [((MID, 16, 128), half)] * 2 + [((FINE, 32, 256), half)] * 2
     coarse_work = [
-        ((AT_MID, 128), half),
+        ((2, AT_MID, 128), half),
         ((3, 816, COARSE), half),
         ((3, 976, COARSE), half),
         ((816, COARSE), half),
         ((8 * PITCH, COARSE), half),
         ((COARSE, 8 * PITCH), half),
-        ((1728, 64), half),
     ]
-    scratch = held + coarse_work + channel_work(MID, 16, 128, AT_FINE - AT_MID) + channel_work(FINE, 32, 256, SUM_ROWS - AT_FINE)
+    scratch = held + coarse_work + channel_work(MID, 16, 128, AT_FINE - AT_MID) + channel_work(FINE, 32, 256, HALF_ROWS - AT_FINE)
     return pl.pallas_call(
         grads_kernel,
         out_shape=[
             jax.ShapeDtypeStruct((3, 816, COARSE), half),
             jax.ShapeDtypeStruct((18 * MID, 256), half),
             jax.ShapeDtypeStruct((34 * FINE, 384), half),
-            jax.ShapeDtypeStruct((SUM_ROWS // 2, 128), half),
-            jax.ShapeDtypeStruct((SUM_ROWS // 2, 128), half),
+            jax.ShapeDtypeStruct((HALF_ROWS, 128), half),
+            pltpu.VMEM((HALF_ROWS, 128), half),
         ],
-        in_specs=[IN_SMEM] + [IN_VMEM] * 9 + [any_memory] * 9,
-        out_specs=[any_memory] * 5,
+        in_specs=[IN_VMEM] * 9 + [any_memory] * 9,
+        out_specs=[any_memory] * 4 + [IN_VMEM],
         scratch_shapes=[pltpu.VMEM(*shape) for shape in scratch]
-        + [pltpu.SemaphoreType.DMA((9,)), pltpu.SemaphoreType.DMA((3,)), pltpu.SemaphoreType.DMA((4,))],
+        + [pltpu.SemaphoreType.DMA((9,)), pltpu.SemaphoreType.DMA((3,)), pltpu.SemaphoreType.DMA((6,))],
         compiler_params=PARAMS,
         name="grads",
-    )(parity, *messages, *seconds, jnp.asarray(coarse_places(), half), lift, *arrays)
+    )(*near(*messages), *seconds, jnp.asarray(coarse_places(), half), lift, *arrays)
 
 
 def coarse_input_kernel(masked, px, first, out):
@@ -635,68 +685,83 @@
     )(masked, px, first)
 
 
-def unpack_kernel(parity, kept, other, *refs):
-    outs, tiles, sems = refs[:8], refs[8:16], refs[16]
-    mine, theirs = kept[...], other[...]
-    first_half = parity[0] == 0
-    halves = (jnp.where(first_half, mine, theirs), jnp.where(first_half, theirs, mine))
-    first_fine, second_fine, first_mid, second_mid, first_coarse, second_coarse, lift_mid, lift_coarse = tiles
-
-    def part(start, size, lanes=slice(0, 128)):
-        at = start % 3840
-        return halves[start // 3840][at : at + size, lanes].astype(jnp.float32)
-
+def unpack_kernel(summed, *refs, kept):
+    outs, (coarse, mid, fine, lift_mid, lift_coarse, sems) = refs[-14:-6], refs[-6:]
+    core, _ = my_parity()
+    is_second = core == (0 if kept else 1)
+    full = jnp.float32
     copies = []
 
-    def leave(tile, out):
-        copy = pltpu.make_async_copy(tile, out, sems.at[len(copies)])
-        copy.start()
-        copies.append(copy)
+    def leave(tile, first_out, second_out):
+        k = len(copies)
+        copies.append(pltpu.make_async_copy(tile, second_out, sems.at[k]))
+        other = pltpu.make_async_copy(tile, first_out, sems.at[k])
+
+        @pl.when(is_second)
+        def _():
+            copies[k].start()
+
+        @pl.when(jnp.logical_not(is_second))
+        def _():
+            other.start()
 
     for tap in range(9):
         row_tap, col_tap = tap // 3, tap % 3
-        tails = part(3456 + tap * COARSE, COARSE)
-        second_coarse[row_tap, col_tap, :, 0:128] = part(tap * COARSE, COARSE)
-        second_coarse[row_tap, col_tap, :, 128:192] = tails[:, :64]
-        first_coarse[row_tap, col_tap, :, 0:128] = part(1728 + tap * COARSE, COARSE)
-        first_coarse[row_tap, col_tap, :, 128:192] = tails[:, 64:]
+        coarse[row_tap, col_tap, :, 0:128] = summed[tap * COARSE : (tap + 1) * COARSE, :].astype(full)
+        tail = summed[AT_TAIL + tap * 96 : AT_TAIL + (tap + 1) * 96, :].astype(full)
+        coarse[row_tap, col_tap, 0:96, 128:192] = tail[:, :64]
+        coarse[row_tap, col_tap, 96:192, 128:192] = tail[:, 64:]
         if col_tap == 2:
-            leave(second_coarse.at[row_tap], outs[5].at[row_tap])
-            leave(first_coarse.at[row_tap], outs[4].at[row_tap])
+            leave(coarse.at[row_tap], outs[4].at[row_tap], outs[5].at[row_tap])
     for tap in range(9):
-        row_tap, col_tap = tap // 3, tap % 3
-        second_mid[row_tap, col_tap] = part(AT_MID + tap * MID, MID, slice(0, 96))
-        first_mid[row_tap, col_tap] = part(AT_MID + 864 + tap * MID, MID, slice(0, 96))
-    leave(second_mid, outs[3])
-    leave(first_mid, outs[2])
-    for tap in range(9):
-        row_tap, col_tap = tap // 3, tap % 3
-        pair = part(AT_FINE + tap * FINE, FINE)
-        second_fine[row_tap, col_tap] = pair[:, 0:48]
-        first_fine[row_tap, col_tap] = pair[:, 48:96]
-    leave(second_fine, outs[1])
-    leave(first_fine, outs[0])
-    lift_mid[...] = part(AT_LIFT, 48, slice(0, 96))
-    lift_coarse[:, 0:128] = part(AT_LIFT + 96, 48)
-    lift_coarse[:, 128:192] = part(AT_LIFT + 48, 48, slice(0, 64))
-    leave(lift_mid, outs[6])
-    leave(lift_coarse, outs[7])
+        mid[tap // 3, tap % 3] = summed[AT_MID + tap * MID : AT_MID + (tap + 1) * MID, 0:96].astype(full)
+    leave(mid, outs[2], outs[3])
+    for col_tap in range(3):
+        rows = slice(AT_FINE + col_tap * FINE, AT_FINE + (col_tap + 1) * FINE)
+        pair = summed[rows, :].astype(full)
+        fine[0, col_tap] = pair[:, 0:48]
+        fine[1, col_tap] = pair[:, 64:112]
+        rows = slice(AT_FINE + 144 + col_tap * FINE, AT_FINE + 144 + (col_tap + 1) * FINE)
+        fine[2, col_tap] = summed[rows, 0:48].astype(full)
+    leave(fine, outs[0], outs[1])
+    lift_mid[...] = summed[AT_LIFT : AT_LIFT + 48, 0:96].astype(full)
+    lift_coarse[:, 0:128] = summed[AT_LIFT : AT_LIFT + 48, :].astype(full)
+    lift_coarse[:, 128:192] = summed[AT_FINE + 144 : AT_FINE + 192, 64:128].astype(full)
+    lift_copies = [
+        pltpu.make_async_copy(tile, out, sems.at[len(copies)]) for tile, out in ((lift_mid, outs[6]), (lift_coarse, outs[7]))
+    ]
+
+    @pl.when(is_second)
+    def _():
+        lift_copies[0].start()
+        lift_copies[0].wait()
+
+    @pl.when(jnp.logical_not(is_second))
+    def _():
+        lift_copies[1].start()
+        lift_copies[1].wait()
+
     for copy in copies:
         copy.wait()
 
 
-def unpack(parity, kept, other):
+def unpack(summed, earlier=()):
     shapes = ((3, 3, 48, 48),) * 2 + ((3, 3, 96, 96),) * 2 + ((3, 3, 192, 192),) * 2 + ((48, 96), (48, 192))
-    *taps, lift_mid, lift_coarse = pl.pallas_call(
-        unpack_kernel,
+    any_memory = pl.BlockSpec(memory_space=pl.ANY)
+
+    def kernel(*refs):
+        unpack_kernel(*refs, kept=not earlier)
+
+    return pl.pallas_call(
+        kernel,
         out_shape=[jax.ShapeDtypeStruct(shape, jnp.float32) for shape in shapes],
-        in_specs=[IN_SMEM, IN_VMEM, IN_VMEM],
-        out_specs=[pl.BlockSpec(memory_space=pl.ANY)] * 8,
-        scratch_shapes=[pltpu.VMEM(shape, jnp.float32) for shape in shapes] + [pltpu.SemaphoreType.DMA((12,))],
+        in_specs=[IN_VMEM] + [any_memory] * len(earlier),
+        out_specs=[any_memory] * 8,
+        scratch_shapes=[pltpu.VMEM(shapes[k], jnp.float32) for k in (4, 2, 0, 6, 7)] + [pltpu.SemaphoreType.DMA((6,))],
+        input_output_aliases={k + 1: k for k in range(len(earlier))},
         compiler_params=PARAMS,
-        name="unpack",
-    )(parity, kept, other)
-    return *taps, jnp.transpose(lift_mid), jnp.transpose(lift_coarse)
+        name="unpack_other" if earlier else "unpack_kept",
+    )(*near(summed), *earlier)
 
 
 def on_device(
@@ -707,22 +772,23 @@
     input_coarse, inner_coarse, unit_coarse = (
         jnp.transpose(x, (1, 2, 0)) for x in (input_coarse, inner_coarse, unit_coarse)
     )
-    parity = jnp.stack([lax.axis_index("row") % 2, lax.axis_index("col") % 2]).astype(jnp.int32)
-    fine, mid, coarse, row_0, row_1, col_0, col_1, lift = prep(
-        parity, grad_joined, joined_fine, unit_fine, inner_fine, unit_mid, inner_mid, unit_coarse, inner_coarse,
+    fine, mid, coarse, row_0, row_1, pooled_mid, pooled_coarse = prep(
+        grad_joined, joined_fine, unit_fine, inner_fine, unit_mid, inner_mid, unit_coarse, inner_coarse,
         jnp.transpose(lift_mid), jnp.transpose(lift_coarse),
     )
     row_0, row_1 = send(row_0, swap_pairs(0, None)), send(row_1, swap_pairs(1, None))
-    col_0, col_1 = corners(parity, row_0, row_1, col_0, col_1)
+    side_0, side_1, lift = side(
+        fine, mid, coarse, inner_fine, inner_mid, inner_coarse, unit_mid, unit_coarse, pooled_mid, pooled_coarse
+    )
+    col_0, col_1 = corners(row_0, row_1, side_0, side_1)
     col_0, col_1 = send(col_0, swap_pairs(None, 0)), send(col_1, swap_pairs(None, 1))
     coarse_px, mid_px, fine_px, kept, given = grads(
-        parity,
         (row_0, row_1, col_0, col_1),
         (second_coarse, stacked(second_mid, MID), stacked(second_fine, FINE)),
         lift,
         (input_coarse, inner_coarse, coarse, input_mid, inner_mid, mid, input_fine, inner_fine, fine),
     )
-    kept, other, fine_input, mid_input, input_grad = all_sum(
+    other, earlier, fine_input, mid_input, input_grad = all_sum(
         kept,
         given,
         (
@@ -730,8 +796,12 @@
             (lambda px: channel_input(mid, px, first_mid, MID, 16, 128, "mid_input"), mid_px),
             (lambda px: coarse_input(coarse, px, first_coarse), coarse_px),
         ),
-    )
-    return (fine_input, mid_input, jnp.transpose(input_grad, (2, 0, 1)), *unpack(parity, kept, other))
+        unpack,
+    )
+    *taps, lift_mid, lift_coarse = unpack(other, earlier)
+    return (
+        fine_input, mid_input, jnp.transpose(input_grad, (2, 0, 1)), *taps, jnp.transpose(lift_mid), jnp.transpose(lift_coarse)
+    )
 
 
 def solution(mesh):

time: 109 us -> 101 us (0.927)
  waiting for transfers between devices: 20.1 us -> 14.1 us
  local copies, waits for them, and re-layouts: 6.5 us -> 4.23 us
  Pallas kernels: 39.4 us -> 41.1 us
    ppermute x21, waiting for transfers between devices: 20.1 us -> 14.1 us  [send(): return lax.ppermute(block, AXES, pairs)]
    unnamed x20 -> x8, local copies, waits for them, and re-layouts: 2.31 us -> 0.02 us
    pallas_call x3 -> x5, Pallas kernels: 12.6 us -> 13.9 us  [the longest x1 5.34 us: prep(): pl.pallas_call(prep_kernel, grid=(2,), out_shape=[jax.ShapeDtypeStruct(sh...]
  transfers between devices with their start and end apart: 21 -> 21, of which waited for: 13 -> 9; matrix products, arithmetic and copies ran while one was open for 4% -> 4% of each run, Pallas kernels for 10% -> 16%
where the time goes in v3:
time: 101 us; the launch traced here: 100 us
  Pallas kernels  41.1 us (41%)
  starting transfers between devices  38.1 us (38%)
  waiting for transfers between devices  14.1 us (14%)
  local copies, waits for them, and re-layouts  4.23 us (4%)
  other arithmetic  1.7 us (2%)
  between operations  1.14 us (1%)
    ppermute x21, starting transfers between devices, send(): return lax.ppermute(block, AXES, pairs)  38.1 us
    pallas_call x1, Pallas kernels, grads(): pl.pallas_call(grads_kernel, out_shape=[jax.ShapeDtypeStruct((3, 816, COA...  16.4 us
    ppermute x21, waiting for transfers between devices, send(): return lax.ppermute(block, AXES, pairs)  14.1 us
    pallas_call x2, Pallas kernels, channel_input(): pl.pallas_call(kernel, out_shape=jax.ShapeDtypeStruct((chans, rows, width...  7.55 us
    pallas_call x1, Pallas kernels, prep(): pl.pallas_call(prep_kernel, grid=(2,), out_shape=[jax.ShapeDtypeStruct(sh...  5.34 us
    pallas_call x1, Pallas kernels, side(): pl.pallas_call(side_kernel, out_shape=[jax.ShapeDtypeStruct(shape, half)...  4.02 us
    reshape x4, local copies, waits for them, and re-layouts, stacked(): jnp.transpose(weight[::-1], (1, 2, 0, 3)).reshape(3 * chans, 3 * chans)  3.28 us
    pallas_call x1, Pallas kernels, coarse_input(): pl.pallas_call(coarse_input_kernel, out_shape=jax.ShapeDtypeStruct((COARS...  3.28 us
  transfers between devices with their start and end apart: 21, of which 9 were waited for; matrix products, arithmetic and copies ran while one was open for 4% of the time, Pallas kernels for 16%

profile of v3, /device:TPU:1, one launch (start us, length us, event | category | flops | bytes accessed | tf_op | source)
XLA Modules:
  0.0 100.3 jit_solution(3124188514937058621)
XLA Ops:
  0.7 5.3 %prep.1 = (bf16[1536,256]{1,0:T(8,128)(2,1)}, bf16[1536,128]{1,0:T(8,128)(2,1)}, bf16[8,64,192]{2,1,0:T(8,128)(2,1)}, bf16[896,128]{1,0:T(8,128)(2,1)}, bf16[896...) custom-call(bf16[48,32,256]{2,1,0:T(8,128)(2,1)} %grad.1, bf16[48,32,256]{2,1,0:T(8,128)(2,1)} %joined.1, ...), custom_call_target="tpu_custom_call" | custom-call | tf_op jit(solution)/shard_map/prep/pallas_call | solution.py:206
  6.0 1.5 %collective-permute-start = (bf16[896,128]{1,0:T(8,128)(2,1)}, bf16[896,128]{1,0:T(8,128)(2,1)S(1)}, u32[]{:S(2)}, u32[]{:S(2)}) collective-permute-start(bf16[896,128]{1,0:T(8,128)(2,1)} %get-tuple-element.67), channel_id=1, source_target_pairs={{0,4},{1,5},{2,6},{3,7},{4,0},{5,1},{6,2},{7,3},{8,12},{9,13},{10,... | collective-permute-start | bytes 688136 | tf_op jit(solution)/shard_map/ppermute | solution.py:41
  7.5 3.5 %collective-permute-start.1 = (bf16[896,128]{1,0:T(8,128)(2,1)}, bf16[896,128]{1,0:T(8,128)(2,1)S(1)}, u32[]{:S(2)}, u32[]{:S(2)}) collective-permute-start(bf16[896,128]{1,0:T(8,128)(2,1)} %get-tuple-element.68), channel_id=1, source_target_pairs={{4,8},{5,9},{6,10},{7,11},{8,4},{9,5},{10,6},{11,7},{12,16},{13,17... | collective-permute-start | bytes 688136 | tf_op jit(solution)/shard_map/ppermute | solution.py:41
  11.1 0.8 reshape.51.refs_6_
  11.9 4.0 %side.1 = (bf16[256,128]{1,0:T(8,128)(2,1)}, bf16[256,128]{1,0:T(8,128)(2,1)}, bf16[144,128]{1,0:T(8,128)(2,1)}) custom-call(bf16[1536,256]{1,0:T(8,128)(2,1)} %get-tuple-element.69.fine.refs_17_.refs_0_, bf16[1536,128]{1,0:T(8,128)(2,1)} %get-tuple-element.70.mid.refs_14_.refs_0_, bf16[8,64,192]{2,1,0:T(8,128)(2,1)} %get-tuple-element.71.coarse.refs_11_.masked, ...), custom_call_target="tpu_custom_call" | custom-call | tf_op jit(solution)/shard_map/side/pallas_call | solution.py:267
  15.9 1.3 %corners.1 = (bf16[352,128]{1,0:T(8,128)(2,1)S(1)}, bf16[352,128]{1,0:T(8,128)(2,1)S(1)}) custom-call(bf16[896,128]{1,0:T(8,128)(2,1)S(1)} %collective-permute-done.row_0.refs_0_, bf16[896,128]{1,0:T(8,128)(2,1)S(1)} %collective-permute-done.1.row_1.refs_1_, bf16[256,128]{1,0:T(8,128)(2,1)} %get-tuple-element.74.side_0, ...), custom_call_target="tpu_custom_call" | custom-call | tf_op jit(solution)/shard_map/corners/pallas_call | solution.py:330
  17.3 1.4 %collective-permute-start.2 = (bf16[352,128]{1,0:T(8,128)(2,1)S(1)}, bf16[352,128]{1,0:T(8,128)(2,1)S(1)}, u32[]{:S(2)}, u32[]{:S(2)}) collective-permute-start(bf16[352,128]{1,0:T(8,128)(2,1)S(1)} %get-tuple-element.76), channel_id=1, source_target_pairs={{0,1},{1,0},{2,3},{3,2},{4,5},{5,4},{6,7},{7,6},{8,9},{9,8},{10,11... | collective-permute-start | bytes 270344 | tf_op jit(solution)/shard_map/ppermute | solution.py:41
  18.6 0.7 collective-permute-start.3
  19.3 0.2 copy.43
  19.5 0.9 reshape.50.refs_5_
  20.4 0.3 collective-permute-done.2.refs_2_
  20.7 16.4 %grads.1 = (bf16[3,816,192]{2,1,0:T(8,128)(2,1)}, bf16[1728,256]{1,0:T(8,128)(2,1)}, bf16[1632,384]{1,0:T(8,128)(2,1)}, bf16[3840,128]{1,0:T(8,128)(2,1)}, bf16[3840,128]{1,0:T(8,128)(2,1)S(1)}) custom-call(bf16[896,128]{1,0:T(8,128)(2,1)S(1)} %collective-permute-done.row_0.refs_0_, bf16[896,128]{1,0:T(8,128)(2,1)S(1)} %collective-permute-done.1.row_1.refs_1_, ...), custom_call_target="tpu_custom_call" | custom-call | tf_op jit(solution)/shard_map/grads/pallas_call | solution.py:653
  37.1 0.1 collective-permute-start.4
  37.3 2.5 %collective-permute-done.4 = bf16[3840,128]{1,0:T(8,128)(2,1)S(1)} collective-permute-done((bf16[3840,128]{1,0:T(8,128)(2,1)S(1)}, bf16[3840,128]{1,0:T(8,128)(2,1)S(1)}, u32[]{:S(2)}, u32[]{:S(2)}) %collective-permute-start.4) | collective-permute-done | bytes 983072 | tf_op jit(solution)/shard_map/ppermute | solution.py:41
  39.8 1.5 %add_convert_fusion = bf16[3840,128]{1,0:T(8,128)(2,1)S(1)} fusion(bf16[3840,128]{1,0:T(8,128)(2,1)S(1)} %collective-permute-done.4, bf16[3840,128]{1,0:T(8,128)(2,1)} %get-tuple-element.79), kind=kLoop, calls=%fused_computation | loop fusion | flops 1966080 | bytes 2949120 | tf_op jit(solution)/shard_map/convert_element_type | solution.py:78
  41.3 0.1 dynamic-slice_bitcast_fusion.2
  41.3 4.5 %collective-permute-start.5 = (bf16[960,128]{1,0:T(8,128)(2,1)S(1)}, bf16[960,128]{1,0:T(8,128)(2,1)S(1)}, u32[]{:S(2)}, u32[]{:S(2)}) collective-permute-start(bf16[960,128]{1,0:T(8,128)(2,1)S(1)} %get-tuple-element.123), channel_id=1, source_target_pairs={{0,1},{1,0},{2,3},{3,2},{4,36},{5,37},{6,38},{7,39},{8,9},{9,8},{1... | collective-permute-start | bytes 737288 | tf_op jit(solution)/shard_map/ppermute | solution.py:41
  45.9 1.8 %collective-permute-start.7 = (bf16[960,128]{1,0:T(8,128)(2,1)S(1)}, bf16[960,128]{1,0:T(8,128)(2,1)S(1)}, u32[]{:S(2)}, u32[]{:S(2)}) collective-permute-start(bf16[960,128]{1,0:T(8,128)(2,1)S(1)} %get-tuple-element.124), channel_id=1, source_target_pairs={{0,3},{1,2},{2,1},{3,0},{4,100},{5,101},{6,102},{7,103},{8,11},{9,... | collective-permute-start | bytes 737288 | tf_op jit(solution)/shard_map/ppermute | solution.py:41
  47.7 0.9 collective-permute-start.6
  48.7 0.8 reshape.53.refs_2_
  49.4 4.0 %fine_input.1 = bf16[48,32,256]{2,1,0:T(8,128)(2,1)} custom-call(bf16[1536,256]{1,0:T(8,128)(2,1)} %get-tuple-element.69.fine.refs_17_.refs_0_, bf16[1632,384]{1,0:T(8,128)(2,1)} %get-tuple-element.83.refs_1_, bf16[144,144]{1,0:T(8,128)(2,1)} %reshape.53.refs_2_), custom_call_target="tpu_custom_call" | custom-call | tf_op jit(solution)/shard_map/fine_input/pallas_call | solution.py:454
  53.4 1.7 %collective-permute-done.6 = bf16[960,128]{1,0:T(8,128)(2,1)S(1)} collective-permute-done((bf16[960,128]{1,0:T(8,128)(2,1)S(1)}, bf16[960,128]{1,0:T(8,128)(2,1)S(1)}, u32[]{:S(2)}, u32[]{:S(2)}) %collective-permute-start.6) | collective-permute-done | bytes 245792 | tf_op jit(solution)/shard_map/ppermute | solution.py:41
  55.1 0.1 fusion.1
  55.3 0.1 collective-permute-start.8
  55.4 1.9 %collective-permute-start.10 = (bf16[240,128]{1,0:T(8,128)(2,1)S(1)}, bf16[240,128]{1,0:T(8,128)(2,1)S(1)}, u32[]{:S(2)}, u32[]{:S(2)}) collective-permute-start(bf16[240,128]{1,0:T(8,128)(2,1)S(1)} %get-tuple-element.127), channel_id=1, source_target_pairs={{0,96},{1,97},{2,98},{3,99},{4,28},{5,29},{6,30},{7,31},{8,104},{9... | collective-permute-start | bytes 184328 | tf_op jit(solution)/shard_map/ppermute | solution.py:41
  57.2 1.4 %collective-permute-start.9 = (bf16[240,128]{1,0:T(8,128)(2,1)S(1)}, bf16[240,128]{1,0:T(8,128)(2,1)S(1)}, u32[]{:S(2)}, u32[]{:S(2)}) collective-permute-start(bf16[240,128]{1,0:T(8,128)(2,1)S(1)} %get-tuple-element.128), channel_id=1, source_target_pairs={{0,64},{1,65},{2,66},{3,67},{4,20},{5,21},{6,22},{7,23},{8,72},{9,... | collective-permute-start | bytes 184328 | tf_op jit(solution)/shard_map/ppermute | solution.py:41
  58.6 1.1 %collective-permute-done.10 = bf16[240,128]{1,0:T(8,128)(2,1)S(1)} collective-permute-done((bf16[240,128]{1,0:T(8,128)(2,1)S(1)}, bf16[240,128]{1,0:T(8,128)(2,1)S(1)}, u32[]{:S(2)}, u32[]{:S(2)}) %collective-permute-start.10) | collective-permute-done | bytes 61472 | tf_op jit(solution)/shard_map/ppermute | solution.py:41
  59.7 2.1 %collective-permute-done.9 = bf16[240,128]{1,0:T(8,128)(2,1)S(1)} collective-permute-done((bf16[240,128]{1,0:T(8,128)(2,1)S(1)}, bf16[240,128]{1,0:T(8,128)(2,1)S(1)}, u32[]{:S(2)}, u32[]{:S(2)}) %collective-permute-start.9) | collective-permute-done | bytes 61472 | tf_op jit(solution)/shard_map/ppermute | solution.py:41
  61.8 2.8 %collective-permute-start.13 = (bf16[240,128]{1,0:T(8,128)(2,1)S(1)}, bf16[240,128]{1,0:T(8,128)(2,1)S(1)}, u32[]{:S(2)}, u32[]{:S(2)}) collective-permute-start(bf16[240,128]{1,0:T(8,128)(2,1)S(1)} %fusion.3), channel_id=1, source_target_pairs={{0,24},{1,25},{2,26},{3,27},{4,7},{5,6},{6,5},{7,4},{8,16},{9,17},... | collective-permute-start | bytes 184328 | tf_op jit(solution)/shard_map/ppermute | solution.py:41
  64.6 2.9 %collective-permute-start.12 = (bf16[240,128]{1,0:T(8,128)(2,1)S(1)}, bf16[240,128]{1,0:T(8,128)(2,1)S(1)}, u32[]{:S(2)}, u32[]{:S(2)}) collective-permute-start(bf16[240,128]{1,0:T(8,128)(2,1)S(1)} %fusion.3), channel_id=1, source_target_pairs={{0,16},{1,17},{2,18},{3,19},{4,6},{5,7},{6,4},{7,5},{8,24},{9,25},... | collective-permute-start | bytes 184328 | tf_op jit(solution)/shard_map/ppermute | solution.py:41
  67.5 0.2 copy.46
  67.7 0.9 reshape.56.refs_2_
  68.6 0.6 collective-permute-done.12
  69.2 1.4 %collective-permute-done.11 = bf16[240,128]{1,0:T(8,128)(2,1)S(1)} collective-permute-done((bf16[240,128]{1,0:T(8,128)(2,1)S(1)}, bf16[240,128]{1,0:T(8,128)(2,1)S(1)}, u32[]{:S(2)}, u32[]{:S(2)}) %collective-permute-start.11) | collective-permute-done | bytes 61472 | tf_op jit(solution)/shard_map/ppermute | solution.py:41
  70.6 1.3 %collective-permute-start.16 = (bf16[240,128]{1,0:T(8,128)(2,1)S(1)}, bf16[240,128]{1,0:T(8,128)(2,1)S(1)}, u32[]{:S(2)}, u32[]{:S(2)}) collective-permute-start(bf16[240,128]{1,0:T(8,128)(2,1)S(1)} %add_convert_fusion.1), channel_id=1, source_target_pairs={{0,96},{1,97},{2,98},{3,99},{4,28},{5,29},{6,30},{7,31},{8,104},{9... | collective-permute-start | bytes 184328 | tf_op jit(solution)/shard_map/ppermute | solution.py:41
  71.9 2.0 %collective-permute-start.15 = (bf16[240,128]{1,0:T(8,128)(2,1)S(1)}, bf16[240,128]{1,0:T(8,128)(2,1)S(1)}, u32[]{:S(2)}, u32[]{:S(2)}) collective-permute-start(bf16[240,128]{1,0:T(8,128)(2,1)S(1)} %add_convert_fusion.1), channel_id=1, source_target_pairs={{0,64},{1,65},{2,66},{3,67},{4,20},{5,21},{6,22},{7,23},{8,72},{9,... | collective-permute-start | bytes 184328 | tf_op jit(solution)/shard_map/ppermute | solution.py:41
  73.8 0.1 collective-permute-start.14
  74.0 3.6 %mid_input.1 = bf16[96,16,128]{2,1,0:T(8,128)(2,1)} custom-call(bf16[1536,128]{1,0:T(8,128)(2,1)} %get-tuple-element.70.mid.refs_14_.refs_0_, bf16[1728,256]{1,0:T(8,128)(2,1)} %get-tuple-element.88.refs_1_, bf16[288,288]{1,0:T(8,128)(2,1)} %reshape.56.refs_2_), custom_call_target="tpu_custom_call" | custom-call | tf_op jit(solution)/shard_map/mid_input/pallas_call | solution.py:454
  77.7 0.2 collective-permute-start.17
  77.9 1.7 %collective-permute-start.19 = (bf16[960,128]{1,0:T(8,128)(2,1)S(1)}, bf16[960,128]{1,0:T(8,128)(2,1)S(1)}, u32[]{:S(2)}, u32[]{:S(2)}) collective-permute-start(bf16[960,128]{1,0:T(8,128)(2,1)S(1)} %bitcast.66), channel_id=1, source_target_pairs={{0,3},{1,2},{2,1},{3,0},{4,100},{5,101},{6,102},{7,103},{8,11},{9,... | collective-permute-start | bytes 737288 | tf_op jit(solution)/shard_map/ppermute | solution.py:41
  79.6 1.4 %collective-permute-start.18 = (bf16[960,128]{1,0:T(8,128)(2,1)S(1)}, bf16[960,128]{1,0:T(8,128)(2,1)S(1)}, u32[]{:S(2)}, u32[]{:S(2)}) collective-permute-start(bf16[960,128]{1,0:T(8,128)(2,1)S(1)} %bitcast.67), channel_id=1, source_target_pairs={{0,2},{1,3},{2,0},{3,1},{4,68},{5,69},{6,70},{7,71},{8,10},{9,11},... | collective-permute-start | bytes 737288 | tf_op jit(solution)/shard_map/ppermute | solution.py:41
  81.0 0.1 broadcast_in_dim.37
  81.2 3.3 %coarse_input.1 = bf16[8,64,192]{2,1,0:T(8,128)(2,1)} custom-call(bf16[8,64,192]{2,1,0:T(8,128)(2,1)} %get-tuple-element.71.coarse.refs_11_.masked, bf16[3,816,192]{2,1,0:T(8,128)(2,1)} %get-tuple-element.93.px, bf16[3,3,192,192]{3,2,1,0:T(8,128)(2,1)} %first.1), custom_call_target="tpu_custom_call" | custom-call | tf_op jit(solution)/shard_map/coarse_input/pallas_call | solution.py:680
  84.5 3.8 %collective-permute-done.18 = bf16[960,128]{1,0:T(8,128)(2,1)S(1)} collective-permute-done((bf16[960,128]{1,0:T(8,128)(2,1)S(1)}, bf16[960,128]{1,0:T(8,128)(2,1)S(1)}, u32[]{:S(2)}, u32[]{:S(2)}) %collective-permute-start.18) | collective-permute-done | bytes 245792 | tf_op jit(solution)/shard_map/ppermute | solution.py:41
  88.4 8.0 %collective-permute-start.20 = (bf16[3840,128]{1,0:T(8,128)(2,1)S(1)}, bf16[3840,128]{1,0:T(8,128)(2,1)S(1)}, u32[]{:S(2)}, u32[]{:S(2)}) collective-permute-start(bf16[3840,128]{1,0:T(8,128)(2,1)S(1)} %bitcast.54), channel_id=1, source_target_pairs={{0,4},{1,5},{2,6},{3,7},{4,0},{5,1},{6,2},{7,3},{8,12},{9,13},{10,... | collective-permute-start | bytes 2949128 | tf_op jit(solution)/shard_map/ppermute | solution.py:41
  96.3 1.6 %unpack_kept.1 = (f32[3,3,48,48]{3,2,1,0:T(8,128)}, f32[3,3,48,48]{3,2,1,0:T(8,128)}, f32[3,3,96,96]{3,2,1,0:T(8,128)}, f32[3,3,96,96]{3,2,1,0:T(8,128)}, f32[3,...) custom-call(bf16[3840,128]{1,0:T(8,128)(2,1)S(1)} %bitcast.55), custom_call_target="tpu_custom_call" | custom-call | tf_op jit(solution)/shard_map/unpack_kept/pallas_call | solution.py:755
  97.9 0.6 collective-permute-done.20.refs_0_
  98.5 1.6 %unpack_other.1 = (f32[3,3,48,48]{3,2,1,0:T(8,128)}, f32[3,3,48,48]{3,2,1,0:T(8,128)}, f32[3,3,96,96]{3,2,1,0:T(8,128)}, f32[3,3,96,96]{3,2,1,0:T(8,128)}, f32[3...) custom-call(bf16[3840,128]{1,0:T(8,128)(2,1)S(1)} %collective-permut, ...), custom_call_target="tpu_custom_call", output_to_operand_aliasing={{0}: (1, {}), {1}: (2, {}), {2}: (3, {}), {3}: (4, {}), {4}... | custom-call | tf_op jit(solution)/shard_map/unpack_other/pallas_call | solution.py:755
  (39 shorter events, 0.6 us)
Async XLA Ops:
  0.6 10.4 %copy-start.2 = (bf16[3,3,48,48]{3,2,1,0:T(8,128)(2,1)S(1)}, bf16[3,3,48,48]{3,2,1,0:T(8,128)(2,1)}, u32[]{:S(2)}) copy-start(bf16[3,3,48,48]{3,2,1,0:T(8,128)(2,1)} %param.32) | copy-start | bytes 124420
  6.0 9.9 %collective-permute-start = (bf16[896,128]{1,0:T(8,128)(2,1)}, bf16[896,128]{1,0:T(8,128)(2,1)S(1)}, u32[]{:S(2)}, u32[]{:S(2)}) collective-permute-start(bf16[896,128]{1,0:T(8,128)(2,1)} %get-tuple-element.67), channel_id=1, source_target_pairs={{0,4},{1,5},{2,6},{3,7},{4,0},{5,1},{6,2},{7,3},{8,12},{9,13},{10,... | collective-permute-start | bytes 688136 | tf_op jit(solution)/shard_map/ppermute | solution.py:41
  7.5 8.4 %collective-permute-start.1 = (bf16[896,128]{1,0:T(8,128)(2,1)}, bf16[896,128]{1,0:T(8,128)(2,1)S(1)}, u32[]{:S(2)}, u32[]{:S(2)}) collective-permute-start(bf16[896,128]{1,0:T(8,128)(2,1)} %get-tuple-element.68), channel_id=1, source_target_pairs={{4,8},{5,9},{6,10},{7,11},{8,4},{9,5},{10,6},{11,7},{12,16},{13,17... | collective-permute-start | bytes 688136 | tf_op jit(solution)/shard_map/ppermute | solution.py:41
  11.9 7.4 %copy-start = (bf16[3,3,96,96]{3,2,1,0:T(8,128)(2,1)S(1)}, bf16[3,3,96,96]{3,2,1,0:T(8,128)(2,1)}, u32[]{:S(2)}) copy-start(bf16[3,3,96,96]{3,2,1,0:T(8,128)(2,1)} %param.34) | copy-start | bytes 497668
  17.3 3.5 %collective-permute-start.2 = (bf16[352,128]{1,0:T(8,128)(2,1)S(1)}, bf16[352,128]{1,0:T(8,128)(2,1)S(1)}, u32[]{:S(2)}, u32[]{:S(2)}) collective-permute-start(bf16[352,128]{1,0:T(8,128)(2,1)S(1)} %get-tuple-element.76), channel_id=1, source_target_pairs={{0,1},{1,0},{2,3},{3,2},{4,5},{5,4},{6,7},{7,6},{8,9},{9,8},{10,11... | collective-permute-start | bytes 270344 | tf_op jit(solution)/shard_map/ppermute | solution.py:41
  18.6 2.1 %collective-permute-start.3 = (bf16[352,128]{1,0:T(8,128)(2,1)S(1)}, bf16[352,128]{1,0:T(8,128)(2,1)S(1)}, u32[]{:S(2)}, u32[]{:S(2)}) collective-permute-start(bf16[352,128]{1,0:T(8,128)(2,1)S(1)} %get-tuple-element.77), channel_id=1, source_target_pairs={{1,2},{2,1},{5,6},{6,5},{9,10},{10,9},{13,14},{14,13},{17,18},{18,... | collective-permute-start | bytes 270344 | tf_op jit(solution)/shard_map/ppermute | solution.py:41
  37.1 2.6 %collective-permute-start.4 = (bf16[3840,128]{1,0:T(8,128)(2,1)S(1)}, bf16[3840,128]{1,0:T(8,128)(2,1)S(1)}, u32[]{:S(2)}, u32[]{:S(2)}) collective-permute-start(bf16[3840,128]{1,0:T(8,128)(2,1)S(1)} %get-tuple-element.80), channel_id=1, source_target_pairs={{0,4},{1,5},{2,6},{3,7},{4,0},{5,1},{6,2},{7,3},{8,12},{9,13},{10,... | collective-permute-start | bytes 2949128 | tf_op jit(solution)/shard_map/ppermute | solution.py:41
  39.8 8.8 %copy-start.3 = (bf16[3,3,48,48]{3,2,1,0:T(8,128)(2,1)S(1)}, bf16[3,3,48,48]{3,2,1,0:T(8,128)(2,1)}, u32[]{:S(2)}) copy-start(bf16[3,3,48,48]{3,2,1,0:T(8,128)(2,1)} %param.31) | copy-start | bytes 124420
  41.3 12.1 %collective-permute-start.5 = (bf16[960,128]{1,0:T(8,128)(2,1)S(1)}, bf16[960,128]{1,0:T(8,128)(2,1)S(1)}, u32[]{:S(2)}, u32[]{:S(2)}) collective-permute-start(bf16[960,128]{1,0:T(8,128)(2,1)S(1)} %get-tuple-element.123), channel_id=1, source_target_pairs={{0,1},{1,0},{2,3},{3,2},{4,36},{5,37},{6,38},{7,39},{8,9},{9,8},{1... | collective-permute-start | bytes 737288 | tf_op jit(solution)/shard_map/ppermute | solution.py:41
  45.9 7.6 %collective-permute-start.7 = (bf16[960,128]{1,0:T(8,128)(2,1)S(1)}, bf16[960,128]{1,0:T(8,128)(2,1)S(1)}, u32[]{:S(2)}, u32[]{:S(2)}) collective-permute-start(bf16[960,128]{1,0:T(8,128)(2,1)S(1)} %get-tuple-element.124), channel_id=1, source_target_pairs={{0,3},{1,2},{2,1},{3,0},{4,100},{5,101},{6,102},{7,103},{8,11},{9,... | collective-permute-start | bytes 737288 | tf_op jit(solution)/shard_map/ppermute | solution.py:41
  47.7 7.4 %collective-permute-start.6 = (bf16[960,128]{1,0:T(8,128)(2,1)S(1)}, bf16[960,128]{1,0:T(8,128)(2,1)S(1)}, u32[]{:S(2)}, u32[]{:S(2)}) collective-permute-start(bf16[960,128]{1,0:T(8,128)(2,1)S(1)} %get-tuple-element.125), channel_id=1, source_target_pairs={{0,2},{1,3},{2,0},{3,1},{4,68},{5,69},{6,70},{7,71},{8,10},{9,11},... | collective-permute-start | bytes 737288 | tf_op jit(solution)/shard_map/ppermute | solution.py:41
  49.4 18.1 %copy-start.1 = (bf16[3,3,96,96]{3,2,1,0:T(8,128)(2,1)S(1)}, bf16[3,3,96,96]{3,2,1,0:T(8,128)(2,1)}, u32[]{:S(2)}) copy-start(bf16[3,3,96,96]{3,2,1,0:T(8,128)(2,1)} %param.33) | copy-start | bytes 497668
  55.3 3.3 %collective-permute-start.8 = (bf16[240,128]{1,0:T(8,128)(2,1)S(1)}, bf16[240,128]{1,0:T(8,128)(2,1)S(1)}, u32[]{:S(2)}, u32[]{:S(2)}) collective-permute-start(bf16[240,128]{1,0:T(8,128)(2,1)S(1)} %get-tuple-element.126), channel_id=1, source_target_pairs={{0,32},{1,33},{2,34},{3,35},{4,12},{5,13},{6,14},{7,15},{8,40},{9,... | collective-permute-start | bytes 184328 | tf_op jit(solution)/shard_map/ppermute | solution.py:41
  55.4 4.4 %collective-permute-start.10 = (bf16[240,128]{1,0:T(8,128)(2,1)S(1)}, bf16[240,128]{1,0:T(8,128)(2,1)S(1)}, u32[]{:S(2)}, u32[]{:S(2)}) collective-permute-start(bf16[240,128]{1,0:T(8,128)(2,1)S(1)} %get-tuple-element.127), channel_id=1, source_target_pairs={{0,96},{1,97},{2,98},{3,99},{4,28},{5,29},{6,30},{7,31},{8,104},{9... | collective-permute-start | bytes 184328 | tf_op jit(solution)/shard_map/ppermute | solution.py:41
  57.2 4.6 %collective-permute-start.9 = (bf16[240,128]{1,0:T(8,128)(2,1)S(1)}, bf16[240,128]{1,0:T(8,128)(2,1)S(1)}, u32[]{:S(2)}, u32[]{:S(2)}) collective-permute-start(bf16[240,128]{1,0:T(8,128)(2,1)S(1)} %get-tuple-element.128), channel_id=1, source_target_pairs={{0,64},{1,65},{2,66},{3,67},{4,20},{5,21},{6,22},{7,23},{8,72},{9,... | collective-permute-start | bytes 184328 | tf_op jit(solution)/shard_map/ppermute | solution.py:41
  61.8 6.8 %collective-permute-start.13 = (bf16[240,128]{1,0:T(8,128)(2,1)S(1)}, bf16[240,128]{1,0:T(8,128)(2,1)S(1)}, u32[]{:S(2)}, u32[]{:S(2)}) collective-permute-start(bf16[240,128]{1,0:T(8,128)(2,1)S(1)} %fusion.3), channel_id=1, source_target_pairs={{0,24},{1,25},{2,26},{3,27},{4,7},{5,6},{6,5},{7,4},{8,16},{9,17},... | collective-permute-start | bytes 184328 | tf_op jit(solution)/shard_map/ppermute | solution.py:41
  64.6 4.6 %collective-permute-start.12 = (bf16[240,128]{1,0:T(8,128)(2,1)S(1)}, bf16[240,128]{1,0:T(8,128)(2,1)S(1)}, u32[]{:S(2)}, u32[]{:S(2)}) collective-permute-start(bf16[240,128]{1,0:T(8,128)(2,1)S(1)} %fusion.3), channel_id=1, source_target_pairs={{0,16},{1,17},{2,18},{3,19},{4,6},{5,7},{6,4},{7,5},{8,24},{9,25},... | collective-permute-start | bytes 184328 | tf_op jit(solution)/shard_map/ppermute | solution.py:41
  67.5 3.1 %collective-permute-start.11 = (bf16[240,128]{1,0:T(8,128)(2,1)S(1)}, bf16[240,128]{1,0:T(8,128)(2,1)S(1)}, u32[]{:S(2)}, u32[]{:S(2)}) collective-permute-start(bf16[240,128]{1,0:T(8,128)(2,1)S(1)} %fusion.3), channel_id=1, source_target_pairs={{0,8},{1,9},{2,10},{3,11},{4,5},{5,4},{6,7},{7,6},{8,0},{9,1},{10,... | collective-permute-start | bytes 184328 | tf_op jit(solution)/shard_map/ppermute | solution.py:41
  70.6 7.0 %collective-permute-start.16 = (bf16[240,128]{1,0:T(8,128)(2,1)S(1)}, bf16[240,128]{1,0:T(8,128)(2,1)S(1)}, u32[]{:S(2)}, u32[]{:S(2)}) collective-permute-start(bf16[240,128]{1,0:T(8,128)(2,1)S(1)} %add_convert_fusion.1), channel_id=1, source_target_pairs={{0,96},{1,97},{2,98},{3,99},{4,28},{5,29},{6,30},{7,31},{8,104},{9... | collective-permute-start | bytes 184328 | tf_op jit(solution)/shard_map/ppermute | solution.py:41
  71.9 5.7 %collective-permute-start.15 = (bf16[240,128]{1,0:T(8,128)(2,1)S(1)}, bf16[240,128]{1,0:T(8,128)(2,1)S(1)}, u32[]{:S(2)}, u32[]{:S(2)}) collective-permute-start(bf16[240,128]{1,0:T(8,128)(2,1)S(1)} %add_convert_fusion.1), channel_id=1, source_target_pairs={{0,64},{1,65},{2,66},{3,67},{4,20},{5,21},{6,22},{7,23},{8,72},{9,... | collective-permute-start | bytes 184328 | tf_op jit(solution)/shard_map/ppermute | solution.py:41
  73.8 3.7 %collective-permute-start.14 = (bf16[240,128]{1,0:T(8,128)(2,1)S(1)}, bf16[240,128]{1,0:T(8,128)(2,1)S(1)}, u32[]{:S(2)}, u32[]{:S(2)}) collective-permute-start(bf16[240,128]{1,0:T(8,128)(2,1)S(1)} %add_convert_fusion.1), channel_id=1, source_target_pairs={{0,32},{1,33},{2,34},{3,35},{4,12},{5,13},{6,14},{7,15},{8,40},{9,... | collective-permute-start | bytes 184328 | tf_op jit(solution)/shard_map/ppermute | solution.py:41
  77.7 6.8 %collective-permute-start.17 = (bf16[960,128]{1,0:T(8,128)(2,1)S(1)}, bf16[960,128]{1,0:T(8,128)(2,1)S(1)}, u32[]{:S(2)}, u32[]{:S(2)}) collective-permute-start(bf16[960,128]{1,0:T(8,128)(2,1)S(1)} %bitcast.65), channel_id=1, source_target_pairs={{0,1},{1,0},{2,3},{3,2},{4,36},{5,37},{6,38},{7,39},{8,9},{9,8},{1... | collective-permute-start | bytes 737288 | tf_op jit(solution)/shard_map/ppermute | solution.py:41
  77.9 10.4 %collective-permute-start.19 = (bf16[960,128]{1,0:T(8,128)(2,1)S(1)}, bf16[960,128]{1,0:T(8,128)(2,1)S(1)}, u32[]{:S(2)}, u32[]{:S(2)}) collective-permute-start(bf16[960,128]{1,0:T(8,128)(2,1)S(1)} %bitcast.66), channel_id=1, source_target_pairs={{0,3},{1,2},{2,1},{3,0},{4,100},{5,101},{6,102},{7,103},{8,11},{9,... | collective-permute-start | bytes 737288 | tf_op jit(solution)/shard_map/ppermute | solution.py:41
  79.6 8.6 %collective-permute-start.18 = (bf16[960,128]{1,0:T(8,128)(2,1)S(1)}, bf16[960,128]{1,0:T(8,128)(2,1)S(1)}, u32[]{:S(2)}, u32[]{:S(2)}) collective-permute-start(bf16[960,128]{1,0:T(8,128)(2,1)S(1)} %bitcast.67), channel_id=1, source_target_pairs={{0,2},{1,3},{2,0},{3,1},{4,68},{5,69},{6,70},{7,71},{8,10},{9,11},... | collective-permute-start | bytes 737288 | tf_op jit(solution)/shard_map/ppermute | solution.py:41
  88.4 10.2 %collective-permute-start.20 = (bf16[3840,128]{1,0:T(8,128)(2,1)S(1)}, bf16[3840,128]{1,0:T(8,128)(2,1)S(1)}, u32[]{:S(2)}, u32[]{:S(2)}) collective-permute-start(bf16[3840,128]{1,0:T(8,128)(2,1)S(1)} %bitcast.54), channel_id=1, source_target_pairs={{0,4},{1,5},{2,6},{3,7},{4,0},{5,1},{6,2},{7,3},{8,12},{9,13},{10,... | collective-permute-start | bytes 2949128 | tf_op jit(solution)/shard_map/ppermute | solution.py:41

commit v4 on v3

--- a/solution.py
+++ b/solution.py
@@ -215,7 +215,21 @@
     )(*args)
 
 
-def side_kernel(
+def side_kernel(*refs):
+    arrays, outs, scratch, tiles, sems = refs[:10], refs[10:13], refs[13:16], refs[16:26], refs[26]
+    pull(arrays, tiles, sems)
+    side_work(*tiles, *outs, *scratch)
+
+
+def pull(arrays, tiles, sems):
+    loads = [pltpu.make_async_copy(array, tile, sems.at[k]) for k, (array, tile) in enumerate(zip(arrays, tiles))]
+    for load in loads:
+        load.start()
+    for load in loads:
+        load.wait()
+
+
+def side_work(
     fine, mid, coarse, inner_fine, inner_mid, inner_coarse, unit_mid, unit_coarse, pooled_mid, pooled_coarse,
     side_0, side_1, lift, in_fine, in_mid, gate_mid,
 ):
@@ -267,7 +281,10 @@
     return pl.pallas_call(
         side_kernel,
         out_shape=[jax.ShapeDtypeStruct(shape, half) for shape in ((256, 128), (256, 128), (144, 128))],
-        scratch_shapes=[pltpu.VMEM((CELLS, width), half) for width in (256, 128, 128)],
+        in_specs=[pl.BlockSpec(memory_space=pl.ANY)] * 10,
+        scratch_shapes=[pltpu.VMEM((CELLS, width), half) for width in (256, 128, 128)]
+        + [pltpu.VMEM(array.shape, half) for array in args]
+        + [pltpu.SemaphoreType.DMA((10,))],
         compiler_params=PARAMS,
         name="side",
     )(*args)
@@ -289,8 +306,9 @@
         self.left, self.right = jnp.where(col_even, cols[1], cols[0]), jnp.where(col_even, cols[0], cols[1])
 
 
-def corner_kernel(row_0, row_1, side_0, side_1, col_0, col_1):
+def corner_kernel(row_0, row_1, far_0, far_1, col_0, col_1, side_0, side_1, sems):
     half = jnp.bfloat16
+    pull((far_0, far_1), (side_0, side_1), sems)
     row_parity, col_parity = my_parity()
     row_even = row_parity == 0
     halos = (jnp.where(row_even, row_1[...], row_0[...]), jnp.where(row_even, row_0[...], row_1[...]))
@@ -331,7 +349,8 @@
         corner_kernel,
         out_shape=[pltpu.VMEM((352, 128), jnp.bfloat16)] * 2,
         out_specs=[IN_VMEM] * 2,
-        in_specs=[IN_VMEM] * 4,
+        in_specs=[IN_VMEM] * 2 + [pl.BlockSpec(memory_space=pl.ANY)] * 2,
+        scratch_shapes=[pltpu.VMEM((256, 128), jnp.bfloat16)] * 2 + [pltpu.SemaphoreType.DMA((2,))],
         compiler_params=PARAMS,
         name="corners",
     )(*near(*messages[:2]), *messages[2:])
@@ -400,7 +419,9 @@
     return pltpu.roll(parts[:chans], ring - 1, 1) + parts[chans : 2 * chans] + pltpu.roll(parts[2 * chans :], 1, 1)
 
 
-def input_kernel(masked, px, first, out, ox, *, chans, rows, width):
+def input_kernel(masked, px, raw, out, ox, first, *, chans, rows, width):
+    first[...] = stacked_rows(raw, chans)
+
     def step(row, carry):
         at = pl.multiple_of(row * chans, 16)
         grad = ring_taps(first[...], px[pl.ds(at, 3 * chans), :], chans, width + 128)[:, :width]
@@ -443,8 +464,8 @@
             sums[index, tap * 288 : (tap + 1) * 288, :] = part.astype(jnp.bfloat16)
 
 
-def stacked(weight, chans):
-    return jnp.transpose(weight[::-1], (1, 2, 0, 3)).reshape(3 * chans, 3 * chans)
+def stacked_rows(weight, chans):
+    return jnp.concatenate([weight[tap].reshape(3 * chans, chans) for tap in (2, 1, 0)], axis=1)
 
 
 def channel_input(masked, px, first, chans, rows, width, name):
@@ -454,10 +475,10 @@
     return pl.pallas_call(
         kernel,
         out_shape=jax.ShapeDtypeStruct((chans, rows, width), jnp.bfloat16),
-        scratch_shapes=[pltpu.VMEM((rows, chans, width), jnp.bfloat16)],
+        scratch_shapes=[pltpu.VMEM((rows, chans, width), jnp.bfloat16), pltpu.VMEM((3 * chans, 3 * chans), jnp.bfloat16)],
         compiler_params=PARAMS,
         name=name,
-    )(masked, px, stacked(first, chans))
+    )(masked, px, first)
 
 
 def coarse_places():
@@ -549,18 +570,22 @@
 
 
 def grads_kernel(*refs):
-    messages, (second_coarse, second_mid, second_fine, place, lift), refs = refs[:4], refs[4:9], refs[9:]
+    messages, weights, refs = refs[:4], refs[4:9], refs[9:]
     arrays, (px_coarse, px_mid, px_fine, kept, given), refs = refs[:9], refs[9:14], refs[14:]
-    held, work, (load_sems, px_sems, sum_sems) = refs[:7], refs[7:27], refs[27:]
+    held, work, refs = refs[:7], refs[7:27], refs[27:]
+    (second_coarse, raw_mid, raw_fine, place, lift, second_mid, second_fine), (load_sems, px_sems, sum_sems) = refs[:7], refs[7:]
     coarse_work, mid_work, fine_work = work[:6], work[6:13], work[13:20]
     sum_coarse, sum_mid, sum_fine = coarse_work[0], mid_work[0], fine_work[0]
     mx_mid, mx_fine = mid_work[2], fine_work[2]
     core, _ = my_parity()
 
     places = (
-        *held[:3],
-        held[3], held[4], mx_mid.at[2 * MID : 2 * MID + CELLS, 0:128],
-        held[5], held[6], mx_fine.at[2 * FINE : 2 * FINE + CELLS, 0:256],
+        *held[:3], second_coarse, place,
+        held[3], held[4], mx_mid.at[2 * MID : 2 * MID + CELLS, 0:128], raw_mid,
+        held[5], held[6], mx_fine.at[2 * FINE : 2 * FINE + CELLS, 0:256], raw_fine, lift,
+    )
+    arrays = (
+        *arrays[:3], weights[0], weights[3], *arrays[3:6], weights[1], *arrays[6:], weights[2], weights[4],
     )
     loads = [pltpu.make_async_copy(array, to, load_sems.at[k]) for k, (array, to) in enumerate(zip(arrays, places))]
     for load in loads:
@@ -592,13 +617,14 @@
     pieces = ((sum_coarse, 0, AT_MID), (sum_mid, AT_MID, AT_FINE - AT_MID), (sum_fine, AT_FINE, HALF_ROWS - AT_FINE))
     sums = [sum_copies(*piece, k) for k, piece in enumerate(pieces)]
 
-    for load in loads[:3]:
+    for load in loads[:5]:
         load.wait()
     coarse_part(halo, second_coarse, place, (*held[:3], *coarse_work), px_copies[0].start)
     write(sums[0])
 
-    for load in loads[3:6]:
+    for load in loads[5:9]:
         load.wait()
+    second_mid[...] = stacked_rows(raw_mid, MID)
     channel_part(
         halo, second_mid, (held[3], held[4], *mid_work[1:]), px_copies[1].start,
         chans=MID, rows=16, width=128, edge=3, fill_rows=mid_rows,
@@ -606,8 +632,9 @@
     mid_grads(sum_mid, mid_work[5], mid_work[6])
     write(sums[1])
 
-    for load in loads[6:]:
+    for load in loads[9:]:
         load.wait()
+    second_fine[...] = stacked_rows(raw_fine, FINE)
     channel_part(
         halo, second_fine, (held[5], held[6], *fine_work[1:]), px_copies[2].start,
         chans=FINE, rows=32, width=256, edge=0, fill_rows=fine_rows,
@@ -650,6 +677,11 @@
         ((COARSE, 8 * PITCH), half),
     ]
     scratch = held + coarse_work + channel_work(MID, 16, 128, AT_FINE - AT_MID) + channel_work(FINE, 32, 256, HALF_ROWS - AT_FINE)
+    shapes = (
+        (3, 3, COARSE, COARSE), (3, 3, MID, MID), (3, 3, FINE, FINE), (2 * 13 * 16, 96), (144, 128),
+        (3 * MID, 3 * MID), (3 * FINE, 3 * FINE),
+    )
+    weights = [(shape, half) for shape in shapes]
     return pl.pallas_call(
         grads_kernel,
         out_shape=[
@@ -659,10 +691,10 @@
             jax.ShapeDtypeStruct((HALF_ROWS, 128), half),
             pltpu.VMEM((HALF_ROWS, 128), half),
         ],
-        in_specs=[IN_VMEM] * 9 + [any_memory] * 9,
+        in_specs=[IN_VMEM] * 4 + [any_memory] * 14,
         out_specs=[any_memory] * 4 + [IN_VMEM],
-        scratch_shapes=[pltpu.VMEM(*shape) for shape in scratch]
-        + [pltpu.SemaphoreType.DMA((9,)), pltpu.SemaphoreType.DMA((3,)), pltpu.SemaphoreType.DMA((6,))],
+        scratch_shapes=[pltpu.VMEM(*shape) for shape in scratch + weights]
+        + [pltpu.SemaphoreType.DMA((14,)), pltpu.SemaphoreType.DMA((3,)), pltpu.SemaphoreType.DMA((6,))],
         compiler_params=PARAMS,
         name="grads",
     )(*near(*messages), *seconds, jnp.asarray(coarse_places(), half), lift, *arrays)
@@ -784,7 +816,7 @@
     col_0, col_1 = send(col_0, swap_pairs(None, 0)), send(col_1, swap_pairs(None, 1))
     coarse_px, mid_px, fine_px, kept, given = grads(
         (row_0, row_1, col_0, col_1),
-        (second_coarse, stacked(second_mid, MID), stacked(second_fine, FINE)),
+        (second_coarse, second_mid, second_fine),
         lift,
         (input_coarse, inner_coarse, coarse, input_mid, inner_mid, mid, input_fine, inner_fine, fine),
     )

time: 101 us -> 99.8 us (0.988)
  local copies, waits for them, and re-layouts: 4.23 us -> 0.46 us
  waiting for transfers between devices: 14.1 us -> 17.5 us
    ppermute x21, waiting for transfers between devices: 14.1 us -> 17.5 us  [send(): return lax.ppermute(block, AXES, pairs)]
    reshape x4 -> x0, local copies, waits for them, and re-layouts: 3.28 us -> none  [stacked(): jnp.transpose(weight[::-1], (1, 2, 0, 3)).reshape(3 * chans, 3 * chans)]
  transfers between devices with their start and end apart: 21 -> 21, of which waited for: 9 -> 10; matrix products, arithmetic and copies ran while one was open for 4% -> 0% of each run, Pallas kernels for 16% -> 17%
where the time goes in v4:
time: 99.8 us; the launch traced here: 99.5 us
  Pallas kernels  40.4 us (40%)
  starting transfers between devices  38.3 us (38%)
  waiting for transfers between devices  17.5 us (18%)
  other arithmetic  1.66 us (2%)
  between operations  1.08 us (1%)
    ppermute x21, starting transfers between devices, send(): return lax.ppermute(block, AXES, pairs)  38.3 us
    ppermute x21, waiting for transfers between devices, send(): return lax.ppermute(block, AXES, pairs)  17.5 us
    pallas_call x1, Pallas kernels, grads(): pl.pallas_call(grads_kernel, out_shape=[jax.ShapeDtypeStruct((3, 816, COA...  15.6 us
    pallas_call x2, Pallas kernels, channel_input(): pl.pallas_call(kernel, out_shape=jax.ShapeDtypeStruct((chans, rows, width...  7.61 us
    pallas_call x1, Pallas kernels, prep(): pl.pallas_call(prep_kernel, grid=(2,), out_shape=[jax.ShapeDtypeStruct(sh...  5.35 us
    pallas_call x1, Pallas kernels, side(): pl.pallas_call(side_kernel, out_shape=[jax.ShapeDtypeStruct(shape, half)...  4.08 us
    pallas_call x1, Pallas kernels, coarse_input(): pl.pallas_call(coarse_input_kernel, out_shape=jax.ShapeDtypeStruct((COARS...  3.27 us
    pallas_call x2, Pallas kernels, unpack(): pl.pallas_call(kernel, out_shape=[jax.ShapeDtypeStruct(shape, jnp.float32...  3.16 us
  transfers between devices with their start and end apart: 21, of which 10 were waited for; matrix products, arithmetic and copies ran while one was open for 0% of the time, Pallas kernels for 17%

profile of v4, /device:TPU:1, one launch (start us, length us, event | category | flops | bytes accessed | tf_op | source)
XLA Modules:
  0.0 99.5 jit_solution(842371092200461414)
XLA Ops:
  0.6 5.3 %prep.1 = (bf16[1536,256]{1,0:T(8,128)(2,1)}, bf16[1536,128]{1,0:T(8,128)(2,1)}, bf16[8,64,192]{2,1,0:T(8,128)(2,1)}, bf16[896,128]{1,0:T(8,128)(2,1)}, bf16[896...) custom-call(bf16[48,32,256]{2,1,0:T(8,128)(2,1)} %grad.1, bf16[48,32,256]{2,1,0:T(8,128)(2,1)} %joined.1, ...), custom_call_target="tpu_custom_call" | custom-call | tf_op jit(solution)/shard_map/prep/pallas_call | solution.py:206
  6.0 1.5 %collective-permute-start = (bf16[896,128]{1,0:T(8,128)(2,1)}, bf16[896,128]{1,0:T(8,128)(2,1)S(1)}, u32[]{:S(2)}, u32[]{:S(2)}) collective-permute-start(bf16[896,128]{1,0:T(8,128)(2,1)} %get-tuple-element.67), channel_id=1, source_target_pairs={{0,4},{1,5},{2,6},{3,7},{4,0},{5,1},{6,2},{7,3},{8,12},{9,13},{10,... | collective-permute-start | bytes 688136 | tf_op jit(solution)/shard_map/ppermute | solution.py:41
  7.5 3.5 %collective-permute-start.1 = (bf16[896,128]{1,0:T(8,128)(2,1)}, bf16[896,128]{1,0:T(8,128)(2,1)S(1)}, u32[]{:S(2)}, u32[]{:S(2)}) collective-permute-start(bf16[896,128]{1,0:T(8,128)(2,1)} %get-tuple-element.68), channel_id=1, source_target_pairs={{4,8},{5,9},{6,10},{7,11},{8,4},{9,5},{10,6},{11,7},{12,16},{13,17... | collective-permute-start | bytes 688136 | tf_op jit(solution)/shard_map/ppermute | solution.py:41
  11.0 4.1 %side.1 = (bf16[256,128]{1,0:T(8,128)(2,1)}, bf16[256,128]{1,0:T(8,128)(2,1)}, bf16[144,128]{1,0:T(8,128)(2,1)}) custom-call(bf16[1536,256]{1,0:T(8,128)(2,1)} %get-tuple-element.69.refs_0_.refs_17_, bf16[1536,128]{1,0:T(8,128)(2,1)} %get-tuple-element.70.refs_1_.refs_14_.refs_0_, bf16[8,64,192]{2,1,0:T(8,128)(2,1)} %get-tuple-element.71.refs_2_.refs_11_.masked, ...), custom_call_target="tpu_custom_call" | custom-call | tf_op jit(solution)/shard_map/side/pallas_call | solution.py:281
  15.1 1.4 %corners.1 = (bf16[352,128]{1,0:T(8,128)(2,1)S(1)}, bf16[352,128]{1,0:T(8,128)(2,1)S(1)}) custom-call(bf16[896,128]{1,0:T(8,128)(2,1)S(1)} %collective-permute-done.row_0.refs_0_, bf16[896,128]{1,0:T(8,128)(2,1)S(1)} %collective-permute-done.1.row_1.refs_1_, bf16[256,128]{1,0:T(8,128)(2,1)} %get-tuple-element.74.far_0, bf16[256,128]{1,0:T(8,128)(2,1)} %get-tuple-element.75.far_1), custom_call_target="tpu_custom_call" | custom-call | tf_op jit(solution)/shard_map/corners/pallas_call | solution.py:348
  16.5 1.4 %collective-permute-start.2 = (bf16[352,128]{1,0:T(8,128)(2,1)S(1)}, bf16[352,128]{1,0:T(8,128)(2,1)S(1)}, u32[]{:S(2)}, u32[]{:S(2)}) collective-permute-start(bf16[352,128]{1,0:T(8,128)(2,1)S(1)} %get-tuple-element.76), channel_id=1, source_target_pairs={{0,1},{1,0},{2,3},{3,2},{4,5},{5,4},{6,7},{7,6},{8,9},{9,8},{10,11... | collective-permute-start | bytes 270344 | tf_op jit(solution)/shard_map/ppermute | solution.py:41
  17.9 0.7 collective-permute-start.3
  18.5 1.4 %collective-permute-done.2.refs_2_ = bf16[352,128]{1,0:T(8,128)(2,1)S(1)} collective-permute-done((bf16[352,128]{1,0:T(8,128)(2,1)S(1)}, bf16[352,128]{1,0:T(8,128)(2,1)S(1)}, u32[]{:S(2)}, u32[]{:S(2)}) %collective-permute-start.2) | collective-permute-done | bytes 90144 | tf_op jit(solution)/shard_map/ppermute | solution.py:41
  20.0 15.6 %grads.1 = (bf16[3,816,192]{2,1,0:T(8,128)(2,1)}, bf16[1728,256]{1,0:T(8,128)(2,1)}, bf16[1632,384]{1,0:T(8,128)(2,1)}, bf16[3840,128]{1,0:T(8,128)(2,1)}, bf16[3840,128]{1,0:T(8,128)(2,1)S(1)}) custom-call(bf16[896,128]{1,0:T(8,128)(2,1)S(1)} %collective-permute-done.row_0.refs_0_, bf16[896,128]{1,0:T(8,128)(2,1)S(1)} %collective-permute-done.1.row_1.refs_1_, ...), custom_call_target="tpu_custom_call" | custom-call | tf_op jit(solution)/shard_map/grads/pallas_call | solution.py:685
  35.6 0.1 collective-permute-start.4
  35.7 2.5 %collective-permute-done.4 = bf16[3840,128]{1,0:T(8,128)(2,1)S(1)} collective-permute-done((bf16[3840,128]{1,0:T(8,128)(2,1)S(1)}, bf16[3840,128]{1,0:T(8,128)(2,1)S(1)}, u32[]{:S(2)}, u32[]{:S(2)}) %collective-permute-start.4) | collective-permute-done | bytes 983072 | tf_op jit(solution)/shard_map/ppermute | solution.py:41
  38.2 1.5 %add_convert_fusion = bf16[3840,128]{1,0:T(8,128)(2,1)S(1)} fusion(bf16[3840,128]{1,0:T(8,128)(2,1)S(1)} %collective-permute-done.4, bf16[3840,128]{1,0:T(8,128)(2,1)} %get-tuple-element.79), kind=kLoop, calls=%fused_computation | loop fusion | flops 1966080 | bytes 2949120 | tf_op jit(solution)/shard_map/convert_element_type | solution.py:78
  39.7 0.1 dynamic-slice_bitcast_fusion.2
  39.8 4.5 %collective-permute-start.5 = (bf16[960,128]{1,0:T(8,128)(2,1)S(1)}, bf16[960,128]{1,0:T(8,128)(2,1)S(1)}, u32[]{:S(2)}, u32[]{:S(2)}) collective-permute-start(bf16[960,128]{1,0:T(8,128)(2,1)S(1)} %get-tuple-element.123), channel_id=1, source_target_pairs={{0,1},{1,0},{2,3},{3,2},{4,36},{5,37},{6,38},{7,39},{8,9},{9,8},{1... | collective-permute-start | bytes 737288 | tf_op jit(solution)/shard_map/ppermute | solution.py:41
  44.3 1.8 %collective-permute-start.7 = (bf16[960,128]{1,0:T(8,128)(2,1)S(1)}, bf16[960,128]{1,0:T(8,128)(2,1)S(1)}, u32[]{:S(2)}, u32[]{:S(2)}) collective-permute-start(bf16[960,128]{1,0:T(8,128)(2,1)S(1)} %get-tuple-element.124), channel_id=1, source_target_pairs={{0,3},{1,2},{2,1},{3,0},{4,100},{5,101},{6,102},{7,103},{8,11},{9,... | collective-permute-start | bytes 737288 | tf_op jit(solution)/shard_map/ppermute | solution.py:41
  46.1 0.9 collective-permute-start.6
  47.0 4.0 %fine_input.1 = bf16[48,32,256]{2,1,0:T(8,128)(2,1)} custom-call(bf16[1536,256]{1,0:T(8,128)(2,1)} %get-tuple-element.69.refs_0_.refs_17_, bf16[1632,384]{1,0:T(8,128)(2,1)} %get-tuple-element.83.refs_1_, bf16[3,3,48,48]{3,2,1,0:T(8,128)(2,1)} %refs_2_.2), custom_call_target="tpu_custom_call" | custom-call | tf_op jit(solution)/shard_map/fine_input/pallas_call | solution.py:475
  51.0 0.8 collective-permute-done.7
  51.9 1.7 %collective-permute-done.6 = bf16[960,128]{1,0:T(8,128)(2,1)S(1)} collective-permute-done((bf16[960,128]{1,0:T(8,128)(2,1)S(1)}, bf16[960,128]{1,0:T(8,128)(2,1)S(1)}, u32[]{:S(2)}, u32[]{:S(2)}) %collective-permute-start.6) | collective-permute-done | bytes 245792 | tf_op jit(solution)/shard_map/ppermute | solution.py:41
  53.5 0.1 fusion.1
  53.7 0.1 collective-permute-start.8
  53.8 2.6 %collective-permute-start.10 = (bf16[240,128]{1,0:T(8,128)(2,1)S(1)}, bf16[240,128]{1,0:T(8,128)(2,1)S(1)}, u32[]{:S(2)}, u32[]{:S(2)}) collective-permute-start(bf16[240,128]{1,0:T(8,128)(2,1)S(1)} %get-tuple-element.127), channel_id=1, source_target_pairs={{0,96},{1,97},{2,98},{3,99},{4,28},{5,29},{6,30},{7,31},{8,104},{9... | collective-permute-start | bytes 184328 | tf_op jit(solution)/shard_map/ppermute | solution.py:41
  56.4 1.1 %collective-permute-start.9 = (bf16[240,128]{1,0:T(8,128)(2,1)S(1)}, bf16[240,128]{1,0:T(8,128)(2,1)S(1)}, u32[]{:S(2)}, u32[]{:S(2)}) collective-permute-start(bf16[240,128]{1,0:T(8,128)(2,1)S(1)} %get-tuple-element.128), channel_id=1, source_target_pairs={{0,64},{1,65},{2,66},{3,67},{4,20},{5,21},{6,22},{7,23},{8,72},{9,... | collective-permute-start | bytes 184328 | tf_op jit(solution)/shard_map/ppermute | solution.py:41
  57.5 0.6 collective-permute-done.10
  58.1 2.9 %collective-permute-done.9 = bf16[240,128]{1,0:T(8,128)(2,1)S(1)} collective-permute-done((bf16[240,128]{1,0:T(8,128)(2,1)S(1)}, bf16[240,128]{1,0:T(8,128)(2,1)S(1)}, u32[]{:S(2)}, u32[]{:S(2)}) %collective-permute-start.9) | collective-permute-done | bytes 61472 | tf_op jit(solution)/shard_map/ppermute | solution.py:41
  61.0 2.8 %collective-permute-start.13 = (bf16[240,128]{1,0:T(8,128)(2,1)S(1)}, bf16[240,128]{1,0:T(8,128)(2,1)S(1)}, u32[]{:S(2)}, u32[]{:S(2)}) collective-permute-start(bf16[240,128]{1,0:T(8,128)(2,1)S(1)} %fusion.3), channel_id=1, source_target_pairs={{0,24},{1,25},{2,26},{3,27},{4,7},{5,6},{6,5},{7,4},{8,16},{9,17},... | collective-permute-start | bytes 184328 | tf_op jit(solution)/shard_map/ppermute | solution.py:41
  63.9 2.9 %collective-permute-start.12 = (bf16[240,128]{1,0:T(8,128)(2,1)S(1)}, bf16[240,128]{1,0:T(8,128)(2,1)S(1)}, u32[]{:S(2)}, u32[]{:S(2)}) collective-permute-start(bf16[240,128]{1,0:T(8,128)(2,1)S(1)} %fusion.3), channel_id=1, source_target_pairs={{0,16},{1,17},{2,18},{3,19},{4,6},{5,7},{6,4},{7,5},{8,24},{9,25},... | collective-permute-start | bytes 184328 | tf_op jit(solution)/shard_map/ppermute | solution.py:41
  66.7 0.0 collective-permute-start.11
  66.7 1.7 %collective-permute-done.12 = bf16[240,128]{1,0:T(8,128)(2,1)S(1)} collective-permute-done((bf16[240,128]{1,0:T(8,128)(2,1)S(1)}, bf16[240,128]{1,0:T(8,128)(2,1)S(1)}, u32[]{:S(2)}, u32[]{:S(2)}) %collective-permute-start.12) | collective-permute-done | bytes 61472 | tf_op jit(solution)/shard_map/ppermute | solution.py:41
  68.4 1.4 %collective-permute-done.11 = bf16[240,128]{1,0:T(8,128)(2,1)S(1)} collective-permute-done((bf16[240,128]{1,0:T(8,128)(2,1)S(1)}, bf16[240,128]{1,0:T(8,128)(2,1)S(1)}, u32[]{:S(2)}, u32[]{:S(2)}) %collective-permute-start.11) | collective-permute-done | bytes 61472 | tf_op jit(solution)/shard_map/ppermute | solution.py:41
  69.8 0.5 collective-permute-start.16
  70.3 2.5 %collective-permute-start.15 = (bf16[240,128]{1,0:T(8,128)(2,1)S(1)}, bf16[240,128]{1,0:T(8,128)(2,1)S(1)}, u32[]{:S(2)}, u32[]{:S(2)}) collective-permute-start(bf16[240,128]{1,0:T(8,128)(2,1)S(1)} %add_convert_fusion.1), channel_id=1, source_target_pairs={{0,64},{1,65},{2,66},{3,67},{4,20},{5,21},{6,22},{7,23},{8,72},{9,... | collective-permute-start | bytes 184328 | tf_op jit(solution)/shard_map/ppermute | solution.py:41
  72.7 0.4 collective-permute-start.14
  73.2 3.6 %mid_input.1 = bf16[96,16,128]{2,1,0:T(8,128)(2,1)} custom-call(bf16[1536,128]{1,0:T(8,128)(2,1)} %get-tuple-element.70.refs_1_.refs_14_.refs_0_, bf16[1728,256]{1,0:T(8,128)(2,1)} %get-tuple-element.88.refs_1_, bf16[3,3,96,96]{3,2,1,0:T(8,128)(2,1)} %refs_2_.3), custom_call_target="tpu_custom_call" | custom-call | tf_op jit(solution)/shard_map/mid_input/pallas_call | solution.py:475
  76.8 0.0 collective-permute-done.14
  76.8 0.0 collective-permute-done.15
  76.9 0.0 collective-permute-done.16
  76.9 0.1 collective-permute-start.17
  77.0 2.0 %collective-permute-start.19 = (bf16[960,128]{1,0:T(8,128)(2,1)S(1)}, bf16[960,128]{1,0:T(8,128)(2,1)S(1)}, u32[]{:S(2)}, u32[]{:S(2)}) collective-permute-start(bf16[960,128]{1,0:T(8,128)(2,1)S(1)} %bitcast.58), channel_id=1, source_target_pairs={{0,3},{1,2},{2,1},{3,0},{4,100},{5,101},{6,102},{7,103},{8,11},{9,... | collective-permute-start | bytes 737288 | tf_op jit(solution)/shard_map/ppermute | solution.py:41
  79.0 1.2 %collective-permute-start.18 = (bf16[960,128]{1,0:T(8,128)(2,1)S(1)}, bf16[960,128]{1,0:T(8,128)(2,1)S(1)}, u32[]{:S(2)}, u32[]{:S(2)}) collective-permute-start(bf16[960,128]{1,0:T(8,128)(2,1)S(1)} %bitcast.59), channel_id=1, source_target_pairs={{0,2},{1,3},{2,0},{3,1},{4,68},{5,69},{6,70},{7,71},{8,10},{9,11},... | collective-permute-start | bytes 737288 | tf_op jit(solution)/shard_map/ppermute | solution.py:41
  80.2 0.1 broadcast_in_dim.37
  80.4 3.3 %coarse_input.1 = bf16[8,64,192]{2,1,0:T(8,128)(2,1)} custom-call(bf16[8,64,192]{2,1,0:T(8,128)(2,1)} %get-tuple-element.71.refs_2_.refs_11_.masked, bf16[3,816,192]{2,1,0:T(8,128)(2,1)} %get-tuple-element.93.px, bf16[3,3,192,192]{3,2,1,0:T(8,128)(2,1)} %first.1), custom_call_target="tpu_custom_call" | custom-call | tf_op jit(solution)/shard_map/coarse_input/pallas_call | solution.py:712
  83.7 0.0 collective-permute-done.17
  83.7 3.9 %collective-permute-done.18 = bf16[960,128]{1,0:T(8,128)(2,1)S(1)} collective-permute-done((bf16[960,128]{1,0:T(8,128)(2,1)S(1)}, bf16[960,128]{1,0:T(8,128)(2,1)S(1)}, u32[]{:S(2)}, u32[]{:S(2)}) %collective-permute-start.18) | collective-permute-done | bytes 245792 | tf_op jit(solution)/shard_map/ppermute | solution.py:41
  87.7 7.8 %collective-permute-start.20 = (bf16[3840,128]{1,0:T(8,128)(2,1)S(1)}, bf16[3840,128]{1,0:T(8,128)(2,1)S(1)}, u32[]{:S(2)}, u32[]{:S(2)}) collective-permute-start(bf16[3840,128]{1,0:T(8,128)(2,1)S(1)} %bitcast.46), channel_id=1, source_target_pairs={{0,4},{1,5},{2,6},{3,7},{4,0},{5,1},{6,2},{7,3},{8,12},{9,13},{10,... | collective-permute-start | bytes 2949128 | tf_op jit(solution)/shard_map/ppermute | solution.py:41
  95.5 1.6 %unpack_kept.1 = (f32[3,3,48,48]{3,2,1,0:T(8,128)}, f32[3,3,48,48]{3,2,1,0:T(8,128)}, f32[3,3,96,96]{3,2,1,0:T(8,128)}, f32[3,3,96,96]{3,2,1,0:T(8,128)}, f32[3,...) custom-call(bf16[3840,128]{1,0:T(8,128)(2,1)S(1)} %bitcast.47), custom_call_target="tpu_custom_call" | custom-call | tf_op jit(solution)/shard_map/unpack_kept/pallas_call | solution.py:787
  97.1 0.6 collective-permute-done.20.refs_0_
  97.7 1.6 %unpack_other.1 = (f32[3,3,48,48]{3,2,1,0:T(8,128)}, f32[3,3,48,48]{3,2,1,0:T(8,128)}, f32[3,3,96,96]{3,2,1,0:T(8,128)}, f32[3,3,96,96]{3,2,1,0:T(8,128)}, f32[3...) custom-call(bf16[3840,128]{1,0:T(8,128)(2,1)S(1)} %collective-permut, ...), custom_call_target="tpu_custom_call", output_to_operand_aliasing={{0}: (1, {}), {1}: (2, {}), {2}: (3, {}), {3}: (4, {}), {4}... | custom-call | tf_op jit(solution)/shard_map/unpack_other/pallas_call | solution.py:787
  (19 shorter events, 0.4 us)
Async XLA Ops:
  6.0 9.1 %collective-permute-start = (bf16[896,128]{1,0:T(8,128)(2,1)}, bf16[896,128]{1,0:T(8,128)(2,1)S(1)}, u32[]{:S(2)}, u32[]{:S(2)}) collective-permute-start(bf16[896,128]{1,0:T(8,128)(2,1)} %get-tuple-element.67), channel_id=1, source_target_pairs={{0,4},{1,5},{2,6},{3,7},{4,0},{5,1},{6,2},{7,3},{8,12},{9,13},{10,... | collective-permute-start | bytes 688136 | tf_op jit(solution)/shard_map/ppermute | solution.py:41
  7.5 7.6 %collective-permute-start.1 = (bf16[896,128]{1,0:T(8,128)(2,1)}, bf16[896,128]{1,0:T(8,128)(2,1)S(1)}, u32[]{:S(2)}, u32[]{:S(2)}) collective-permute-start(bf16[896,128]{1,0:T(8,128)(2,1)} %get-tuple-element.68), channel_id=1, source_target_pairs={{4,8},{5,9},{6,10},{7,11},{8,4},{9,5},{10,6},{11,7},{12,16},{13,17... | collective-permute-start | bytes 688136 | tf_op jit(solution)/shard_map/ppermute | solution.py:41
  16.5 3.5 %collective-permute-start.2 = (bf16[352,128]{1,0:T(8,128)(2,1)S(1)}, bf16[352,128]{1,0:T(8,128)(2,1)S(1)}, u32[]{:S(2)}, u32[]{:S(2)}) collective-permute-start(bf16[352,128]{1,0:T(8,128)(2,1)S(1)} %get-tuple-element.76), channel_id=1, source_target_pairs={{0,1},{1,0},{2,3},{3,2},{4,5},{5,4},{6,7},{7,6},{8,9},{9,8},{10,11... | collective-permute-start | bytes 270344 | tf_op jit(solution)/shard_map/ppermute | solution.py:41
  17.9 2.1 %collective-permute-start.3 = (bf16[352,128]{1,0:T(8,128)(2,1)S(1)}, bf16[352,128]{1,0:T(8,128)(2,1)S(1)}, u32[]{:S(2)}, u32[]{:S(2)}) collective-permute-start(bf16[352,128]{1,0:T(8,128)(2,1)S(1)} %get-tuple-element.77), channel_id=1, source_target_pairs={{1,2},{2,1},{5,6},{6,5},{9,10},{10,9},{13,14},{14,13},{17,18},{18,... | collective-permute-start | bytes 270344 | tf_op jit(solution)/shard_map/ppermute | solution.py:41
  35.6 2.6 %collective-permute-start.4 = (bf16[3840,128]{1,0:T(8,128)(2,1)S(1)}, bf16[3840,128]{1,0:T(8,128)(2,1)S(1)}, u32[]{:S(2)}, u32[]{:S(2)}) collective-permute-start(bf16[3840,128]{1,0:T(8,128)(2,1)S(1)} %get-tuple-element.80), channel_id=1, source_target_pairs={{0,4},{1,5},{2,6},{3,7},{4,0},{5,1},{6,2},{7,3},{8,12},{9,13},{10,... | collective-permute-start | bytes 2949128 | tf_op jit(solution)/shard_map/ppermute | solution.py:41
  39.8 11.3 %collective-permute-start.5 = (bf16[960,128]{1,0:T(8,128)(2,1)S(1)}, bf16[960,128]{1,0:T(8,128)(2,1)S(1)}, u32[]{:S(2)}, u32[]{:S(2)}) collective-permute-start(bf16[960,128]{1,0:T(8,128)(2,1)S(1)} %get-tuple-element.123), channel_id=1, source_target_pairs={{0,1},{1,0},{2,3},{3,2},{4,36},{5,37},{6,38},{7,39},{8,9},{9,8},{1... | collective-permute-start | bytes 737288 | tf_op jit(solution)/shard_map/ppermute | solution.py:41
  44.3 7.6 %collective-permute-start.7 = (bf16[960,128]{1,0:T(8,128)(2,1)S(1)}, bf16[960,128]{1,0:T(8,128)(2,1)S(1)}, u32[]{:S(2)}, u32[]{:S(2)}) collective-permute-start(bf16[960,128]{1,0:T(8,128)(2,1)S(1)} %get-tuple-element.124), channel_id=1, source_target_pairs={{0,3},{1,2},{2,1},{3,0},{4,100},{5,101},{6,102},{7,103},{8,11},{9,... | collective-permute-start | bytes 737288 | tf_op jit(solution)/shard_map/ppermute | solution.py:41
  46.1 7.4 %collective-permute-start.6 = (bf16[960,128]{1,0:T(8,128)(2,1)S(1)}, bf16[960,128]{1,0:T(8,128)(2,1)S(1)}, u32[]{:S(2)}, u32[]{:S(2)}) collective-permute-start(bf16[960,128]{1,0:T(8,128)(2,1)S(1)} %get-tuple-element.125), channel_id=1, source_target_pairs={{0,2},{1,3},{2,0},{3,1},{4,68},{5,69},{6,70},{7,71},{8,10},{9,11},... | collective-permute-start | bytes 737288 | tf_op jit(solution)/shard_map/ppermute | solution.py:41
  53.7 3.8 %collective-permute-start.8 = (bf16[240,128]{1,0:T(8,128)(2,1)S(1)}, bf16[240,128]{1,0:T(8,128)(2,1)S(1)}, u32[]{:S(2)}, u32[]{:S(2)}) collective-permute-start(bf16[240,128]{1,0:T(8,128)(2,1)S(1)} %get-tuple-element.126), channel_id=1, source_target_pairs={{0,32},{1,33},{2,34},{3,35},{4,12},{5,13},{6,14},{7,15},{8,40},{9,... | collective-permute-start | bytes 184328 | tf_op jit(solution)/shard_map/ppermute | solution.py:41
  53.8 4.4 %collective-permute-start.10 = (bf16[240,128]{1,0:T(8,128)(2,1)S(1)}, bf16[240,128]{1,0:T(8,128)(2,1)S(1)}, u32[]{:S(2)}, u32[]{:S(2)}) collective-permute-start(bf16[240,128]{1,0:T(8,128)(2,1)S(1)} %get-tuple-element.127), channel_id=1, source_target_pairs={{0,96},{1,97},{2,98},{3,99},{4,28},{5,29},{6,30},{7,31},{8,104},{9... | collective-permute-start | bytes 184328 | tf_op jit(solution)/shard_map/ppermute | solution.py:41
  56.4 4.6 %collective-permute-start.9 = (bf16[240,128]{1,0:T(8,128)(2,1)S(1)}, bf16[240,128]{1,0:T(8,128)(2,1)S(1)}, u32[]{:S(2)}, u32[]{:S(2)}) collective-permute-start(bf16[240,128]{1,0:T(8,128)(2,1)S(1)} %get-tuple-element.128), channel_id=1, source_target_pairs={{0,64},{1,65},{2,66},{3,67},{4,20},{5,21},{6,22},{7,23},{8,72},{9,... | collective-permute-start | bytes 184328 | tf_op jit(solution)/shard_map/ppermute | solution.py:41
  61.0 5.7 %collective-permute-start.13 = (bf16[240,128]{1,0:T(8,128)(2,1)S(1)}, bf16[240,128]{1,0:T(8,128)(2,1)S(1)}, u32[]{:S(2)}, u32[]{:S(2)}) collective-permute-start(bf16[240,128]{1,0:T(8,128)(2,1)S(1)} %fusion.3), channel_id=1, source_target_pairs={{0,24},{1,25},{2,26},{3,27},{4,7},{5,6},{6,5},{7,4},{8,16},{9,17},... | collective-permute-start | bytes 184328 | tf_op jit(solution)/shard_map/ppermute | solution.py:41
  63.9 4.6 %collective-permute-start.12 = (bf16[240,128]{1,0:T(8,128)(2,1)S(1)}, bf16[240,128]{1,0:T(8,128)(2,1)S(1)}, u32[]{:S(2)}, u32[]{:S(2)}) collective-permute-start(bf16[240,128]{1,0:T(8,128)(2,1)S(1)} %fusion.3), channel_id=1, source_target_pairs={{0,16},{1,17},{2,18},{3,19},{4,6},{5,7},{6,4},{7,5},{8,24},{9,25},... | collective-permute-start | bytes 184328 | tf_op jit(solution)/shard_map/ppermute | solution.py:41
  66.7 3.1 %collective-permute-start.11 = (bf16[240,128]{1,0:T(8,128)(2,1)S(1)}, bf16[240,128]{1,0:T(8,128)(2,1)S(1)}, u32[]{:S(2)}, u32[]{:S(2)}) collective-permute-start(bf16[240,128]{1,0:T(8,128)(2,1)S(1)} %fusion.3), channel_id=1, source_target_pairs={{0,8},{1,9},{2,10},{3,11},{4,5},{5,4},{6,7},{7,6},{8,0},{9,1},{10,... | collective-permute-start | bytes 184328 | tf_op jit(solution)/shard_map/ppermute | solution.py:41
  69.8 7.0 %collective-permute-start.16 = (bf16[240,128]{1,0:T(8,128)(2,1)S(1)}, bf16[240,128]{1,0:T(8,128)(2,1)S(1)}, u32[]{:S(2)}, u32[]{:S(2)}) collective-permute-start(bf16[240,128]{1,0:T(8,128)(2,1)S(1)} %add_convert_fusion.1), channel_id=1, source_target_pairs={{0,96},{1,97},{2,98},{3,99},{4,28},{5,29},{6,30},{7,31},{8,104},{9... | collective-permute-start | bytes 184328 | tf_op jit(solution)/shard_map/ppermute | solution.py:41
  70.3 6.5 %collective-permute-start.15 = (bf16[240,128]{1,0:T(8,128)(2,1)S(1)}, bf16[240,128]{1,0:T(8,128)(2,1)S(1)}, u32[]{:S(2)}, u32[]{:S(2)}) collective-permute-start(bf16[240,128]{1,0:T(8,128)(2,1)S(1)} %add_convert_fusion.1), channel_id=1, source_target_pairs={{0,64},{1,65},{2,66},{3,67},{4,20},{5,21},{6,22},{7,23},{8,72},{9,... | collective-permute-start | bytes 184328 | tf_op jit(solution)/shard_map/ppermute | solution.py:41
  72.7 4.1 %collective-permute-start.14 = (bf16[240,128]{1,0:T(8,128)(2,1)S(1)}, bf16[240,128]{1,0:T(8,128)(2,1)S(1)}, u32[]{:S(2)}, u32[]{:S(2)}) collective-permute-start(bf16[240,128]{1,0:T(8,128)(2,1)S(1)} %add_convert_fusion.1), channel_id=1, source_target_pairs={{0,32},{1,33},{2,34},{3,35},{4,12},{5,13},{6,14},{7,15},{8,40},{9,... | collective-permute-start | bytes 184328 | tf_op jit(solution)/shard_map/ppermute | solution.py:41
  76.9 6.8 %collective-permute-start.17 = (bf16[960,128]{1,0:T(8,128)(2,1)S(1)}, bf16[960,128]{1,0:T(8,128)(2,1)S(1)}, u32[]{:S(2)}, u32[]{:S(2)}) collective-permute-start(bf16[960,128]{1,0:T(8,128)(2,1)S(1)} %bitcast.57), channel_id=1, source_target_pairs={{0,1},{1,0},{2,3},{3,2},{4,36},{5,37},{6,38},{7,39},{8,9},{9,8},{1... | collective-permute-start | bytes 737288 | tf_op jit(solution)/shard_map/ppermute | solution.py:41
  77.0 10.7 %collective-permute-start.19 = (bf16[960,128]{1,0:T(8,128)(2,1)S(1)}, bf16[960,128]{1,0:T(8,128)(2,1)S(1)}, u32[]{:S(2)}, u32[]{:S(2)}) collective-permute-start(bf16[960,128]{1,0:T(8,128)(2,1)S(1)} %bitcast.58), channel_id=1, source_target_pairs={{0,3},{1,2},{2,1},{3,0},{4,100},{5,101},{6,102},{7,103},{8,11},{9,... | collective-permute-start | bytes 737288 | tf_op jit(solution)/shard_map/ppermute | solution.py:41
  79.0 8.6 %collective-permute-start.18 = (bf16[960,128]{1,0:T(8,128)(2,1)S(1)}, bf16[960,128]{1,0:T(8,128)(2,1)S(1)}, u32[]{:S(2)}, u32[]{:S(2)}) collective-permute-start(bf16[960,128]{1,0:T(8,128)(2,1)S(1)} %bitcast.59), channel_id=1, source_target_pairs={{0,2},{1,3},{2,0},{3,1},{4,68},{5,69},{6,70},{7,71},{8,10},{9,11},... | collective-permute-start | bytes 737288 | tf_op jit(solution)/shard_map/ppermute | solution.py:41
  87.7 10.0 %collective-permute-start.20 = (bf16[3840,128]{1,0:T(8,128)(2,1)S(1)}, bf16[3840,128]{1,0:T(8,128)(2,1)S(1)}, u32[]{:S(2)}, u32[]{:S(2)}) collective-permute-start(bf16[3840,128]{1,0:T(8,128)(2,1)S(1)} %bitcast.46), channel_id=1, source_target_pairs={{0,4},{1,5},{2,6},{3,7},{4,0},{5,1},{6,2},{7,3},{8,12},{9,13},{10,... | collective-permute-start | bytes 2949128 | tf_op jit(solution)/shard_map/ppermute | solution.py:41
